TPU v7x, 32 devices: a whole 2x2x4 slice. The times are simulated.
32 devices in a mesh: shard: 8 (over z, x), replica: 4 (over y, core).
Axes of the slice: x: 2, y: 2, z: 4, core: 2. Of those that a mesh axis runs over, the one named last changes fastest.
Arguments:
- tokens: bfloat16 [4096, 1024], P(('shard', 'replica')), may hold values from -6 to 6
- cotangent: bfloat16 [4096, 1024], P(('shard', 'replica')), may hold values from -6 to 6
- seq_lengths: int32 [32, 4], P(('shard', 'replica')), may hold values from 0 to 128, as said below
- seq_starts: int32 [32, 4], P(('shard', 'replica')), may hold values from 0 to 128, as said below
- in_gain: bfloat16 [1024], P('shard'), may hold values from 0.5 to 1.5
- w_in: bfloat16 [1024, 3352], P('shard'), may hold values from -0.1875 to 0.1875
- conv_w: bfloat16 [4, 1792], P(None, 'shard'), may hold values from -3 to 3
- conv_b: bfloat16 [1792], P('shard'), may hold values from -0.5 to 0.5
- a_log: float32 [24], replicated, may hold values from -3 to 1
- dt_bias: float32 [24], replicated, may hold values from -5 to -1
- skip_d: float32 [24], replicated, may hold values from 0.5 to 1.5
- ssm_gain: bfloat16 [1536], P('shard'), may hold values from 0.5 to 1.5
- w_out: bfloat16 [1536, 1024], P('shard'), may hold values from -0.15625 to 0.15625
- w_query: bfloat16 [1024, 512], P('shard'), may hold values from -0.1875 to 0.1875
- w_key: bfloat16 [1024, 128], P('shard'), may hold values from -0.1875 to 0.1875
- w_value: bfloat16 [1024, 128], P('shard'), may hold values from -0.1875 to 0.1875
- w_attn_out: bfloat16 [512, 1024], P('shard'), may hold values from -1 to 1
- ff_gain: bfloat16 [1024], P('shard'), may hold values from 0.5 to 1.5
- w_gate: bfloat16 [1024, 2048], P('shard'), may hold values from -0.1875 to 0.1875
- w_up: bfloat16 [1024, 2048], P('shard'), may hold values from -0.1875 to 0.1875
- w_down: bfloat16 [2048, 1024], P('shard'), may hold values from -0.125 to 0.125
Outputs:
- block_out: bfloat16 [4096, 1024], P(('shard', 'replica'))
- tokens_grad: bfloat16 [4096, 1024], P(('shard', 'replica'))
- in_gain_grad: float32 [1024], P('shard')
- w_in_grad: float32 [1024, 3352], P('shard')
- conv_w_grad: float32 [4, 1792], P(None, 'shard')
- conv_b_grad: float32 [1792], P('shard')
- a_log_grad: float32 [24], replicated
- dt_bias_grad: float32 [24], replicated
- skip_d_grad: float32 [24], replicated
- ssm_gain_grad: float32 [1536], P('shard')
- w_out_grad: float32 [1536, 1024], P('shard')
- w_query_grad: float32 [1024, 512], P('shard')
- w_key_grad: float32 [1024, 128], P('shard')
- w_value_grad: float32 [1024, 128], P('shard')
- w_attn_out_grad: float32 [512, 1024], P('shard')
- ff_gain_grad: float32 [1024], P('shard')
- w_gate_grad: float32 [1024, 2048], P('shard')
- w_up_grad: float32 [1024, 2048], P('shard')
- w_down_grad: float32 [2048, 1024], P('shard')
Inputs may be any that keep to these rules, and one draw needn't show every extreme that they name: `seq_lengths`: in each row the sequences lie in order, without intersection, inside the 128 slots; empty slots have length 0; some device holds one sequence of exactly 128 tokens. `seq_starts`: start of each slot's sequence in its row; starts do not fall along a row.
All inputs are finite; a program needn't handle non-finite values.
Results may differ from a plain program's by a relative error of at most 0.019.
Values may be sent and summed in bfloat16 or wider, within the bound.
No kernel may reach another device: no remote copies, remote signals or barrier semaphores. Data moves between devices by JAX's collectives and lax.ppermute only.
A program may use at most 192 MiB of HBM per device.

v0:
```python
import jax
import jax.numpy as jnp
from jax import lax
from jax.sharding import PartitionSpec as P

FF = 2048
MH = 24
HD = 64
NS = 128
QH = 8
KVH = 2
ATTENTION_HEAD = 64
CONV_K = 4


EPSILON = 1e-05
ROPE_BASE = 100000000000.0


def matmul_plain(left, right):
    return jnp.dot(left, right, preferred_element_type=jnp.float32)


def matmul_left(left, right):
    return lax.dot_general(
        left, right, (((0,), (0,)), ((), ())), preferred_element_type=jnp.float32
    )


def matmul_right(left, right):
    return lax.dot_general(
        left, right, (((1,), (1,)), ((), ())), preferred_element_type=jnp.float32
    )


def rms_scale(values, gain):
    return values * lax.rsqrt(jnp.mean(values * values, axis=-1, keepdims=True) + EPSILON) * gain


def layout(lengths, starts, extent):
    position = jnp.arange(extent, dtype=jnp.int32)
    inside = (position[:, None] >= starts[None, :]) & (
        position[:, None] < starts[None, :] + lengths[None, :]
    )
    number = jnp.arange(1, lengths.shape[0] + 1, dtype=jnp.int32)
    segment = jnp.sum(jnp.where(inside, number[None, :], 0), axis=1) - 1
    first = jnp.sum(jnp.where(inside, starts[None, :], 0), axis=1)
    return (segment, position - first)


def causal_allowed(segment):
    position = jnp.arange(segment.shape[0], dtype=jnp.int32)
    return (segment[:, None] == segment[None, :]) & (position[:, None] >= position[None, :])


def mixer_front(conv_in, raw_step, conv_w, conv_b, dt_bias, a_log, segment):
    extent = conv_in.shape[0]
    summed = conv_b[None, :] + conv_w[CONV_K - 1][None, :] * conv_in
    for offset in range(1, CONV_K):
        shifted = jnp.concatenate(
            [jnp.zeros((offset, conv_in.shape[1]), conv_in.dtype), conv_in[: extent - offset]],
            axis=0,
        )
        seg_moved = jnp.concatenate(
            [jnp.full((offset,), -2, jnp.int32), segment[: extent - offset]]
        )
        summed = summed + conv_w[CONV_K - 1 - offset][None, :] * jnp.where(
            (seg_moved == segment)[:, None], shifted, 0.0
        )
    conv_act = jax.nn.silu(summed)
    time_step = jax.nn.softplus(raw_step + dt_bias[None, :])
    log_decay = jnp.cumsum(time_step * (-jnp.exp(a_log))[None, :], axis=0).T
    allowed = causal_allowed(segment)[None]
    spread = log_decay[:, :, None] - log_decay[:, None, :]
    decay_mat = jnp.where(allowed, jnp.exp(jnp.where(allowed, spread, 0.0)), 0.0)
    return (conv_act, time_step, decay_mat)


def rotate(values, position, heads):
    half_size = ATTENTION_HEAD // 2
    inverse = ROPE_BASE ** (-jnp.arange(half_size, dtype=jnp.float32) / half_size)
    angle = position.astype(jnp.float32)[:, None] * inverse[None, :]
    cosine = jnp.cos(angle)[:, None, :]
    sine_val = jnp.sin(angle)[:, None, :]
    shaped = values.reshape(values.shape[0], heads, ATTENTION_HEAD)
    first_half = shaped[..., :half_size]
    second_half = shaped[..., half_size:]
    return jnp.concatenate(
        [
            first_half * cosine - second_half * sine_val,
            second_half * cosine + first_half * sine_val,
        ],
        axis=-1,
    )


def gate_norm(scan_out, gate_z, gain):
    return rms_scale(scan_out * jax.nn.silu(gate_z), gain)


def swiglu(gate_val, up_val):
    return jax.nn.silu(gate_val) * up_val


def attention_probs(query_reduced, key_reduced, allowed):
    attention_scores = jnp.einsum(
        "khei,whi->hekw", query_reduced, key_reduced, preferred_element_type=jnp.float32
    ) * ATTENTION_HEAD ** (-0.5)
    attention_scores = jnp.where(allowed, attention_scores, -1e30)
    row_max = jnp.max(attention_scores, axis=-1, keepdims=True)
    exp_scores = jnp.exp(attention_scores - row_max)
    return exp_scores / jnp.sum(exp_scores, axis=-1, keepdims=True)


def forward_pass(tokens_f, gathered, a_log, dt_bias, skip_d, segment, position):
    (
        in_gain,
        w_in,
        conv_w,
        conv_b,
        ssm_gain,
        w_out,
        w_query,
        w_key,
        w_value,
        w_attn_out,
        ff_gain,
        w_gate,
        w_up,
        w_down,
    ) = gathered
    extent = tokens_f.shape[0]
    width = MH * HD
    normed_f, pull_norm_one = jax.vjp(rms_scale, tokens_f, in_gain.astype(jnp.float32))
    normed = normed_f.astype(jnp.bfloat16)
    mixed_in = matmul_plain(normed, w_in)
    gate_z = mixed_in[:, :width]
    conv_in = mixed_in[:, width : 2 * width + 2 * NS]
    raw_step = mixed_in[:, 2 * width + 2 * NS :]

    def front(conv_value, step_value, tap_value, bias_value, shift_value, rate_value):
        return mixer_front(
            conv_value, step_value, tap_value, bias_value, shift_value, rate_value, segment
        )

    (conv_act, time_step, decay_mat), pull_front = jax.vjp(
        front,
        conv_in,
        raw_step,
        conv_w.astype(jnp.float32),
        conv_b.astype(jnp.float32),
        dt_bias,
        a_log,
    )
    act_low = conv_act.astype(jnp.bfloat16)
    x_heads = act_low[:, :width].reshape(extent, MH, HD)
    b_state = act_low[:, width : width + NS]
    c_state = act_low[:, width + NS :]
    inner_bc = matmul_right(c_state, b_state)
    mixer_weights = (decay_mat * inner_bc[None]).astype(jnp.bfloat16)
    scaled_x = (x_heads.astype(jnp.float32) * time_step[:, :, None]).astype(jnp.bfloat16)
    scan_out = jnp.einsum(
        "hts,shd->thd", mixer_weights, scaled_x, preferred_element_type=jnp.float32
    )
    scan_out = (scan_out + skip_d[None, :, None] * x_heads.astype(jnp.float32)).reshape(
        extent, width
    )
    gated_f, pull_gate = jax.vjp(gate_norm, scan_out, gate_z, ssm_gain.astype(jnp.float32))
    gated = gated_f.astype(jnp.bfloat16)
    mixer_out = matmul_plain(gated, w_out)
    query = matmul_plain(normed, w_query)
    key_proj = matmul_plain(normed, w_key)
    value_proj = matmul_plain(normed, w_value)

    def turn(query_value, key_value):
        return (rotate(query_value, position, QH), rotate(key_value, position, KVH))

    (q_rot, k_rot), pull_rotate = jax.vjp(turn, query, key_proj)
    query_reduced = q_rot.astype(jnp.bfloat16).reshape(extent, KVH, QH // KVH, ATTENTION_HEAD)
    key_reduced = k_rot.astype(jnp.bfloat16)
    value_reduced = value_proj.astype(jnp.bfloat16).reshape(extent, KVH, ATTENTION_HEAD)
    prob_all = attention_probs(query_reduced, key_reduced, causal_allowed(segment))
    probability_reduced = prob_all.astype(jnp.bfloat16)
    head_rows_out = jnp.einsum(
        "lwmi,ilu->mlwu", probability_reduced, value_reduced, preferred_element_type=jnp.float32
    )
    head_rows_out = head_rows_out.astype(jnp.bfloat16).reshape(extent, QH * ATTENTION_HEAD)
    attn_out = matmul_plain(head_rows_out, w_attn_out)
    residual = tokens_f + mixer_out + attn_out
    normed_two_f, pull_norm_two = jax.vjp(rms_scale, residual, ff_gain.astype(jnp.float32))
    normed_two = normed_two_f.astype(jnp.bfloat16)
    gate_val = matmul_plain(normed_two, w_gate)
    up_val = matmul_plain(normed_two, w_up)
    hidden_f, pull_swiglu = jax.vjp(swiglu, gate_val, up_val)
    hidden = hidden_f.astype(jnp.bfloat16)
    feed_out = matmul_plain(hidden, w_down)
    valid_mask = (segment >= 0)[:, None]
    result = jnp.where(valid_mask, residual + feed_out, 0.0).astype(jnp.bfloat16)
    kept = (
        pull_norm_one,
        normed,
        pull_front,
        x_heads,
        b_state,
        c_state,
        inner_bc,
        decay_mat,
        mixer_weights,
        scaled_x,
        time_step,
        pull_gate,
        gated,
        pull_rotate,
        query_reduced,
        key_reduced,
        value_reduced,
        prob_all,
        probability_reduced,
        head_rows_out,
        pull_norm_two,
        normed_two,
        pull_swiglu,
        hidden,
        valid_mask,
    )
    return (result, kept)


def backward_pass(cotangent, matrices, skip_d, kept):
    w_in, w_out, w_query, w_key, w_value, w_attn_out, w_gate, w_up, w_down = matrices
    (
        pull_norm_one,
        normed,
        pull_front,
        x_heads,
        b_state,
        c_state,
        inner_bc,
        decay_mat,
        mixer_weights,
        scaled_x,
        time_step,
        pull_gate,
        gated,
        pull_rotate,
        query_reduced,
        key_reduced,
        value_reduced,
        prob_all,
        probability_reduced,
        head_rows_out,
        pull_norm_two,
        normed_two,
        pull_swiglu,
        hidden,
        valid_mask,
    ) = kept
    extent = cotangent.shape[0]
    out_grad = jnp.where(valid_mask, cotangent.astype(jnp.float32), 0.0)
    feed_grad = out_grad.astype(jnp.bfloat16)
    hidden_grad = matmul_right(feed_grad, w_down)
    gate_grad, up_grad = pull_swiglu(hidden_grad)
    gate_low = gate_grad.astype(jnp.bfloat16)
    up_low = up_grad.astype(jnp.bfloat16)
    normed_two_grad = matmul_right(gate_low, w_gate) + matmul_right(up_low, w_up)
    residual_part, grad_ff_gain = pull_norm_two(normed_two_grad)
    residual_grad = out_grad + residual_part
    branch_grad = residual_grad.astype(jnp.bfloat16)
    head_rows_grad = (
        matmul_right(branch_grad, w_attn_out)
        .astype(jnp.bfloat16)
        .reshape(extent, KVH, QH // KVH, ATTENTION_HEAD)
    )
    probability_grad = jnp.einsum(
        "khei,whi->hekw", head_rows_grad, value_reduced, preferred_element_type=jnp.float32
    )
    value_grad = jnp.einsum(
        "muhi,hmuy->imy", probability_reduced, head_rows_grad, preferred_element_type=jnp.float32
    )
    scores_gradient = prob_all * (
        probability_grad - jnp.sum(prob_all * probability_grad, axis=-1, keepdims=True)
    )
    scores_gradient = scores_gradient.astype(jnp.bfloat16)
    q_rot_grad = jnp.einsum(
        "lwmi,ilu->mlwu", scores_gradient, key_reduced, preferred_element_type=jnp.float32
    ) * ATTENTION_HEAD ** (-0.5)
    k_rot_grad = jnp.einsum(
        "muhi,hmuy->imy", scores_gradient, query_reduced, preferred_element_type=jnp.float32
    ) * ATTENTION_HEAD ** (-0.5)
    query_grad, key_grad = pull_rotate((q_rot_grad.reshape(extent, QH, ATTENTION_HEAD), k_rot_grad))
    query_low = query_grad.astype(jnp.bfloat16)
    key_low = key_grad.astype(jnp.bfloat16)
    value_low = value_grad.reshape(extent, KVH * ATTENTION_HEAD).astype(jnp.bfloat16)
    normed_grad = (
        matmul_right(query_low, w_query)
        + matmul_right(key_low, w_key)
        + matmul_right(value_low, w_value)
    )
    gated_grad = matmul_right(branch_grad, w_out)
    scan_grad, gate_z_grad, grad_ssm_gain = pull_gate(gated_grad)
    scan_low = scan_grad.astype(jnp.bfloat16).reshape(extent, MH, HD)
    weight_grad = jnp.einsum("thd,shd->hts", scan_low, scaled_x, preferred_element_type=jnp.float32)
    scaled_grad = jnp.einsum(
        "hts,thd->shd", mixer_weights, scan_low, preferred_element_type=jnp.float32
    )
    inner_low = jnp.sum(weight_grad * decay_mat, axis=0).astype(jnp.bfloat16)
    decay_grad = weight_grad * inner_bc[None]
    c_grad = matmul_plain(inner_low, b_state)
    b_grad = matmul_left(inner_low, c_state)
    heads_f = x_heads.astype(jnp.float32)
    scan_f = scan_low.astype(jnp.float32)
    x_grad = scaled_grad * time_step[:, :, None] + skip_d[None, :, None] * scan_f
    step_grad = jnp.sum(scaled_grad * heads_f, axis=2)
    grad_skip = jnp.sum(scan_f * heads_f, axis=(0, 2))
    act_grad = jnp.concatenate([x_grad.reshape(extent, MH * HD), b_grad, c_grad], axis=1)
    conv_grad, raw_grad, grad_conv_w, grad_conv_b, grad_dt_bias, grad_a_log = pull_front(
        (act_grad, step_grad, decay_grad)
    )
    mixed_low = jnp.concatenate([gate_z_grad, conv_grad, raw_grad], axis=1).astype(jnp.bfloat16)
    normed_grad = normed_grad + matmul_right(mixed_low, w_in)
    token_part, grad_in_gain = pull_norm_one(normed_grad)
    tokens_grad = (residual_grad + token_part).astype(jnp.bfloat16)
    model_right = jnp.concatenate([mixed_low, query_low, key_low, value_low], axis=1)
    feed_right = jnp.concatenate([gate_low, up_low], axis=1)
    factors = (
        normed,
        model_right,
        normed_two,
        feed_right,
        gated,
        branch_grad,
        head_rows_out,
        hidden,
        feed_grad,
    )
    small = (grad_in_gain, grad_conv_w, grad_conv_b, grad_ssm_gain, grad_ff_gain)
    return (tokens_grad, factors, small, (grad_a_log, grad_dt_bias, grad_skip))


def model_rows(factors):
    (
        normed,
        model_right,
        normed_two,
        feed_right,
        gated,
        branch_grad,
        head_rows_out,
        hidden,
        feed_grad,
    ) = factors
    first = matmul_left(normed, model_right)
    second = matmul_left(normed_two, feed_right)
    return jnp.concatenate([first, second], axis=1)


def split_model(joined):
    in_cols = 2 * MH * HD + 2 * NS + MH
    query_cols = QH * ATTENTION_HEAD
    key_cols = KVH * ATTENTION_HEAD
    edges = (
        0,
        in_cols,
        in_cols + query_cols,
        in_cols + query_cols + key_cols,
        in_cols + query_cols + 2 * key_cols,
        in_cols + query_cols + 2 * key_cols + FF,
        in_cols + query_cols + 2 * key_cols + 2 * FF,
    )
    return tuple((joined[:, edges[index] : edges[index + 1]] for index in range(6)))


def shards(
    tokens,
    cotangent,
    seq_lengths,
    seq_starts,
    in_gain,
    w_in,
    conv_w,
    conv_b,
    a_log,
    dt_bias,
    skip_d,
    ssm_gain,
    w_out,
    w_query,
    w_key,
    w_value,
    w_attn_out,
    ff_gain,
    w_gate,
    w_up,
    w_down,
):
    gathered = (
        lax.all_gather(in_gain, "shard", axis=0, tiled=True),
        lax.all_gather(w_in, "shard", axis=0, tiled=True),
        lax.all_gather(conv_w, "shard", axis=1, tiled=True),
        lax.all_gather(conv_b, "shard", axis=0, tiled=True),
        lax.all_gather(ssm_gain, "shard", axis=0, tiled=True),
        lax.all_gather(w_out, "shard", axis=0, tiled=True),
        lax.all_gather(w_query, "shard", axis=0, tiled=True),
        lax.all_gather(w_key, "shard", axis=0, tiled=True),
        lax.all_gather(w_value, "shard", axis=0, tiled=True),
        lax.all_gather(w_attn_out, "shard", axis=0, tiled=True),
        lax.all_gather(ff_gain, "shard", axis=0, tiled=True),
        lax.all_gather(w_gate, "shard", axis=0, tiled=True),
        lax.all_gather(w_up, "shard", axis=0, tiled=True),
        lax.all_gather(w_down, "shard", axis=0, tiled=True),
    )
    segment, position = layout(seq_lengths[0], seq_starts[0], tokens.shape[0])
    result, kept = forward_pass(
        tokens.astype(jnp.float32), gathered, a_log, dt_bias, skip_d, segment, position
    )
    matrices = (
        gathered[1],
        gathered[5],
        gathered[6],
        gathered[7],
        gathered[8],
        gathered[9],
        gathered[11],
        gathered[12],
        gathered[13],
    )
    tokens_grad, factors, small, head_grads = backward_pass(cotangent, matrices, skip_d, kept)
    (
        normed,
        model_right,
        normed_two,
        feed_right,
        gated,
        branch_grad,
        head_rows_out,
        hidden,
        feed_grad,
    ) = factors
    grad_a_log, grad_dt_bias, grad_skip = head_grads
    model_share = lax.psum_scatter(
        model_rows(factors).astype(jnp.bfloat16), "shard", scatter_dimension=0, tiled=True
    )
    out_share = lax.psum_scatter(
        matmul_left(gated, branch_grad).astype(jnp.bfloat16),
        "shard",
        scatter_dimension=0,
        tiled=True,
    )
    attn_share = lax.psum_scatter(
        matmul_left(head_rows_out, branch_grad).astype(jnp.bfloat16),
        "shard",
        scatter_dimension=0,
        tiled=True,
    )
    down_share = lax.psum_scatter(
        matmul_left(hidden, feed_grad).astype(jnp.bfloat16),
        "shard",
        scatter_dimension=0,
        tiled=True,
    )
    small_part = (
        lax.psum_scatter(
            small[0].astype(jnp.bfloat16), "shard", scatter_dimension=0, tiled=True
        ).astype(jnp.float32),
        lax.psum_scatter(
            small[1].astype(jnp.bfloat16), "shard", scatter_dimension=1, tiled=True
        ).astype(jnp.float32),
        lax.psum_scatter(
            small[2].astype(jnp.bfloat16), "shard", scatter_dimension=0, tiled=True
        ).astype(jnp.float32),
        lax.psum_scatter(
            small[3].astype(jnp.bfloat16), "shard", scatter_dimension=0, tiled=True
        ).astype(jnp.float32),
        lax.psum_scatter(
            small[4].astype(jnp.bfloat16), "shard", scatter_dimension=0, tiled=True
        ).astype(jnp.float32),
    )
    summed = (
        lax.psum(model_share, "replica").astype(jnp.float32),
        lax.psum(out_share, "replica").astype(jnp.float32),
        lax.psum(attn_share, "replica").astype(jnp.float32),
        lax.psum(down_share, "replica").astype(jnp.float32),
        lax.psum(small_part[0].astype(jnp.bfloat16), "replica").astype(jnp.float32),
        lax.psum(small_part[1].astype(jnp.bfloat16), "replica").astype(jnp.float32),
        lax.psum(small_part[2].astype(jnp.bfloat16), "replica").astype(jnp.float32),
        lax.psum(small_part[3].astype(jnp.bfloat16), "replica").astype(jnp.float32),
        lax.psum(small_part[4].astype(jnp.bfloat16), "replica").astype(jnp.float32),
    )
    model_parts = split_model(summed[0])
    mats = (
        model_parts[0],
        summed[1],
        model_parts[1],
        model_parts[2],
        model_parts[3],
        summed[2],
        model_parts[4],
        model_parts[5],
        summed[3],
    )
    small_owned = (summed[4], summed[5], summed[6], summed[7], summed[8])
    head_total = lax.psum((grad_a_log, grad_dt_bias, grad_skip), ("shard", "replica"))
    return (
        result,
        tokens_grad,
        small_owned[0],
        mats[0],
        small_owned[1],
        small_owned[2],
        head_total[0],
        head_total[1],
        head_total[2],
        small_owned[3],
        mats[1],
        mats[2],
        mats[3],
        mats[4],
        mats[5],
        small_owned[4],
        mats[6],
        mats[7],
        mats[8],
    )


def solution(mesh):
    in_specs = (
        P(("shard", "replica"), None),
        P(("shard", "replica"), None),
        P(("shard", "replica"), None),
        P(("shard", "replica"), None),
        P("shard"),
        P("shard", None),
        P(None, "shard"),
        P("shard"),
        P(),
        P(),
        P(),
        P("shard"),
        P("shard", None),
        P("shard", None),
        P("shard", None),
        P("shard", None),
        P("shard", None),
        P("shard"),
        P("shard", None),
        P("shard", None),
        P("shard", None),
    )
    out_specs = (
        P(("shard", "replica"), None),
        P(("shard", "replica"), None),
        P("shard"),
        P("shard", None),
        P(None, "shard"),
        P("shard"),
        P(),
        P(),
        P(),
        P("shard"),
        P("shard", None),
        P("shard", None),
        P("shard", None),
        P("shard", None),
        P("shard", None),
        P("shard"),
        P("shard", None),
        P("shard", None),
        P("shard", None),
    )
    return jax.shard_map(shards, mesh=mesh, in_specs=in_specs, out_specs=out_specs, check_vma=False)
```

profile of v0, /device:TPU:0, one launch (start us, length us, event | category | flops | bytes accessed | tf_op | source)
XLA Modules:
  0.0 1295.3 jit_solution(15994099488136674309)
XLA Ops:
  12.2 27.9 %all-gather = bf16[8,224,4]{1,2,0:T(4,128)(2,1)S(1)} all-gather(bf16[1,224,4]{1,2,0:T(4,128)(2,1)S(1)} %bitcast.206), channel_id=1, replica_groups=mesh['shard'=8,'replica'=4] {'shard'}, dimensions={0}, use_global_device_ids=true | all-gather | bytes 16128 | tf_op jit(solution)/shard_map/all_gather | solution.py:399
  40.2 31.4 %all_gather.48 = bf16[1024,128]{1,0:T(8,128)(2,1)S(1)} all-gather(bf16[128,128]{1,0:T(8,128)(2,1)S(1)} %copy-done.82), channel_id=1, replica_groups=mesh['shard'=8,'replica'=4] {'shard'}, dimensions={0}, use_global_device_ids=true | all-gather | bytes 294912 | tf_op jit(solution)/shard_map/all_gather | solution.py:405
  71.6 31.5 %all_gather.49 = bf16[1024,128]{1,0:T(8,128)(2,1)S(1)} all-gather(bf16[128,128]{1,0:T(8,128)(2,1)S(1)} %copy-done.83), channel_id=1, replica_groups=mesh['shard'=8,'replica'=4] {'shard'}, dimensions={0}, use_global_device_ids=true | all-gather | bytes 294912 | tf_op jit(solution)/shard_map/all_gather | solution.py:404
  103.8 18.8 %all-gather.1 = bf16[8,1,128]{2,1,0:T(2,128)(2,1)S(1)} all-gather(bf16[1,1,128]{2,1,0:T(2,128)(2,1)S(1)} %bitcast.208), channel_id=1, replica_groups=mesh['shard'=8,'replica'=4] {'shard'}, dimensions={0}, use_global_device_ids=true | all-gather | bytes 2304 | tf_op jit(solution)/shard_map/all_gather | solution.py:397
  125.1 18.1 %all-reduce.24 = (bf16[1792]{0:T(1024)(128)(2,1)S(1)}, bf16[1536]{0:T(1024)(128)(2,1)S(1)}) all-reduce(bf16[1792]{0:T(1024)(128)(2,1)S(1)} %dynamic-update-slice, bf16[1536]{0:T(1024)(128)(2,1)S(1)} %dynamic-update-slice.1), channel_id=1, replica_groups=mesh['shard'=8,'replica'=4] {'shard'}, use_global_device_ids=true, to_apply=%add.16 | all-reduce | flops 3328 | bytes 13312
  143.4 21.5 %all-gather.2 = bf16[8,1,128]{2,1,0:T(2,128)(2,1)S(1)} all-gather(bf16[1,1,128]{2,1,0:T(2,128)(2,1)S(1)} %bitcast.209), channel_id=1, replica_groups=mesh['shard'=8,'replica'=4] {'shard'}, dimensions={0}, use_global_device_ids=true | all-gather | bytes 2304 | tf_op jit(solution)/shard_map/all_gather | solution.py:407
  173.3 5.3 fusion.93
  182.2 4.8 multiply_convert_fusion.3
  189.8 37.4 %all-gather.13.cloned.1.call-done = bf16[1536,1024]{1,0:T(8,128)(2,1)} async-done(((bf16[192,1024]{1,0:T(8,128)(2,1)}), bf16[1536,1024]{1,0:T(8,128)(2,1)}) %all-gather.13.cloned.1.call-update) | async-done | bytes 3145744 | tf_op jit(solution)/shard_map/all_gather | solution.py:402
  230.1 37.9 %all-gather.17.cloned.1.call-done = bf16[512,1024]{1,0:T(8,128)(2,1)} async-done(((bf16[64,1024]{1,0:T(8,128)(2,1)}), bf16[512,1024]{1,0:T(8,128)(2,1)}) %all-gather.17.cloned.1.call-update) | async-done | bytes 1048592 | tf_op jit(solution)/shard_map/all_gather | solution.py:406
  270.3 71.8 %all-gather.19.cloned.1.call-done = bf16[1024,2048]{1,0:T(8,128)(2,1)} async-done(((bf16[128,2048]{1,0:T(8,128)(2,1)}), bf16[1024,2048]{1,0:T(8,128)(2,1)}) %all-gather.19.cloned.1.call-update) | async-done | bytes 4194320 | tf_op jit(solution)/shard_map/all_gather | solution.py:408
  342.1 3.9 fusion.105
  346.0 69.8 %all-gather.21.cloned.1.call-done = bf16[1024,2048]{1,0:T(8,128)(2,1)} async-done(((bf16[128,2048]{1,0:T(8,128)(2,1)}), bf16[1024,2048]{1,0:T(8,128)(2,1)}) %all-gather.21.cloned.1.call-update) | async-done | bytes 4194320 | tf_op jit(solution)/shard_map/all_gather | solution.py:409
  415.8 3.9 fusion.106
  419.7 69.9 %all-gather.23.cloned.1.call-done = bf16[2048,1024]{1,0:T(8,128)(2,1)} async-done(((bf16[256,1024]{1,0:T(8,128)(2,1)}), bf16[2048,1024]{1,0:T(8,128)(2,1)}) %all-gather.23.cloned.1.call-update) | async-done | bytes 4194320 | tf_op jit(solution)/shard_map/all_gather | solution.py:410
  489.6 5.5 multiply_convert_fusion.1
  516.6 5.7 convolution_convert_fusion.1
  543.4 3.8 convolution_convert_fusion
  547.2 51.9 %pad_maximum_fusion = bf16[1024,8216]{0,1:T(8,128)(2,1)} fusion(bf16[1024,4096]{0,1:T(8,128)(2,1)S(1)} %bitcast.161, bf16[1024,4120]{0,1:T(8,128)(2,1)S(1)} %convolution_convert_fusion), kind=kLoop, calls=%fused_computation.1 | loop fusion | flops 33652736 | bytes 33652736 | tf_op jit(solution)/shard_map/concatenate | solution.py:354
  599.1 20.8 %copy.160 = bf16[1024,8216]{1,0:T(8,128)(2,1)} copy(bf16[1024,8216]{0,1:T(8,128)(2,1)} %pad_maximum_fusion) | data formatting | bytes 33652736
  634.0 41.2 %all-reduce.22 = (f32[24]{0:T(128)}, f32[24]{0:T(128)}, f32[24]{0:T(128)}) all-reduce(f32[24]{0:T(128)S(1)} %negate_multiply_fusion, f32[24]{0:T(128)S(1)} %copy-done.118, f32[24]{0:T(128)S(1)} %reduce_sum.273), channel_id=1, replica_groups=mesh['shard'=8,'replica'=4] {'shard','replica'}, use_global_device_ids=true, to_apply=%region_32.33 | all-reduce | flops 72 | bytes 576 | tf_op jit(solution)/shard_map/psum | solution.py:502
  675.2 231.2 %reduce-scatter.16.cloned.1.call-done = bf16[128,8216]{1,0:T(8,128)(2,1)} async-done(((bf16[1024,8216]{1,0:T(8,128)(2,1)}), bf16[128,8216]{1,0:T(8,128)(2,1)}) %reduce-scatter.16.cloned.1.call-update) | async-done | bytes 2103312
  906.4 4.1 copy.161
  910.6 62.6 %reduce-scatter.12.cloned.1.call-done = bf16[64,1024]{1,0:T(8,128)(2,1)} async-done(((bf16[512,1024]{1,0:T(8,128)(2,1)}), bf16[64,1024]{1,0:T(8,128)(2,1)}) %reduce-scatter.12.cloned.1.call-update) | async-done | bytes 131088 | tf_op jit(solution)/shard_map/reduce_scatter | solution.py:449
  973.2 76.8 %reduce-scatter.10.cloned.1.call-done = bf16[192,1024]{1,0:T(8,128)(2,1)} async-done(((bf16[1536,1024]{1,0:T(8,128)(2,1)}), bf16[192,1024]{1,0:T(8,128)(2,1)}) %reduce-scatter.10.cloned.1.call-update) | async-done | bytes 393232 | tf_op jit(solution)/shard_map/reduce_scatter | solution.py:443
  1049.9 90.7 %reduce-scatter.14.cloned.1.call-done = bf16[256,1024]{1,0:T(8,128)(2,1)} async-done(((bf16[2048,1024]{1,0:T(8,128)(2,1)}), bf16[256,1024]{1,0:T(8,128)(2,1)}) %reduce-scatter.14.cloned.1.call-update) | async-done | bytes 524304 | tf_op jit(solution)/shard_map/reduce_scatter | solution.py:455
  1140.7 4.3 fusion.28
  1146.5 36.1 %all-reduce.23 = (bf16[1024]{0:T(1024)(128)(2,1)S(1)}, bf16[1792]{0:T(1024)(128)(2,1)S(1)}, bf16[1536]{0:T(1024)(128)(2,1)S(1)}, bf16[1024]{0:T(1024)(128)(2,1)S(1)}) all-reduce(bf16[1024]{0:T(1024)(128)(2,1)S(1)} %get-tuple-element.126, bf16[1792]{0:T(1024)(128)(2,1)S(1)} %copy-done.89, ...), channel_id=2, replica_groups=mesh['shard'=8,'replica'=4] {'shard'}, use_global_device_ids=true, to_apply=%region_18.19.clone | all-reduce | flops 5376 | bytes 21504
  1184.8 3.6 fusion.10
  1188.5 17.8 %reduce-scatter.18.cloned.1.call-done = bf16[224,4]{1,0:T(8,128)(2,1)} async-done(((bf16[1792,4]{1,0:T(8,128)(2,1)}), bf16[224,4]{1,0:T(8,128)(2,1)}) %reduce-scatter.18.cloned.1.call-update) | async-done | bytes 1808
  1207.2 5.7 all-reduce.25
  1215.6 61.6 %all-reduce.29.cloned.1.call-done = (bf16[128,8216]{0,1:T(8,128)(2,1)}, bf16[192,1024]{1,0:T(8,128)(2,1)}, bf16[64,1024]{1,0:T(8,128)(2,1)}, bf16[256,1024]{1,0:T(8,128)(2,1)}) async-done(((bf16[128,8216]{0,1:T(8,128)(2,1)}, bf16[192,1024]{1,0:T(8,128)(2,1)}, bf16[64,1024]{1,0:T(8,128)(2,1)}, bf16[256,1024]{1,0:T(8,128)(2,1)}), (bf16[128,8216]{0,1:T(8,128)(2,1)}, bf16[192,1024]{1,0:T(8,128)(2,1)}, ...) | async-done | bytes 3151888 | tf_op jit(solution)/shard_map/psum | solution.py:479
  (436 shorter events, 98.8 us)
Async XLA Ops:
  7.2 161.8 %all-gather.15.cloned.1.call-start = ((), (), s32[]{:S(2)}) async-start(), calls=%async_computation.7 | async-start | bytes 1179648 | tf_op jit(solution)/shard_map/all_gather | solution.py:403
  8.0 95.8 %copy-start.125 = (bf16[128]{0:T(256)(128)(2,1)S(1)}, bf16[128]{0:T(256)(128)(2,1)}, u32[]{:S(2)}) copy-start(bf16[128]{0:T(256)(128)(2,1)} %param.25) | copy-start | bytes 772
  8.0 114.7 %copy-start.115 = (u32[32]{0:T(128)S(1)}, u32[32]{0:T(128)}, u32[]{:S(2)}) copy-start(u32[32]{0:T(128)} %constant.108) | copy-start | bytes 388
  8.0 116.6 %copy-start.131 = (bf16[224]{0:T(256)(128)(2,1)S(1)}, bf16[224]{0:T(256)(128)(2,1)}, u32[]{:S(2)}) copy-start(bf16[224]{0:T(256)(128)(2,1)} %param.28) | copy-start | bytes 1348
  8.0 116.8 %copy-start.132 = (bf16[192]{0:T(256)(128)(2,1)S(1)}, bf16[192]{0:T(256)(128)(2,1)}, u32[]{:S(2)}) copy-start(bf16[192]{0:T(256)(128)(2,1)} %param.32) | copy-start | bytes 1156
  8.0 135.4 %copy-start.126 = (bf16[128]{0:T(256)(128)(2,1)S(1)}, bf16[128]{0:T(256)(128)(2,1)}, u32[]{:S(2)}) copy-start(bf16[128]{0:T(256)(128)(2,1)} %param.38) | copy-start | bytes 772
  8.0 165.3 %all-gather.11.cloned.1.call-start = ((), (), s32[]{:S(2)}) async-start(), calls=%async_computation.5 | async-start | bytes 7723008 | tf_op jit(solution)/shard_map/all_gather | solution.py:398
  8.8 158.7 %copy-start.2 = (bf16[128,1024]{1,0:T(8,128)(2,1)S(1)}, bf16[128,1024]{1,0:T(8,128)(2,1)}, u32[]{:S(2)}) copy-start(bf16[128,1024]{1,0:T(8,128)(2,1)} %param.21) | copy-start | bytes 786436
  8.8 158.8 %copy-start.135 = (f32[24]{0:T(128)S(1)}, f32[24]{0:T(128)}, u32[]{:S(2)}) copy-start(f32[24]{0:T(128)} %param.29) | copy-start | bytes 292
  8.8 218.4 %all-gather.13.cloned.1.call-start = ((), (), s32[]{:S(2)}) async-start(), calls=%async_computation.6 | async-start | bytes 3538944 | tf_op jit(solution)/shard_map/all_gather | solution.py:402
  9.5 258.4 %all-gather.17.cloned.1.call-start = ((), (), s32[]{:S(2)}) async-start(), calls=%async_computation.8 | async-start | bytes 1179648 | tf_op jit(solution)/shard_map/all_gather | solution.py:406
  10.1 332.0 %all-gather.19.cloned.1.call-start = ((), (), s32[]{:S(2)}) async-start(), calls=%async_computation.9 | async-start | bytes 4718592 | tf_op jit(solution)/shard_map/all_gather | solution.py:408
  10.7 405.1 %all-gather.21.cloned.1.call-start = ((), (), s32[]{:S(2)}) async-start(), calls=%async_computation.10 | async-start | bytes 4718592 | tf_op jit(solution)/shard_map/all_gather | solution.py:409
  11.3 478.3 %all-gather.23.cloned.1.call-start = ((), (), s32[]{:S(2)}) async-start(), calls=%async_computation.11 | async-start | bytes 4718592 | tf_op jit(solution)/shard_map/all_gather | solution.py:410
  12.0 894.4 %reduce-scatter.16.cloned.1.call-start = ((), (), s32[]{:S(2)}) async-start(), calls=%async_computation.15 | async-start | bytes 19169280
  40.2 131.9 %copy-start.68 = (pred[128,128]{0,1:T(8,128)(4,1)}, pred[128,128]{0,1:T(8,128)(4,1)S(1)}, u32[]{:S(2)}) copy-start(pred[128,128]{0,1:T(8,128)(4,1)S(1)} %fusion.56) | copy-start | bytes 49156
  71.6 99.2 %copy-start.33 = (bf16[1024,128]{1,0:T(8,128)(2,1)}, bf16[1024,128]{1,0:T(8,128)(2,1)S(1)}, u32[]{:S(2)}) copy-start(bf16[1024,128]{1,0:T(8,128)(2,1)S(1)} %all_gather.48) | copy-start | bytes 786436
  103.7 78.4 %copy-start.102 = (pred[128]{0:T(512)(128)(4,1)}, pred[128]{0:T(512)(128)(4,1)S(1)}, u32[]{:S(2)}) copy-start(pred[128]{0:T(512)(128)(4,1)S(1)} %get-tuple-element.193) | copy-start | bytes 388
  103.7 78.4 %copy-start.104 = (pred[128]{0:T(512)(128)(4,1)}, pred[128]{0:T(512)(128)(4,1)S(1)}, u32[]{:S(2)}) copy-start(pred[128]{0:T(512)(128)(4,1)S(1)} %get-tuple-element.194) | copy-start | bytes 388
  103.7 78.4 %copy-start.106 = (pred[128]{0:T(512)(128)(4,1)}, pred[128]{0:T(512)(128)(4,1)S(1)}, u32[]{:S(2)}) copy-start(pred[128]{0:T(512)(128)(4,1)S(1)} %get-tuple-element.195) | copy-start | bytes 388
  143.4 83.8 %copy-start.54 = (f32[1536]{0:T(1024)}, f32[1536]{0:T(1024)S(1)}, u32[]{:S(2)}) copy-start(f32[1536]{0:T(1024)S(1)} %convert_element_type.206) | copy-start | bytes 18436
  269.7 230.2 %copy-start.4 = (f32[128,1024]{1,0:T(8,128)}, f32[128,1024]{1,0:T(8,128)S(1)}, u32[]{:S(2)}) copy-start(f32[128,1024]{1,0:T(8,128)S(1)} %get-tuple-element.199) | copy-start | bytes 1572868
  269.7 72.4 %copy-start.108 = (f32[128]{0:T(128)}, f32[128]{0:T(128)S(1)}, u32[]{:S(2)}) copy-start(f32[128]{0:T(128)S(1)} %fusion.73) | copy-start | bytes 1540
  346.0 143.6 %copy-start.29 = (bf16[128,1024]{1,0:T(8,128)(2,1)S(1)}, bf16[128,1024]{1,0:T(8,128)(2,1)}, u32[]{:S(2)}) copy-start(bf16[128,1024]{1,0:T(8,128)(2,1)} %param.22) | copy-start | bytes 786436
  620.0 353.2 %reduce-scatter.12.cloned.1.call-start = ((), (), s32[]{:S(2)}) async-start(), calls=%async_computation.13 | async-start | bytes 1179648 | tf_op jit(solution)/shard_map/reduce_scatter | solution.py:449
  622.3 427.6 %reduce-scatter.10.cloned.1.call-start = ((), (), s32[]{:S(2)}) async-start(), calls=%async_computation.12 | async-start | bytes 3538944 | tf_op jit(solution)/shard_map/reduce_scatter | solution.py:443
  625.2 515.4 %reduce-scatter.14.cloned.1.call-start = ((), (), s32[]{:S(2)}) async-start(), calls=%async_computation.14 | async-start | bytes 4718592 | tf_op jit(solution)/shard_map/reduce_scatter | solution.py:455
  629.9 576.4 %reduce-scatter.18.cloned.1.call-start = ((), (), s32[]{:S(2)}) async-start(), calls=%async_computation.16 | async-start | bytes 516096
  633.7 643.5 %all-reduce.29.cloned.1.call-start = ((), (), s32[]{:S(2)}) async-start(), calls=%async_computation.17 | async-start | bytes 6303744 | tf_op jit(solution)/shard_map/psum | solution.py:479
  910.6 230.1 %copy-start.20 = (bf16[128,1536]{0,1:T(8,128)(2,1)S(1)}, bf16[128,1536]{0,1:T(8,128)(2,1)}, u32[]{:S(2)}) copy-start(bf16[128,1536]{0,1:T(8,128)(2,1)} %get-tuple-element.169) | copy-start | bytes 1179652
  910.6 230.1 %copy-start.28 = (bf16[128,1792]{0,1:T(8,128)(2,1)S(1)}, bf16[128,1792]{0,1:T(8,128)(2,1)}, u32[]{:S(2)}) copy-start(bf16[128,1792]{0,1:T(8,128)(2,1)} %get-tuple-element.159) | copy-start | bytes 1376260
  910.6 230.1 %copy-start.87 = (bf16[128,24]{0,1:T(8,128)(2,1)S(1)}, bf16[128,24]{0,1:T(8,128)(2,1)}, u32[]{:S(2)}) copy-start(bf16[128,24]{0,1:T(8,128)(2,1)} %get-tuple-element.157) | copy-start | bytes 18436
  (121 other events, 836.4 us)
Sparse Core Ops, SparseCore 0:
  10.2 43.6 all-gather.14
  55.9 110.2 all-gather.10
  168.4 58.6 all-gather.12
  229.2 38.7 all-gather.16
  269.9 72.1 all-gather.18
  344.1 71.6 all-gather.20
  417.9 71.6 all-gather.22
  620.1 286.3 reduce-scatter.15
  910.8 62.3 reduce-scatter.11
  976.6 73.2 reduce-scatter.9
  1053.6 86.9 reduce-scatter.13
  1144.7 61.5 reduce-scatter.17
  1208.9 68.3 all-reduce.28
where the time goes:
time: 1300 us
  waiting for transfers between devices  832 us (64%)
  blocking collectives  232 us (18%)
  other arithmetic  85.3 us (7%)
  matrix products  71.6 us (6%)
  local copies, waits for them, and re-layouts  54.5 us (4%)
  between operations  19.2 us (1%)
    unnamed x15, waiting for transfers between devices  253 us
    reduce_scatter x1, waiting for transfers between devices, shards(): lax.psum_scatter(matmul_left(hidden, feed_grad).astype(jnp.bfloat16), 'sh...  90.7 us
    reduce_scatter x1, waiting for transfers between devices, shards(): lax.psum_scatter(matmul_left(gated, branch_grad).astype(jnp.bfloat16), 's...  76.8 us
    all_gather x1, waiting for transfers between devices, shards(): lax.all_gather(w_gate, 'shard', axis=0, tiled=True)  71.8 us
    all_gather x1, waiting for transfers between devices, shards(): lax.all_gather(w_down, 'shard', axis=0, tiled=True)  69.9 us
    all_gather x1, waiting for transfers between devices, shards(): lax.all_gather(w_up, 'shard', axis=0, tiled=True)  69.8 us
    reduce_scatter x1, waiting for transfers between devices, shards(): lax.psum_scatter(matmul_left(head_rows_out, branch_grad).astype(jnp.bfloa...  62.6 us
    psum x1, waiting for transfers between devices, shards(): lax.psum(model_share, 'replica').astype(jnp.float32)  61.6 us
  transfers between devices with their start and end apart: 13, of which 11 were waited for; matrix products, arithmetic and copies ran while one was open for 5% of the time, Pallas kernels for 0%

commit v1 on v0

--- a/solution.py
+++ b/solution.py
@@ -1,6 +1,8 @@
 import jax
 import jax.numpy as jnp
 from jax import lax
+from jax.experimental import pallas as pl
+from jax.experimental.pallas import tpu as pltpu
 from jax.sharding import PartitionSpec as P
 
 FF = 2048
@@ -112,31 +114,31 @@
     return exp_scores / jnp.sum(exp_scores, axis=-1, keepdims=True)
 
 
-def forward_pass(tokens_f, gathered, a_log, dt_bias, skip_d, segment, position):
-    (
-        in_gain,
-        w_in,
-        conv_w,
-        conv_b,
-        ssm_gain,
-        w_out,
-        w_query,
-        w_key,
-        w_value,
-        w_attn_out,
-        ff_gain,
-        w_gate,
-        w_up,
-        w_down,
-    ) = gathered
+def join_rows(gated, heads, parts):
+    extent = gated.shape[0]
+    return jnp.concatenate(
+        [gated.reshape(extent, parts, -1), heads.reshape(extent, parts, -1)], axis=2
+    ).reshape(extent, -1)
+
+
+def split_rows(joined, parts):
+    extent = joined.shape[0]
+    shaped = joined.reshape(extent, parts, -1)
+    cut = MH * HD // parts
+    return shaped[:, :, :cut].reshape(extent, -1), shaped[:, :, cut:].reshape(extent, -1)
+
+
+def forward_pass(tokens_f, gains, mats, a_log, dt_bias, skip_d, segment, position, parts):
+    in_gain, conv_w, conv_b, ssm_gain, ff_gain, w_raw = gains
+    w_conv, w_z, w_qkv, w_cat, w_gate, w_up, w_down = mats
     extent = tokens_f.shape[0]
     width = MH * HD
+    q_cols = QH * ATTENTION_HEAD
+    k_cols = KVH * ATTENTION_HEAD
     normed_f, pull_norm_one = jax.vjp(rms_scale, tokens_f, in_gain.astype(jnp.float32))
     normed = normed_f.astype(jnp.bfloat16)
-    mixed_in = matmul_plain(normed, w_in)
-    gate_z = mixed_in[:, :width]
-    conv_in = mixed_in[:, width : 2 * width + 2 * NS]
-    raw_step = mixed_in[:, 2 * width + 2 * NS :]
+    conv_in = matmul_plain(normed, w_conv)
+    raw_step = matmul_right(normed, w_raw)
 
     def front(conv_value, step_value, tap_value, bias_value, shift_value, rate_value):
         return mixer_front(
@@ -165,12 +167,13 @@
     scan_out = (scan_out + skip_d[None, :, None] * x_heads.astype(jnp.float32)).reshape(
         extent, width
     )
+    gate_z = matmul_plain(normed, w_z)
     gated_f, pull_gate = jax.vjp(gate_norm, scan_out, gate_z, ssm_gain.astype(jnp.float32))
     gated = gated_f.astype(jnp.bfloat16)
-    mixer_out = matmul_plain(gated, w_out)
-    query = matmul_plain(normed, w_query)
-    key_proj = matmul_plain(normed, w_key)
-    value_proj = matmul_plain(normed, w_value)
+    qkv = matmul_plain(normed, w_qkv)
+    query = qkv[:, :q_cols]
+    key_proj = qkv[:, q_cols : q_cols + k_cols]
+    value_proj = qkv[:, q_cols + k_cols :]
 
     def turn(query_value, key_value):
         return (rotate(query_value, position, QH), rotate(key_value, position, KVH))
@@ -185,8 +188,8 @@
         "lwmi,ilu->mlwu", probability_reduced, value_reduced, preferred_element_type=jnp.float32
     )
     head_rows_out = head_rows_out.astype(jnp.bfloat16).reshape(extent, QH * ATTENTION_HEAD)
-    attn_out = matmul_plain(head_rows_out, w_attn_out)
-    residual = tokens_f + mixer_out + attn_out
+    joined = join_rows(gated, head_rows_out, parts)
+    residual = tokens_f + matmul_plain(joined, w_cat)
     normed_two_f, pull_norm_two = jax.vjp(rms_scale, residual, ff_gain.astype(jnp.float32))
     normed_two = normed_two_f.astype(jnp.bfloat16)
     gate_val = matmul_plain(normed_two, w_gate)
@@ -209,14 +212,13 @@
         scaled_x,
         time_step,
         pull_gate,
-        gated,
+        joined,
         pull_rotate,
         query_reduced,
         key_reduced,
         value_reduced,
         prob_all,
         probability_reduced,
-        head_rows_out,
         pull_norm_two,
         normed_two,
         pull_swiglu,
@@ -226,8 +228,8 @@
     return (result, kept)
 
 
-def backward_pass(cotangent, matrices, skip_d, kept):
-    w_in, w_out, w_query, w_key, w_value, w_attn_out, w_gate, w_up, w_down = matrices
+def backward_pass(cotangent, w_raw, mats, skip_d, kept, parts):
+    w_conv, w_z, w_qkv, w_cat, w_gate, w_up, w_down = mats
     (
         pull_norm_one,
         normed,
@@ -241,14 +243,13 @@
         scaled_x,
         time_step,
         pull_gate,
-        gated,
+        joined,
         pull_rotate,
         query_reduced,
         key_reduced,
         value_reduced,
         prob_all,
         probability_reduced,
-        head_rows_out,
         pull_norm_two,
         normed_two,
         pull_swiglu,
@@ -266,10 +267,9 @@
     residual_part, grad_ff_gain = pull_norm_two(normed_two_grad)
     residual_grad = out_grad + residual_part
     branch_grad = residual_grad.astype(jnp.bfloat16)
-    head_rows_grad = (
-        matmul_right(branch_grad, w_attn_out)
-        .astype(jnp.bfloat16)
-        .reshape(extent, KVH, QH // KVH, ATTENTION_HEAD)
+    gated_grad, heads_grad = split_rows(matmul_right(branch_grad, w_cat), parts)
+    head_rows_grad = heads_grad.astype(jnp.bfloat16).reshape(
+        extent, KVH, QH // KVH, ATTENTION_HEAD
     )
     probability_grad = jnp.einsum(
         "khei,whi->hekw", head_rows_grad, value_reduced, preferred_element_type=jnp.float32
@@ -291,12 +291,8 @@
     query_low = query_grad.astype(jnp.bfloat16)
     key_low = key_grad.astype(jnp.bfloat16)
     value_low = value_grad.reshape(extent, KVH * ATTENTION_HEAD).astype(jnp.bfloat16)
-    normed_grad = (
-        matmul_right(query_low, w_query)
-        + matmul_right(key_low, w_key)
-        + matmul_right(value_low, w_value)
-    )
-    gated_grad = matmul_right(branch_grad, w_out)
+    qkv_low = jnp.concatenate([query_low, key_low, value_low], axis=1)
+    normed_grad = matmul_right(qkv_low, w_qkv)
     scan_grad, gate_z_grad, grad_ssm_gain = pull_gate(gated_grad)
     scan_low = scan_grad.astype(jnp.bfloat16).reshape(extent, MH, HD)
     weight_grad = jnp.einsum("thd,shd->hts", scan_low, scaled_x, preferred_element_type=jnp.float32)
@@ -316,61 +312,206 @@
     conv_grad, raw_grad, grad_conv_w, grad_conv_b, grad_dt_bias, grad_a_log = pull_front(
         (act_grad, step_grad, decay_grad)
     )
-    mixed_low = jnp.concatenate([gate_z_grad, conv_grad, raw_grad], axis=1).astype(jnp.bfloat16)
-    normed_grad = normed_grad + matmul_right(mixed_low, w_in)
+    z_low = gate_z_grad.astype(jnp.bfloat16)
+    conv_low = conv_grad.astype(jnp.bfloat16)
+    raw_low = raw_grad.astype(jnp.bfloat16)
+    normed_grad = (
+        normed_grad
+        + matmul_right(z_low, w_z)
+        + matmul_right(conv_low, w_conv)
+        + matmul_plain(raw_low, w_raw)
+    )
     token_part, grad_in_gain = pull_norm_one(normed_grad)
     tokens_grad = (residual_grad + token_part).astype(jnp.bfloat16)
-    model_right = jnp.concatenate([mixed_low, query_low, key_low, value_low], axis=1)
-    feed_right = jnp.concatenate([gate_low, up_low], axis=1)
-    factors = (
-        normed,
-        model_right,
-        normed_two,
-        feed_right,
-        gated,
-        branch_grad,
-        head_rows_out,
-        hidden,
-        feed_grad,
-    )
-    small = (grad_in_gain, grad_conv_w, grad_conv_b, grad_ssm_gain, grad_ff_gain)
-    return (tokens_grad, factors, small, (grad_a_log, grad_dt_bias, grad_skip))
-
-
-def model_rows(factors):
-    (
-        normed,
-        model_right,
-        normed_two,
-        feed_right,
-        gated,
-        branch_grad,
-        head_rows_out,
-        hidden,
-        feed_grad,
-    ) = factors
-    first = matmul_left(normed, model_right)
-    second = matmul_left(normed_two, feed_right)
-    return jnp.concatenate([first, second], axis=1)
-
-
-def split_model(joined):
-    in_cols = 2 * MH * HD + 2 * NS + MH
-    query_cols = QH * ATTENTION_HEAD
-    key_cols = KVH * ATTENTION_HEAD
-    edges = (
-        0,
-        in_cols,
-        in_cols + query_cols,
-        in_cols + query_cols + key_cols,
-        in_cols + query_cols + 2 * key_cols,
-        in_cols + query_cols + 2 * key_cols + FF,
-        in_cols + query_cols + 2 * key_cols + 2 * FF,
-    )
-    return tuple((joined[:, edges[index] : edges[index + 1]] for index in range(6)))
+    raw_rows = matmul_left(raw_low, normed)
+    pairs = (
+        (hidden, feed_grad),
+        (normed_two, jnp.concatenate([gate_low, up_low], axis=1)),
+        (joined, branch_grad),
+        (normed, jnp.concatenate([z_low, query_low], axis=1)),
+        (normed, jnp.concatenate([conv_low, key_low, value_low], axis=1)),
+    )
+    small = (
+        grad_in_gain,
+        grad_conv_w,
+        grad_conv_b,
+        grad_ssm_gain,
+        grad_ff_gain,
+        raw_rows,
+        grad_a_log,
+        grad_dt_bias,
+        grad_skip,
+    )
+    return (tokens_grad, pairs, small)
+
+
+AXES = ("shard", "replica")
+
+
+def place(pieces, positions, dim, count):
+    shape = list(pieces[0].shape)
+    shape[dim] = count
+    total = len(pieces)
+
+    def body(where, *refs):
+        out, sems = refs[total], refs[total + 1]
+        copies = []
+        for number in range(total):
+            spot = (slice(None),) * dim + (pl.ds(where[number], 1),)
+            copies.append(
+                pltpu.make_async_copy(refs[number], out.at[spot], sems.at[number])
+            )
+        for copy in copies:
+            copy.start()
+        for copy in copies:
+            copy.wait()
+
+    moved = 2 * sum(piece.size * piece.dtype.itemsize for piece in pieces)
+    return pl.pallas_call(
+        body,
+        out_shape=jax.ShapeDtypeStruct(tuple(shape), pieces[0].dtype),
+        in_specs=[pl.BlockSpec(memory_space=pltpu.SMEM)]
+        + [pl.BlockSpec(memory_space=pl.ANY)] * total,
+        out_specs=pl.BlockSpec(memory_space=pl.ANY),
+        scratch_shapes=[pltpu.SemaphoreType.DMA((total,))],
+        cost_estimate=pl.CostEstimate(flops=0, bytes_accessed=moved, transcendentals=0),
+        name="place",
+    )(jnp.stack(positions).astype(jnp.int32), *pieces)
+
+
+class Links:
+    def __init__(self, shards_of, copies):
+        self.z_size = shards_of // 2
+        shard = lax.axis_index("shard")
+        replica = lax.axis_index("replica")
+        self.z, self.x = shard // 2, shard % 2
+        self.y, self.c = replica // 2, replica % 2
+        everyone = [(s, r) for s in range(shards_of) for r in range(copies)]
+
+        def table(step):
+            return [(s * copies + r, step(s, r)) for s, r in everyone]
+
+        self.tables = {
+            "x": table(lambda s, r: (s ^ 1) * copies + r),
+            "y": table(lambda s, r: s * copies + (r ^ 2)),
+            "c": table(lambda s, r: s * copies + (r ^ 1)),
+            "z": table(lambda s, r: ((s + 2) % shards_of) * copies + r),
+        }
+
+    def send(self, value, axis):
+        return lax.ppermute(value, AXES, self.tables[axis])
+
+    def spread(self, value, axis):
+        if axis == "z":
+            pieces, spots = [value], [self.z]
+            for step in range(1, self.z_size):
+                pieces.append(self.send(pieces[-1], "z"))
+                spots.append((self.z + self.z_size - step) % self.z_size)
+            return place(pieces, spots, 0, self.z_size)
+        spot = {"x": self.x, "y": self.y, "c": self.c}[axis]
+        return place([value, self.send(value, axis)], [spot, 1 - spot], "zxyc".index(axis), 2)
+
+    def gather(self, own, order):
+        rows, columns = own.shape
+        cut = own.reshape(1, 1, 2, 2, rows // 4, columns)
+        cut = lax.dynamic_slice_in_dim(cut, self.c, 1, 3)
+        if "y" in order:
+            cut = lax.dynamic_slice_in_dim(cut, self.y, 1, 2)
+        for axis in order:
+            cut = self.spread(cut, axis)
+        return cut.reshape(-1, columns)
+
+    def gather_small(self, own):
+        other = self.send(own, "x")
+        pair = jnp.stack(
+            [jnp.where(self.x == 0, own, other), jnp.where(self.x == 0, other, own)]
+        )
+        pieces = [pair]
+        for _ in range(1, self.z_size):
+            pieces.append(self.send(pieces[-1], "z"))
+        stacked = jnp.stack(pieces)
+        return jnp.concatenate(
+            [
+                lax.dynamic_index_in_dim(stacked, (self.z + self.z_size - at) % self.z_size, 0, False)
+                for at in range(self.z_size)
+            ]
+        )
+
+    def share_rows(self, left):
+        tokens, width = left.shape
+        rows = width // (2 * self.z_size)
+        halves = left.reshape(tokens, self.z_size, 2, rows).transpose(2, 0, 1, 3)
+        halves = halves.reshape(2, tokens, self.z_size * rows)
+        for axis in "yc":
+            halves = jnp.concatenate([halves, self.send(halves, axis)], axis=1)
+        return halves
+
+    def share_columns(self, right):
+        for axis, spot in (("y", self.y), ("c", self.c)):
+            tokens, columns = right.shape
+            halves = jnp.stack([right[:, : columns // 2], right[:, columns // 2 :]])
+            mine = lax.dynamic_index_in_dim(halves, spot, 0, False)
+            theirs = lax.dynamic_index_in_dim(halves, 1 - spot, 0, False)
+            right = jnp.concatenate([mine, self.send(theirs, axis)], axis=0)
+        return right
+
+    def reduce(self, halves, right):
+        theirs = lax.dynamic_index_in_dim(halves, 1 - self.x, 0, False)
+        mine = lax.dynamic_index_in_dim(halves, self.x, 0, False)
+        moved = self.send(matmul_left(theirs, right).astype(jnp.bfloat16), "x")
+        partial = (matmul_left(mine, right) + moved.astype(jnp.float32)).astype(jnp.bfloat16)
+        partial = partial.reshape(self.z_size, -1, partial.shape[1])
+
+        def block(step):
+            at = (self.z + 2 * self.z_size - 1 - step) % self.z_size
+            return lax.dynamic_index_in_dim(partial, at, 0, False)
+
+        total = block(0)
+        for step in range(1, self.z_size):
+            arrived = self.send(total, "z")
+            total = (arrived.astype(jnp.float32) + block(step).astype(jnp.float32)).astype(
+                jnp.bfloat16
+            )
+        by_y = self.send(total, "y")
+        by_c = self.send(total, "c")
+        by_yc = self.send(by_y, "c")
+        first_y, first_c = self.y == 0, self.c == 0
+        near = (jnp.where(first_c, total, by_c), jnp.where(first_c, by_c, total))
+        far = (jnp.where(first_c, by_y, by_yc), jnp.where(first_c, by_yc, by_y))
+        quarters = [jnp.where(first_y, a, b) for a, b in zip(near, far)] + [
+            jnp.where(first_y, b, a) for a, b in zip(near, far)
+        ]
+        return jnp.concatenate([part.astype(jnp.float32) for part in quarters], axis=1)
+
+
+def pack_small(in_gain, conv_w, conv_b, ssm_gain, ff_gain, raw):
+    def rows(value):
+        flat = value.reshape(-1)
+        return jnp.pad(flat, (0, -flat.shape[0] % 128)).reshape(-1, 128)
+
+    packed = jnp.concatenate([rows(v) for v in (raw.T, in_gain, conv_w, conv_b, ssm_gain, ff_gain)])
+    return jnp.pad(packed, ((0, -packed.shape[0] % 16), (0, 0)))
+
+
+def unpack_small(gathered, own):
+    in_gain, conv_w, conv_b, ssm_gain, ff_gain, raw = own
+    parts = gathered.shape[0]
+    at = 0
+    out = []
+    for value in (raw.T, in_gain, conv_w, conv_b, ssm_gain, ff_gain):
+        count = -(-value.size // 128)
+        flat = gathered[:, at : at + count].reshape(parts, -1)[:, : value.size]
+        at += count
+        shaped = flat.reshape((parts,) + value.shape)
+        if value.ndim == 1:
+            out.append(shaped.reshape(-1))
+        else:
+            out.append(shaped.transpose(1, 0, 2).reshape(value.shape[0], -1))
+    return tuple(out[1:]) + (out[0],)
 
 
 def shards(
+    copies,
     tokens,
     cotangent,
     seq_lengths,
@@ -393,133 +534,89 @@
     w_up,
     w_down,
 ):
-    gathered = (
-        lax.all_gather(in_gain, "shard", axis=0, tiled=True),
-        lax.all_gather(w_in, "shard", axis=0, tiled=True),
-        lax.all_gather(conv_w, "shard", axis=1, tiled=True),
-        lax.all_gather(conv_b, "shard", axis=0, tiled=True),
-        lax.all_gather(ssm_gain, "shard", axis=0, tiled=True),
-        lax.all_gather(w_out, "shard", axis=0, tiled=True),
-        lax.all_gather(w_query, "shard", axis=0, tiled=True),
-        lax.all_gather(w_key, "shard", axis=0, tiled=True),
-        lax.all_gather(w_value, "shard", axis=0, tiled=True),
-        lax.all_gather(w_attn_out, "shard", axis=0, tiled=True),
-        lax.all_gather(ff_gain, "shard", axis=0, tiled=True),
-        lax.all_gather(w_gate, "shard", axis=0, tiled=True),
-        lax.all_gather(w_up, "shard", axis=0, tiled=True),
-        lax.all_gather(w_down, "shard", axis=0, tiled=True),
-    )
+    parts = MH * HD // w_out.shape[0]
+    width = MH * HD
+    channels = width + 2 * NS
+    quick = parts == 8 and copies == 4
+    links = Links(parts, copies)
+    own_small = (in_gain, conv_w, conv_b, ssm_gain, ff_gain, w_in[:, width + channels :])
+    own = (
+        w_in[:, width : width + channels],
+        w_in[:, :width],
+        jnp.concatenate([w_query, w_key, w_value], axis=1),
+        jnp.concatenate([w_out, w_attn_out], axis=0),
+        w_gate,
+        w_up,
+        w_down,
+    )
+    if quick:
+        orders = ("zxyc", "zyxc", "xzc", "xzc", "zxyc", "zyxc", "zyxc")
+        small_all = links.gather_small(pack_small(*own_small))
+        mats = tuple(links.gather(value, order) for value, order in zip(own, orders))
+    else:
+        small_all = lax.all_gather(pack_small(*own_small), "shard", axis=0)
+        mats = tuple(lax.all_gather(value, "shard", axis=0, tiled=True) for value in own)
+    gains = unpack_small(small_all, own_small)
     segment, position = layout(seq_lengths[0], seq_starts[0], tokens.shape[0])
     result, kept = forward_pass(
-        tokens.astype(jnp.float32), gathered, a_log, dt_bias, skip_d, segment, position
-    )
-    matrices = (
-        gathered[1],
-        gathered[5],
-        gathered[6],
-        gathered[7],
-        gathered[8],
-        gathered[9],
-        gathered[11],
-        gathered[12],
-        gathered[13],
-    )
-    tokens_grad, factors, small, head_grads = backward_pass(cotangent, matrices, skip_d, kept)
-    (
-        normed,
-        model_right,
-        normed_two,
-        feed_right,
-        gated,
-        branch_grad,
-        head_rows_out,
-        hidden,
-        feed_grad,
-    ) = factors
-    grad_a_log, grad_dt_bias, grad_skip = head_grads
-    model_share = lax.psum_scatter(
-        model_rows(factors).astype(jnp.bfloat16), "shard", scatter_dimension=0, tiled=True
-    )
-    out_share = lax.psum_scatter(
-        matmul_left(gated, branch_grad).astype(jnp.bfloat16),
-        "shard",
-        scatter_dimension=0,
-        tiled=True,
-    )
-    attn_share = lax.psum_scatter(
-        matmul_left(head_rows_out, branch_grad).astype(jnp.bfloat16),
-        "shard",
-        scatter_dimension=0,
-        tiled=True,
-    )
-    down_share = lax.psum_scatter(
-        matmul_left(hidden, feed_grad).astype(jnp.bfloat16),
-        "shard",
-        scatter_dimension=0,
-        tiled=True,
-    )
-    small_part = (
-        lax.psum_scatter(
-            small[0].astype(jnp.bfloat16), "shard", scatter_dimension=0, tiled=True
-        ).astype(jnp.float32),
-        lax.psum_scatter(
-            small[1].astype(jnp.bfloat16), "shard", scatter_dimension=1, tiled=True
-        ).astype(jnp.float32),
-        lax.psum_scatter(
-            small[2].astype(jnp.bfloat16), "shard", scatter_dimension=0, tiled=True
-        ).astype(jnp.float32),
-        lax.psum_scatter(
-            small[3].astype(jnp.bfloat16), "shard", scatter_dimension=0, tiled=True
-        ).astype(jnp.float32),
-        lax.psum_scatter(
-            small[4].astype(jnp.bfloat16), "shard", scatter_dimension=0, tiled=True
-        ).astype(jnp.float32),
-    )
-    summed = (
-        lax.psum(model_share, "replica").astype(jnp.float32),
-        lax.psum(out_share, "replica").astype(jnp.float32),
-        lax.psum(attn_share, "replica").astype(jnp.float32),
-        lax.psum(down_share, "replica").astype(jnp.float32),
-        lax.psum(small_part[0].astype(jnp.bfloat16), "replica").astype(jnp.float32),
-        lax.psum(small_part[1].astype(jnp.bfloat16), "replica").astype(jnp.float32),
-        lax.psum(small_part[2].astype(jnp.bfloat16), "replica").astype(jnp.float32),
-        lax.psum(small_part[3].astype(jnp.bfloat16), "replica").astype(jnp.float32),
-        lax.psum(small_part[4].astype(jnp.bfloat16), "replica").astype(jnp.float32),
-    )
-    model_parts = split_model(summed[0])
-    mats = (
-        model_parts[0],
-        summed[1],
-        model_parts[1],
-        model_parts[2],
-        model_parts[3],
-        summed[2],
-        model_parts[4],
-        model_parts[5],
-        summed[3],
-    )
-    small_owned = (summed[4], summed[5], summed[6], summed[7], summed[8])
-    head_total = lax.psum((grad_a_log, grad_dt_bias, grad_skip), ("shard", "replica"))
+        tokens.astype(jnp.float32), gains, mats, a_log, dt_bias, skip_d, segment, position, parts
+    )
+    tokens_grad, pairs, small = backward_pass(cotangent, gains[5], mats, skip_d, kept, parts)
+    if quick:
+        shared = {}
+        summed = []
+        for left, right in pairs:
+            if id(left) not in shared:
+                shared[id(left)] = links.share_rows(left)
+            summed.append(links.reduce(shared[id(left)], links.share_columns(right)))
+    else:
+        summed = []
+        for left, right in pairs:
+            share = lax.psum_scatter(
+                matmul_left(left, right).astype(jnp.bfloat16),
+                "shard",
+                scatter_dimension=0,
+                tiled=True,
+            )
+            summed.append(lax.psum(share, "replica").astype(jnp.float32))
+    down, feed, joined, first, second = summed
+    flat = jnp.concatenate([value.reshape(-1) for value in small])
+    flat = jnp.pad(flat, (0, -flat.shape[0] % 1024)).reshape(-1, 128)
+    flat = lax.psum(flat, AXES).reshape(-1)
+    totals = []
+    at = 0
+    for value in small:
+        totals.append(flat[at : at + value.size].reshape(value.shape))
+        at += value.size
+    here = lax.axis_index("shard")
+
+    def mine(value):
+        size = value.shape[-1] // parts
+        return lax.dynamic_slice_in_dim(value, here * size, size, value.ndim - 1)
+
+    q_cols = QH * ATTENTION_HEAD
+    k_cols = KVH * ATTENTION_HEAD
+    out_rows = width // parts
     return (
         result,
         tokens_grad,
-        small_owned[0],
-        mats[0],
-        small_owned[1],
-        small_owned[2],
-        head_total[0],
-        head_total[1],
-        head_total[2],
-        small_owned[3],
-        mats[1],
-        mats[2],
-        mats[3],
-        mats[4],
-        mats[5],
-        small_owned[4],
-        mats[6],
-        mats[7],
-        mats[8],
+        mine(totals[0]),
+        jnp.concatenate([first[:, :width], second[:, :channels], mine(totals[5]).T], axis=1),
+        mine(totals[1]),
+        mine(totals[2]),
+        totals[6],
+        totals[7],
+        totals[8],
+        mine(totals[3]),
+        joined[:out_rows],
+        first[:, width : width + q_cols],
+        second[:, channels : channels + k_cols],
+        second[:, channels + k_cols :],
+        joined[out_rows:],
+        mine(totals[4]),
+        feed[:, :FF],
+        feed[:, FF:],
+        down,
     )
 
 
@@ -568,4 +665,8 @@
         P("shard", None),
         P("shard", None),
     )
-    return jax.shard_map(shards, mesh=mesh, in_specs=in_specs, out_specs=out_specs, check_vma=False)
+
+    def local(*args):
+        return shards(mesh.shape["replica"], *args)
+
+    return jax.shard_map(local, mesh=mesh, in_specs=in_specs, out_specs=out_specs, check_vma=False)

time: 1300 us -> 1960 us (1.51)
  Pallas kernels: 0 us -> 1430 us
  waiting for transfers between devices: 832 us -> 257 us
  blocking collectives: 232 us -> 0 us
  starting transfers between devices: 0.51 us -> 57.9 us
  other arithmetic: 85.3 us -> 56.1 us
    pallas_call x0 -> x26, Pallas kernels: none -> 1430 us  [place(): pl.pallas_call(body, out_shape=jax.ShapeDtypeStruct(tuple(shape), pieces[...]
    all_gather x7 -> x0, waiting for transfers between devices: 287 us -> none  [the longest x1 71.8 us: shards(): lax.all_gather(w_gate, 'shard', axis=0, tiled=True)]
    unnamed x15 -> x1, waiting for transfers between devices: 253 us -> 0.02 us
    reduce_scatter x3 -> x0, waiting for transfers between devices: 230 us -> none  [the longest x1 90.7 us: shards(): lax.psum_scatter(matmul_left(hidden, feed_grad).astype(jnp.bfloat16), 'sh...]
    ppermute x0 -> x97, waiting for transfers between devices: none -> 151 us  [send(): return lax.ppermute(value, AXES, self.tables[axis])]
    all_gather x5 -> x0, blocking collectives: 131 us -> none  [the longest x1 31.5 us: shards(): lax.all_gather(w_key, 'shard', axis=0, tiled=True)]
    ppermute x0 -> x97, starting transfers between devices: none -> 57.8 us  [send(): return lax.ppermute(value, AXES, self.tables[axis])]
    unnamed x2 -> x0, blocking collectives: 54.3 us -> none
  transfers between devices with their start and end apart: 13 -> 98, of which waited for: 11 -> 31; matrix products, arithmetic and copies ran while one was open for 5% -> 9% of each run, Pallas kernels for 0% -> 73%
where the time goes in v1:
time: 1960 us; the launch traced here: 1950 us
  Pallas kernels  1430 us (73%)
  waiting for transfers between devices  257 us (13%)
  matrix products  66.5 us (3%)
  local copies, waits for them, and re-layouts  66.3 us (3%)
  starting transfers between devices  57.9 us (3%)
  other arithmetic  56.1 us (3%)
    pallas_call x26, Pallas kernels, place(): pl.pallas_call(body, out_shape=jax.ShapeDtypeStruct(tuple(shape), pieces[...  1430 us
    ppermute x97, waiting for transfers between devices, send(): return lax.ppermute(value, AXES, self.tables[axis])  151 us
    psum x1, waiting for transfers between devices, shards(): flat = lax.psum(flat, AXES).reshape(-1)  106 us
    ppermute x97, starting transfers between devices, send(): return lax.ppermute(value, AXES, self.tables[axis])  57.8 us
  transfers between devices with their start and end apart: 98, of which 31 were waited for; matrix products, arithmetic and copies ran while one was open for 9% of the time, Pallas kernels for 73%

profile of v1, /device:TPU:0, one launch (start us, length us, event | category | flops | bytes accessed | tf_op | source)
XLA Modules:
  0.0 1953.8 jit_solution(2717996296151621048)
XLA Ops:
  54.1 8.2 collective-permute-done.11.refs_2_
  64.8 15.7 place.26.refs_0_
  94.0 13.7 place.30.refs_0_
  117.9 17.7 place.37.refs_0_
  135.6 29.6 %place.27.refs_0_ = bf16[4,2,1,1,32,1792]{5,4,3,2,1,0:T(8,128)(2,1)} custom-call(s32[2]{0:T(128)} %pad_add_fusion.3.where, bf16[4,1,1,1,32,1792]{5,4,3,2,1,0:T(8,128)(2,1)} %place.26.refs_0_, bf16[4,1,1,1,32,1792]{5,4,3,2,1,0:T(8,128)(2,1)} %copy-done.52), custom_call_target="tpu_custom_call" | custom-call | bytes 1835008 | tf_op jit(solution)/shard_map/place/pallas_call | solution.py:370
  174.1 17.7 place.48.refs_0_
  191.8 25.6 %place.31.refs_0_ = bf16[4,1,2,1,32,1536]{5,4,3,2,1,0:T(8,128)(2,1)} custom-call(s32[2]{0:T(128)} %pad_add_fusion.2.where, bf16[4,1,1,1,32,1536]{5,4,3,2,1,0:T(8,128)(2,1)} %place.30.refs_0_, bf16[4,1,1,1,32,1536]{5,4,3,2,1,0:T(8,128)(2,1)} %copy-done.57), custom_call_target="tpu_custom_call" | custom-call | bytes 1572864 | tf_op jit(solution)/shard_map/place/pallas_call | solution.py:370
  223.0 17.7 place.44.refs_0_
  241.9 25.6 %place.35.refs_0_ = bf16[4,2,2,1,32,768]{5,4,3,2,1,0:T(8,128)(2,1)} custom-call(s32[4]{0:T(128)} %pad_add_fusion.4.where, bf16[1,2,2,1,32,768]{5,4,3,2,1,0:T(8,128)(2,1)} %place.34.refs_0_, bf16[1,2,2,1,32,768]{5,4,3,2,1,0:T(8,128)(2,1)} %copy-done.67, bf16[1,2,2,1,32,768]{5,4,3,2,1,0:T(8,128)(2,1)} %collective-permute-done.18.refs_2_, ...), custom_call_target="tpu_custom_call" | custom-call | bytes 1572864 | tf_op jit(solution)/shard_map/place/pallas_call | solution.py:370
  268.5 57.4 %place.28.refs_0_ = bf16[4,2,2,1,32,1792]{5,4,3,2,1,0:T(8,128)(2,1)} custom-call(s32[2]{0:T(128)} %pad_add_fusion.2.where, bf16[4,2,1,1,32,1792]{5,4,3,2,1,0:T(8,128)(2,1)} %place.27.refs_0_, bf16[4,2,1,1,32,1792]{5,4,3,2,1,0:T(8,128)(2,1)} %copy-done.39), custom_call_target="tpu_custom_call" | custom-call | bytes 3670016 | tf_op jit(solution)/shard_map/place/pallas_call | solution.py:370
  332.5 17.8 place.40.refs_0_
  352.6 49.4 %place.32.refs_0_ = bf16[4,2,2,1,32,1536]{5,4,3,2,1,0:T(8,128)(2,1)} custom-call(s32[2]{0:T(128)} %pad_add_fusion.3.where, bf16[4,1,2,1,32,1536]{5,4,3,2,1,0:T(8,128)(2,1)} %place.31.refs_0_, bf16[4,1,2,1,32,1536]{5,4,3,2,1,0:T(8,128)(2,1)} %copy-done.43), custom_call_target="tpu_custom_call" | custom-call | bytes 3145728 | tf_op jit(solution)/shard_map/place/pallas_call | solution.py:370
  405.1 33.5 %place.49.refs_0_ = bf16[4,1,2,1,64,1024]{5,4,3,2,1,0:T(8,128)(2,1)} custom-call(s32[2]{0:T(128)} %pad_add_fusion.2.where, bf16[4,1,1,1,64,1024]{5,4,3,2,1,0:T(8,128)(2,1)} %place.48.refs_0_, bf16[4,1,1,1,64,1024]{5,4,3,2,1,0:T(8,128)(2,1)} %collective-permute-done.41.refs_1_), custom_call_target="tpu_custom_call" | custom-call | bytes 2097152 | tf_op jit(solution)/shard_map/place/pallas_call | solution.py:370
  438.6 33.7 %place.45.refs_0_ = bf16[4,1,2,1,32,2048]{5,4,3,2,1,0:T(8,128)(2,1)} custom-call(s32[2]{0:T(128)} %pad_add_fusion.2.where, bf16[4,1,1,1,32,2048]{5,4,3,2,1,0:T(8,128)(2,1)} %place.44.refs_0_, bf16[4,1,1,1,32,2048]{5,4,3,2,1,0:T(8,128)(2,1)} %collective-permute-done.35.refs_1_), custom_call_target="tpu_custom_call" | custom-call | bytes 2097152 | tf_op jit(solution)/shard_map/place/pallas_call | solution.py:370
  473.9 33.5 %place.41.refs_0_ = bf16[4,2,1,1,32,2048]{5,4,3,2,1,0:T(8,128)(2,1)} custom-call(s32[2]{0:T(128)} %pad_add_fusion.3.where, bf16[4,1,1,1,32,2048]{5,4,3,2,1,0:T(8,128)(2,1)} %place.40.refs_0_, bf16[4,1,1,1,32,2048]{5,4,3,2,1,0:T(8,128)(2,1)} %collective-permute-done.29.refs_1_), custom_call_target="tpu_custom_call" | custom-call | bytes 2097152 | tf_op jit(solution)/shard_map/place/pallas_call | solution.py:370
  508.3 49.4 %place.36 = bf16[4,2,2,2,32,768]{5,4,3,2,1,0:T(8,128)(2,1)} custom-call(s32[2]{0:T(128)} %pad_add_fusion.1.where, bf16[4,2,2,1,32,768]{5,4,3,2,1,0:T(8,128)(2,1)} %place.35.refs_0_, bf16[4,2,2,1,32,768]{5,4,3,2,1,0:T(8,128)(2,1)} %copy-done.42), custom_call_target="tpu_custom_call" | custom-call | bytes 3145728 | tf_op jit(solution)/shard_map/place/pallas_call | solution.py:370
  563.4 65.3 %place.38.refs_0_ = bf16[4,2,2,1,64,1024]{5,4,3,2,1,0:T(8,128)(2,1)} custom-call(s32[4]{0:T(128)} %pad_add_fusion.4.where, bf16[1,2,2,1,64,1024]{5,4,3,2,1,0:T(8,128)(2,1)} %place.37.refs_0_, bf16[1,2,2,1,64,1024]{5,4,3,2,1,0:T(8,128)(2,1)} %collective-permute-done.22.refs_1_, bf16[1,2,2,1,64,1024]{5,4,3,2,1,0:T(8,128)(2,1)} %collective-permute-done.23.refs_2_, ...), custom_call_target="tpu_custom_call" | custom-call | bytes 4194304 | tf_op jit(solution)/shard_map/place/pallas_call | solution.py:370
  629.7 65.3 %place.50.refs_0_ = bf16[4,2,2,1,64,1024]{5,4,3,2,1,0:T(8,128)(2,1)} custom-call(s32[2]{0:T(128)} %pad_add_fusion.3.where, bf16[4,1,2,1,64,1024]{5,4,3,2,1,0:T(8,128)(2,1)} %place.49.refs_0_, bf16[4,1,2,1,64,1024]{5,4,3,2,1,0:T(8,128)(2,1)} %copy-done.31), custom_call_target="tpu_custom_call" | custom-call | bytes 4194304 | tf_op jit(solution)/shard_map/place/pallas_call | solution.py:370
  695.1 65.4 %place.46.refs_0_ = bf16[4,2,2,1,32,2048]{5,4,3,2,1,0:T(8,128)(2,1)} custom-call(s32[2]{0:T(128)} %pad_add_fusion.3.where, bf16[4,1,2,1,32,2048]{5,4,3,2,1,0:T(8,128)(2,1)} %place.45.refs_0_, bf16[4,1,2,1,32,2048]{5,4,3,2,1,0:T(8,128)(2,1)} %collective-permute-done.36.refs_1_), custom_call_target="tpu_custom_call" | custom-call | bytes 4194304 | tf_op jit(solution)/shard_map/place/pallas_call | solution.py:370
  761.0 65.3 %place.42.refs_0_ = bf16[4,2,2,1,32,2048]{5,4,3,2,1,0:T(8,128)(2,1)} custom-call(s32[2]{0:T(128)} %pad_add_fusion.2.where, bf16[4,2,1,1,32,2048]{5,4,3,2,1,0:T(8,128)(2,1)} %place.41.refs_0_, bf16[4,2,1,1,32,2048]{5,4,3,2,1,0:T(8,128)(2,1)} %collective-permute-done.30.refs_1_), custom_call_target="tpu_custom_call" | custom-call | bytes 4194304 | tf_op jit(solution)/shard_map/place/pallas_call | solution.py:370
  826.6 97.1 %place.33 = bf16[4,2,2,2,32,1536]{5,4,3,2,1,0:T(8,128)(2,1)} custom-call(s32[2]{0:T(128)} %pad_add_fusion.1.where, bf16[4,2,2,1,32,1536]{5,4,3,2,1,0:T(8,128)(2,1)} %place.32.refs_0_, bf16[4,2,2,1,32,1536]{5,4,3,2,1,0:T(8,128)(2,1)} %collective-permute-done.15.refs_1_), custom_call_target="tpu_custom_call" | custom-call | bytes 6291456 | tf_op jit(solution)/shard_map/place/pallas_call | solution.py:370
  924.1 113.0 %place.29 = bf16[4,2,2,2,32,1792]{5,4,3,2,1,0:T(8,128)(2,1)} custom-call(s32[2]{0:T(128)} %pad_add_fusion.1.where, bf16[4,2,2,1,32,1792]{5,4,3,2,1,0:T(8,128)(2,1)} %place.28.refs_0_, bf16[4,2,2,1,32,1792]{5,4,3,2,1,0:T(8,128)(2,1)} %collective-permute-done.9.refs_1_), custom_call_target="tpu_custom_call" | custom-call | bytes 7340032 | tf_op jit(solution)/shard_map/place/pallas_call | solution.py:370
  1061.1 128.8 %place.39 = bf16[4,2,2,2,64,1024]{5,4,3,2,1,0:T(8,128)(2,1)} custom-call(s32[2]{0:T(128)} %pad_add_fusion.1.where, bf16[4,2,2,1,64,1024]{5,4,3,2,1,0:T(8,128)(2,1)} %place.38.refs_0_, bf16[4,2,2,1,64,1024]{5,4,3,2,1,0:T(8,128)(2,1)} %collective-permute-done.25.refs_1_), custom_call_target="tpu_custom_call" | custom-call | bytes 8388608 | tf_op jit(solution)/shard_map/place/pallas_call | solution.py:370
  1200.1 128.8 %place.51 = bf16[4,2,2,2,64,1024]{5,4,3,2,1,0:T(8,128)(2,1)} custom-call(s32[2]{0:T(128)} %pad_add_fusion.1.where, bf16[4,2,2,1,64,1024]{5,4,3,2,1,0:T(8,128)(2,1)} %place.50.refs_0_, bf16[4,2,2,1,64,1024]{5,4,3,2,1,0:T(8,128)(2,1)} %collective-permute-done.43.refs_1_), custom_call_target="tpu_custom_call" | custom-call | bytes 8388608 | tf_op jit(solution)/shard_map/place/pallas_call | solution.py:370
  1329.0 129.0 %place.47 = bf16[4,2,2,2,32,2048]{5,4,3,2,1,0:T(8,128)(2,1)} custom-call(s32[2]{0:T(128)} %pad_add_fusion.1.where, bf16[4,2,2,1,32,2048]{5,4,3,2,1,0:T(8,128)(2,1)} %place.46.refs_0_, bf16[4,2,2,1,32,2048]{5,4,3,2,1,0:T(8,128)(2,1)} %collective-permute-done.37.refs_1_), custom_call_target="tpu_custom_call" | custom-call | bytes 8388608 | tf_op jit(solution)/shard_map/place/pallas_call | solution.py:370
  1463.6 128.8 %place.43 = bf16[4,2,2,2,32,2048]{5,4,3,2,1,0:T(8,128)(2,1)} custom-call(s32[2]{0:T(128)} %pad_add_fusion.1.where, bf16[4,2,2,1,32,2048]{5,4,3,2,1,0:T(8,128)(2,1)} %place.42.refs_0_, bf16[4,2,2,1,32,2048]{5,4,3,2,1,0:T(8,128)(2,1)} %collective-permute-done.31.refs_1_), custom_call_target="tpu_custom_call" | custom-call | bytes 8388608 | tf_op jit(solution)/shard_map/place/pallas_call | solution.py:370
  1674.6 105.8 %all-reduce.22.cloned.1.call-done = f32[296,128]{1,0:T(8,128)} async-done(((f32[296,128]{1,0:T(8,128)}), f32[296,128]{1,0:T(8,128)}) %all-reduce.22.cloned.1.call-update) | async-done | bytes 151568 | tf_op jit(solution)/shard_map/psum | solution.py:585
  1795.3 8.1 collective-permute-done.77
  1805.6 9.1 collective-permute-done.86
  1819.5 9.9 collective-permute-done.48
  1829.9 9.9 collective-permute-done.57
  1906.1 8.3 collective-permute-done.91
  (779 shorter events, 352.0 us)
Async XLA Ops:
  7.2 1773.2 %all-reduce.22.cloned.1.call-start = ((), (), s32[]{:S(2)}) async-start(), calls=%async_computation | async-start | bytes 303104 | tf_op jit(solution)/shard_map/psum | solution.py:585
  107.8 57.4 %collective-permute-start.44 = (bf16[2,128,512]{1,2,0:T(8,128)(2,1)S(1)}, bf16[2,128,512]{1,2,0:T(8,128)(2,1)S(1)}, u32[]{:S(2)}, u32[]{:S(2)}) collective-permute-start(bf16[2,128,512]{1,2,0:T(8,128)(2,1)S(1)} %bitcast.449), channel_id=1, source_target_pairs={{0,2},{1,3},{2,0},{3,1},{4,6},{5,7},{6,4},{7,5},{8,10},{9,11},{10,... | collective-permute-start | bytes 786440 | tf_op jit(solution)/shard_map/ppermute | solution.py:402
  109.5 57.0 %collective-permute-start.40 = (bf16[1,1,1,1,64,1024]{5,4,3,2,1,0:T(8,128)(2,1)S(1)}, bf16[1,1,1,1,64,1024]{5,4,3,2,1,0:T(8,128)(2,1)}, u32[]{:S(2)}, u32[]{:S(2)}) collective-permute-start(bf16[1,1,1,1,64,1024]{5,4,3,2,1,0:T(8,128)(2,1)S(1)} %collective-permute-done.39.refs_2_), channel_id=1, source_target_pairs={{0,8},{1,9},{2,10},{3,11},{4,12},{5,13},{6,14},{7,15},{8,16},{9,17... | collective-permute-start | bytes 393224 | tf_op jit(solution)/shard_map/ppermute | solution.py:402
  109.6 61.3 %collective-permute-start.13 = (bf16[4,1,1,1,32,1536]{5,4,3,2,1,0:T(8,128)(2,1)}, bf16[4,1,1,1,32,1536]{5,4,3,2,1,0:T(8,128)(2,1)S(1)}, u32[]{:S(2)}, u32[]{:S(2)}) collective-permute-start(bf16[4,1,1,1,32,1536]{5,4,3,2,1,0:T(8,128)(2,1)} %place.30.refs_0_), channel_id=1, source_target_pairs={{0,2},{1,3},{2,0},{3,1},{4,6},{5,7},{6,4},{7,5},{8,10},{9,11},{10,... | collective-permute-start | bytes 1179656 | tf_op jit(solution)/shard_map/ppermute | solution.py:402
  117.2 53.6 %collective-permute-start.18 = (bf16[1,2,2,1,32,768]{5,4,3,2,1,0:T(8,128)(2,1)S(1)}, bf16[1,2,2,1,32,768]{5,4,3,2,1,0:T(8,128)(2,1)}, u32[]{:S(2)}, u32[]{:S(2)}) collective-permute-start(bf16[1,2,2,1,32,768]{5,4,3,2,1,0:T(8,128)(2,1)S(1)} %collective-permute-done.17.refs_1_), channel_id=1, source_target_pairs={{0,8},{1,9},{2,10},{3,11},{4,12},{5,13},{6,14},{7,15},{8,16},{9,17... | collective-permute-start | bytes 589832 | tf_op jit(solution)/shard_map/ppermute | solution.py:402
  165.2 57.1 %collective-permute-start.22 = (bf16[1,2,2,1,64,1024]{5,4,3,2,1,0:T(8,128)(2,1)}, bf16[1,2,2,1,64,1024]{5,4,3,2,1,0:T(8,128)(2,1)}, u32[]{:S(2)}, u32[]{:S(2)}) collective-permute-start(bf16[1,2,2,1,64,1024]{5,4,3,2,1,0:T(8,128)(2,1)} %place.37.refs_0_), channel_id=1, source_target_pairs={{0,8},{1,9},{2,10},{3,11},{4,12},{5,13},{6,14},{7,15},{8,16},{9,17... | collective-permute-start | bytes 1572872 | tf_op jit(solution)/shard_map/ppermute | solution.py:402
  166.4 101.2 %collective-permute-start.8 = (bf16[4,2,1,1,32,1792]{5,4,3,2,1,0:T(8,128)(2,1)}, bf16[4,2,1,1,32,1792]{5,4,3,2,1,0:T(8,128)(2,1)S(1)}, u32[]{:S(2)}, u32[]{:S(2)}) collective-permute-start(bf16[4,2,1,1,32,1792]{5,4,3,2,1,0:T(8,128)(2,1)} %place.27.refs_0_), channel_id=1, source_target_pairs={{0,2},{1,3},{2,0},{3,1},{4,6},{5,7},{6,4},{7,5},{8,10},{9,11},{10,... | collective-permute-start | bytes 2752520 | tf_op jit(solution)/shard_map/ppermute | solution.py:402
  167.1 50.4 %collective-permute-start.28 = (bf16[1,1,1,1,32,2048]{5,4,3,2,1,0:T(8,128)(2,1)}, bf16[1,1,1,1,32,2048]{5,4,3,2,1,0:T(8,128)(2,1)S(1)}, u32[]{:S(2)}, u32[]{:S(2)}) collective-permute-start(bf16[1,1,1,1,32,2048]{5,4,3,2,1,0:T(8,128)(2,1)} %copy-done.79), channel_id=1, source_target_pairs={{0,8},{1,9},{2,10},{3,11},{4,12},{5,13},{6,14},{7,15},{8,16},{9,17... | collective-permute-start | bytes 393224 | tf_op jit(solution)/shard_map/ppermute | solution.py:402
  170.8 69.9 %collective-permute-start.45 = (bf16[2,256,512]{1,2,0:T(8,128)(2,1)S(1)}, bf16[2,256,512]{1,2,0:T(8,128)(2,1)}, u32[]{:S(2)}, u32[]{:S(2)}) collective-permute-start(bf16[2,256,512]{1,2,0:T(8,128)(2,1)S(1)} %pad_maximum_fusion.16), channel_id=1, source_target_pairs={{0,1},{1,0},{2,3},{3,2},{4,5},{5,4},{6,7},{7,6},{8,9},{9,8},{10,11... | collective-permute-start | bytes 1572872 | tf_op jit(solution)/shard_map/ppermute | solution.py:402
  217.5 108.4 %collective-permute-start.41 = (bf16[4,1,1,1,64,1024]{5,4,3,2,1,0:T(8,128)(2,1)}, bf16[4,1,1,1,64,1024]{5,4,3,2,1,0:T(8,128)(2,1)}, u32[]{:S(2)}, u32[]{:S(2)}) collective-permute-start(bf16[4,1,1,1,64,1024]{5,4,3,2,1,0:T(8,128)(2,1)} %place.48.refs_0_), channel_id=1, source_target_pairs={{0,2},{1,3},{2,0},{3,1},{4,6},{5,7},{6,4},{7,5},{8,10},{9,11},{10,... | collective-permute-start | bytes 1572872 | tf_op jit(solution)/shard_map/ppermute | solution.py:402
  219.1 131.5 %collective-permute-start.14 = (bf16[4,1,2,1,32,1536]{5,4,3,2,1,0:T(8,128)(2,1)}, bf16[4,1,2,1,32,1536]{5,4,3,2,1,0:T(8,128)(2,1)S(1)}, u32[]{:S(2)}, u32[]{:S(2)}) collective-permute-start(bf16[4,1,2,1,32,1536]{5,4,3,2,1,0:T(8,128)(2,1)} %place.31.refs_0_), channel_id=1, source_target_pairs={{0,4},{1,5},{2,6},{3,7},{4,0},{5,1},{6,2},{7,3},{8,12},{9,13},{10,... | collective-permute-start | bytes 2359304 | tf_op jit(solution)/shard_map/ppermute | solution.py:402
  222.3 127.9 %collective-permute-start.23 = (bf16[1,2,2,1,64,1024]{5,4,3,2,1,0:T(8,128)(2,1)}, bf16[1,2,2,1,64,1024]{5,4,3,2,1,0:T(8,128)(2,1)}, u32[]{:S(2)}, u32[]{:S(2)}) collective-permute-start(bf16[1,2,2,1,64,1024]{5,4,3,2,1,0:T(8,128)(2,1)} %collective-permute-done.22.refs_1_), channel_id=1, source_target_pairs={{0,8},{1,9},{2,10},{3,11},{4,12},{5,13},{6,14},{7,15},{8,16},{9,17... | collective-permute-start | bytes 1572872 | tf_op jit(solution)/shard_map/ppermute | solution.py:402
  240.7 161.3 %collective-permute-start.35 = (bf16[4,1,1,1,32,2048]{5,4,3,2,1,0:T(8,128)(2,1)}, bf16[4,1,1,1,32,2048]{5,4,3,2,1,0:T(8,128)(2,1)}, u32[]{:S(2)}, u32[]{:S(2)}) collective-permute-start(bf16[4,1,1,1,32,2048]{5,4,3,2,1,0:T(8,128)(2,1)} %place.44.refs_0_), channel_id=1, source_target_pairs={{0,2},{1,3},{2,0},{3,1},{4,6},{5,7},{6,4},{7,5},{8,10},{9,11},{10,... | collective-permute-start | bytes 1572872 | tf_op jit(solution)/shard_map/ppermute | solution.py:402
  267.6 239.8 %collective-permute-start.20 = (bf16[4,2,2,1,32,768]{5,4,3,2,1,0:T(8,128)(2,1)}, bf16[4,2,2,1,32,768]{5,4,3,2,1,0:T(8,128)(2,1)S(1)}, u32[]{:S(2)}, u32[]{:S(2)}) collective-permute-start(bf16[4,2,2,1,32,768]{5,4,3,2,1,0:T(8,128)(2,1)} %place.35.refs_0_), channel_id=1, source_target_pairs={{0,1},{1,0},{2,3},{3,2},{4,5},{5,4},{6,7},{7,6},{8,9},{9,8},{10,11... | collective-permute-start | bytes 2359304 | tf_op jit(solution)/shard_map/ppermute | solution.py:402
  325.9 597.8 %collective-permute-start.9 = (bf16[4,2,2,1,32,1792]{5,4,3,2,1,0:T(8,128)(2,1)}, bf16[4,2,2,1,32,1792]{5,4,3,2,1,0:T(8,128)(2,1)}, u32[]{:S(2)}, u32[]{:S(2)}) collective-permute-start(bf16[4,2,2,1,32,1792]{5,4,3,2,1,0:T(8,128)(2,1)} %place.28.refs_0_), channel_id=1, source_target_pairs={{0,1},{1,0},{2,3},{3,2},{4,5},{5,4},{6,7},{7,6},{8,9},{9,8},{10,11... | collective-permute-start | bytes 5505032 | tf_op jit(solution)/shard_map/ppermute | solution.py:402
  350.3 122.0 %collective-permute-start.29 = (bf16[4,1,1,1,32,2048]{5,4,3,2,1,0:T(8,128)(2,1)}, bf16[4,1,1,1,32,2048]{5,4,3,2,1,0:T(8,128)(2,1)}, u32[]{:S(2)}, u32[]{:S(2)}) collective-permute-start(bf16[4,1,1,1,32,2048]{5,4,3,2,1,0:T(8,128)(2,1)} %place.40.refs_0_), channel_id=1, source_target_pairs={{0,4},{1,5},{2,6},{3,7},{4,0},{5,1},{6,2},{7,3},{8,12},{9,13},{10,... | collective-permute-start | bytes 1572872 | tf_op jit(solution)/shard_map/ppermute | solution.py:402
  350.6 207.2 %collective-permute-start.24 = (bf16[1,2,2,1,64,1024]{5,4,3,2,1,0:T(8,128)(2,1)}, bf16[1,2,2,1,64,1024]{5,4,3,2,1,0:T(8,128)(2,1)}, u32[]{:S(2)}, u32[]{:S(2)}) collective-permute-start(bf16[1,2,2,1,64,1024]{5,4,3,2,1,0:T(8,128)(2,1)} %collective-permute-done.23.refs_2_), channel_id=1, source_target_pairs={{0,8},{1,9},{2,10},{3,11},{4,12},{5,13},{6,14},{7,15},{8,16},{9,17... | collective-permute-start | bytes 1572872 | tf_op jit(solution)/shard_map/ppermute | solution.py:402
  402.0 424.4 %collective-permute-start.15 = (bf16[4,2,2,1,32,1536]{5,4,3,2,1,0:T(8,128)(2,1)}, bf16[4,2,2,1,32,1536]{5,4,3,2,1,0:T(8,128)(2,1)}, u32[]{:S(2)}, u32[]{:S(2)}) collective-permute-start(bf16[4,2,2,1,32,1536]{5,4,3,2,1,0:T(8,128)(2,1)} %place.32.refs_0_), channel_id=1, source_target_pairs={{0,1},{1,0},{2,3},{3,2},{4,5},{5,4},{6,7},{7,6},{8,9},{9,8},{10,11... | collective-permute-start | bytes 4718600 | tf_op jit(solution)/shard_map/ppermute | solution.py:402
  472.3 156.4 %collective-permute-start.42 = (bf16[4,1,2,1,64,1024]{5,4,3,2,1,0:T(8,128)(2,1)S(1)}, bf16[4,1,2,1,64,1024]{5,4,3,2,1,0:T(8,128)(2,1)S(1)}, u32[]{:S(2)}, u32[]{:S(2)}) collective-permute-start(bf16[4,1,2,1,64,1024]{5,4,3,2,1,0:T(8,128)(2,1)S(1)} %copy-done.16), channel_id=1, source_target_pairs={{0,4},{1,5},{2,6},{3,7},{4,0},{5,1},{6,2},{7,3},{8,12},{9,13},{10,... | collective-permute-start | bytes 3145736 | tf_op jit(solution)/shard_map/ppermute | solution.py:402
  507.5 187.6 %collective-permute-start.36 = (bf16[4,1,2,1,32,2048]{5,4,3,2,1,0:T(8,128)(2,1)}, bf16[4,1,2,1,32,2048]{5,4,3,2,1,0:T(8,128)(2,1)}, u32[]{:S(2)}, u32[]{:S(2)}) collective-permute-start(bf16[4,1,2,1,32,2048]{5,4,3,2,1,0:T(8,128)(2,1)} %place.45.refs_0_), channel_id=1, source_target_pairs={{0,4},{1,5},{2,6},{3,7},{4,0},{5,1},{6,2},{7,3},{8,12},{9,13},{10,... | collective-permute-start | bytes 3145736 | tf_op jit(solution)/shard_map/ppermute | solution.py:402
  557.8 202.8 %collective-permute-start.30 = (bf16[4,2,1,1,32,2048]{5,4,3,2,1,0:T(8,128)(2,1)}, bf16[4,2,1,1,32,2048]{5,4,3,2,1,0:T(8,128)(2,1)}, u32[]{:S(2)}, u32[]{:S(2)}) collective-permute-start(bf16[4,2,1,1,32,2048]{5,4,3,2,1,0:T(8,128)(2,1)} %place.41.refs_0_), channel_id=1, source_target_pairs={{0,2},{1,3},{2,0},{3,1},{4,6},{5,7},{6,4},{7,5},{8,10},{9,11},{10,... | collective-permute-start | bytes 3145736 | tf_op jit(solution)/shard_map/ppermute | solution.py:402
  628.8 1251.3 %collective-permute-start.89 = (bf16[256,256]{1,0:T(8,128)(2,1)}, bf16[256,256]{1,0:T(8,128)(2,1)}, u32[]{:S(2)}, u32[]{:S(2)}) collective-permute-start(bf16[256,256]{1,0:T(8,128)(2,1)} %get-tuple-element.194), channel_id=1, source_target_pairs={{0,1},{1,0},{2,3},{3,2},{4,5},{5,4},{6,7},{7,6},{8,9},{9,8},{10,11... | collective-permute-start | bytes 393224 | tf_op jit(solution)/shard_map/ppermute | solution.py:402
  695.1 365.5 %collective-permute-start.25 = (bf16[4,2,2,1,64,1024]{5,4,3,2,1,0:T(8,128)(2,1)}, bf16[4,2,2,1,64,1024]{5,4,3,2,1,0:T(8,128)(2,1)}, u32[]{:S(2)}, u32[]{:S(2)}) collective-permute-start(bf16[4,2,2,1,64,1024]{5,4,3,2,1,0:T(8,128)(2,1)} %place.38.refs_0_), channel_id=1, source_target_pairs={{0,1},{1,0},{2,3},{3,2},{4,5},{5,4},{6,7},{7,6},{8,9},{9,8},{10,11... | collective-permute-start | bytes 6291464 | tf_op jit(solution)/shard_map/ppermute | solution.py:402
  760.6 438.1 %collective-permute-start.43 = (bf16[4,2,2,1,64,1024]{5,4,3,2,1,0:T(8,128)(2,1)S(1)}, bf16[4,2,2,1,64,1024]{5,4,3,2,1,0:T(8,128)(2,1)}, u32[]{:S(2)}, u32[]{:S(2)}) collective-permute-start(bf16[4,2,2,1,64,1024]{5,4,3,2,1,0:T(8,128)(2,1)S(1)} %copy-done.9), channel_id=1, source_target_pairs={{0,1},{1,0},{2,3},{3,2},{4,5},{5,4},{6,7},{7,6},{8,9},{9,8},{10,11... | collective-permute-start | bytes 6291464 | tf_op jit(solution)/shard_map/ppermute | solution.py:402
  826.4 502.6 %collective-permute-start.37 = (bf16[4,2,2,1,32,2048]{5,4,3,2,1,0:T(8,128)(2,1)}, bf16[4,2,2,1,32,2048]{5,4,3,2,1,0:T(8,128)(2,1)}, u32[]{:S(2)}, u32[]{:S(2)}) collective-permute-start(bf16[4,2,2,1,32,2048]{5,4,3,2,1,0:T(8,128)(2,1)} %place.46.refs_0_), channel_id=1, source_target_pairs={{0,1},{1,0},{2,3},{3,2},{4,5},{5,4},{6,7},{7,6},{8,9},{9,8},{10,11... | collective-permute-start | bytes 6291464 | tf_op jit(solution)/shard_map/ppermute | solution.py:402
  923.7 539.9 %collective-permute-start.31 = (bf16[4,2,2,1,32,2048]{5,4,3,2,1,0:T(8,128)(2,1)}, bf16[4,2,2,1,32,2048]{5,4,3,2,1,0:T(8,128)(2,1)}, u32[]{:S(2)}, u32[]{:S(2)}) collective-permute-start(bf16[4,2,2,1,32,2048]{5,4,3,2,1,0:T(8,128)(2,1)} %place.42.refs_0_), channel_id=1, source_target_pairs={{0,1},{1,0},{2,3},{3,2},{4,5},{5,4},{6,7},{7,6},{8,9},{9,8},{10,11... | collective-permute-start | bytes 6291464 | tf_op jit(solution)/shard_map/ppermute | solution.py:402
  1060.5 611.1 %collective-permute-start.64 = (bf16[2,128,1024]{1,2,0:T(8,128)(2,1)}, bf16[2,128,1024]{1,2,0:T(8,128)(2,1)}, u32[]{:S(2)}, u32[]{:S(2)}) collective-permute-start(bf16[2,128,1024]{1,2,0:T(8,128)(2,1)} %bitcast.128), channel_id=1, source_target_pairs={{0,2},{1,3},{2,0},{3,1},{4,6},{5,7},{6,4},{7,5},{8,10},{9,11},{10,... | collective-permute-start | bytes 1572872 | tf_op jit(solution)/shard_map/ppermute | solution.py:402
  1198.7 591.6 %collective-permute-start.75 = (bf16[2,128,512]{1,2,0:T(8,128)(2,1)}, bf16[2,128,512]{1,2,0:T(8,128)(2,1)}, u32[]{:S(2)}, u32[]{:S(2)}) collective-permute-start(bf16[2,128,512]{1,2,0:T(8,128)(2,1)} %bitcast.446), channel_id=1, source_target_pairs={{0,2},{1,3},{2,0},{3,1},{4,6},{5,7},{6,4},{7,5},{8,10},{9,11},{10,... | collective-permute-start | bytes 786440 | tf_op jit(solution)/shard_map/ppermute | solution.py:402
  1659.8 132.3 %collective-permute-start.46 = (bf16[128,1024]{1,0:T(8,128)(2,1)}, bf16[128,1024]{1,0:T(8,128)(2,1)}, u32[]{:S(2)}, u32[]{:S(2)}) collective-permute-start(bf16[128,1024]{1,0:T(8,128)(2,1)} %get-tuple-element.183), channel_id=1, source_target_pairs={{0,2},{1,3},{2,0},{3,1},{4,6},{5,7},{6,4},{7,5},{8,10},{9,11},{10,... | collective-permute-start | bytes 786440 | tf_op jit(solution)/shard_map/ppermute | solution.py:402
  1665.3 128.7 %collective-permute-start.55 = (bf16[128,1024]{1,0:T(8,128)(2,1)}, bf16[128,1024]{1,0:T(8,128)(2,1)}, u32[]{:S(2)}, u32[]{:S(2)}) collective-permute-start(bf16[128,1024]{1,0:T(8,128)(2,1)} %get-tuple-element.177), channel_id=1, source_target_pairs={{0,2},{1,3},{2,0},{3,1},{4,6},{5,7},{6,4},{7,5},{8,10},{9,11},{10,... | collective-permute-start | bytes 786440 | tf_op jit(solution)/shard_map/ppermute | solution.py:402
  1671.6 117.1 %collective-permute-start.66 = (bf16[128,512]{1,0:T(8,128)(2,1)S(1)}, bf16[128,512]{1,0:T(8,128)(2,1)S(1)}, u32[]{:S(2)}, u32[]{:S(2)}) collective-permute-start(bf16[128,512]{1,0:T(8,128)(2,1)S(1)} %get-tuple-element.207), channel_id=1, source_target_pairs={{0,2},{1,3},{2,0},{3,1},{4,6},{5,7},{6,4},{7,5},{8,10},{9,11},{10,... | collective-permute-start | bytes 393224 | tf_op jit(solution)/shard_map/ppermute | solution.py:402
  1839.8 58.0 %collective-permute-start.79 = (bf16[512,1024]{1,0:T(8,128)(2,1)S(1)}, bf16[512,1024]{1,0:T(8,128)(2,1)S(1)}, u32[]{:S(2)}, u32[]{:S(2)}) collective-permute-start(bf16[512,1024]{1,0:T(8,128)(2,1)S(1)} %convolution_convert_fusion), channel_id=1, source_target_pairs={{0,4},{1,5},{2,6},{3,7},{4,0},{5,1},{6,2},{7,3},{8,12},{9,13},{10,... | collective-permute-start | bytes 3145736 | tf_op jit(solution)/shard_map/ppermute | solution.py:402
  (236 other events, 4885.8 us)
Sparse Core Ops, SparseCore 0:
  1658.8 121.5 all-reduce.21

commit v2 on v1

v2 whole, which is shorter than its diff:
```python
import jax
import jax.numpy as jnp
from jax import lax
from jax.experimental import pallas as pl
from jax.experimental.pallas import tpu as pltpu
from jax.sharding import PartitionSpec as P

FF = 2048
MH = 24
HD = 64
NS = 128
QH = 8
KVH = 2
ATTENTION_HEAD = 64
CONV_K = 4
MIXED = 2 * MH * HD + 2 * NS + (QH + 2 * KVH) * ATTENTION_HEAD
BLOCK = 1024


EPSILON = 1e-05
ROPE_BASE = 100000000000.0


def matmul_plain(left, right):
    return jnp.dot(left, right, preferred_element_type=jnp.float32)


def matmul_left(left, right):
    return lax.dot_general(
        left, right, (((0,), (0,)), ((), ())), preferred_element_type=jnp.float32
    )


def matmul_right(left, right):
    return lax.dot_general(
        left, right, (((1,), (1,)), ((), ())), preferred_element_type=jnp.float32
    )


def rms_scale(values, gain):
    return values * lax.rsqrt(jnp.mean(values * values, axis=-1, keepdims=True) + EPSILON) * gain


def layout(lengths, starts, extent):
    position = jnp.arange(extent, dtype=jnp.int32)
    inside = (position[:, None] >= starts[None, :]) & (
        position[:, None] < starts[None, :] + lengths[None, :]
    )
    number = jnp.arange(1, lengths.shape[0] + 1, dtype=jnp.int32)
    segment = jnp.sum(jnp.where(inside, number[None, :], 0), axis=1) - 1
    first = jnp.sum(jnp.where(inside, starts[None, :], 0), axis=1)
    return (segment, position - first)


def causal_allowed(segment):
    position = jnp.arange(segment.shape[0], dtype=jnp.int32)
    return (segment[:, None] == segment[None, :]) & (position[:, None] >= position[None, :])


def swiglu(gate_val, up_val):
    return jax.nn.silu(gate_val) * up_val


def sigmoid(value):
    return 1.0 / (1.0 + jnp.exp(-value))


def dot_exact(left, right, dims):
    return lax.dot_general(
        left,
        right,
        (dims, ((), ())),
        precision=lax.Precision.HIGHEST,
        preferred_element_type=jnp.float32,
    )


def lane_half(rows):
    return lax.broadcasted_iota(jnp.int32, (rows, 2 * HD), 1) < HD


def pick(half, first, second):
    return jnp.where(half, first, second)


def call_whole(body, outs, args, flops, scratch=(), name="kernel"):
    moved = sum(arg.size * arg.dtype.itemsize for arg in args)
    moved += sum(out.size * out.dtype.itemsize for out in outs)
    return pl.pallas_call(
        body,
        out_shape=outs,
        in_specs=[
            pl.BlockSpec(memory_space=pltpu.SMEM if arg.dtype == jnp.int32 else pltpu.VMEM)
            for arg in args
        ],
        out_specs=[pl.BlockSpec(memory_space=pltpu.VMEM)] * len(outs),
        scratch_shapes=list(scratch),
        compiler_params=pltpu.CompilerParams(vmem_limit_bytes=40 * 1024 * 1024),
        cost_estimate=pl.CostEstimate(flops=flops, bytes_accessed=moved, transcendentals=0),
        name=name,
    )(*args)


def shape(dims, kind=jnp.float32):
    return jax.ShapeDtypeStruct(dims, kind)


def turned(values, cosine, sine, back):
    width = values.shape[1]
    quarter = lax.broadcasted_iota(jnp.int32, values.shape, 1) % ATTENTION_HEAD
    half = ATTENTION_HEAD // 2
    swapped = jnp.where(
        quarter < half,
        -pltpu.roll(values, width - half, 1),
        pltpu.roll(values, half, 1),
    )
    return values * cosine - swapped * sine if back else values * cosine + swapped * sine


def doubled(values, half):
    moved = pltpu.roll(values, ATTENTION_HEAD, 1)
    return (pick(half, values, moved), pick(half, moved, values))


def masked_dot(pair, half, keep_first, other):
    zero = jnp.zeros_like(pair)
    chosen = jnp.where(half, pair, zero) if keep_first else jnp.where(half, zero, pair)
    return matmul_right(chosen, other)


def softmax_rows(scores, allowed):
    scores = jnp.where(allowed, scores * ATTENTION_HEAD ** (-0.5), -1e30)
    raised = jnp.exp(scores - jnp.max(scores, axis=-1, keepdims=True))
    return raised / jnp.sum(raised, axis=-1, keepdims=True)


def attention_front(qkv, cosine, sine, allowed):
    extent = qkv.shape[0]
    pair = 2 * ATTENTION_HEAD
    pairs = QH // 2

    def body(qkv_ref, cos_ref, sin_ref, allowed_ref, low_ref, out_ref):
        half = lane_half(extent)
        can = allowed_ref[...] > 0.0
        cos_val, sin_val = cos_ref[...], sin_ref[...]
        key = turned(qkv_ref[:, pairs * pair : (pairs + 1) * pair], cos_val, sin_val, False)
        key = key.astype(jnp.bfloat16)
        value = qkv_ref[:, (pairs + 1) * pair :].astype(jnp.bfloat16)
        low_ref[:, pairs * pair : (pairs + 1) * pair] = key
        low_ref[:, (pairs + 1) * pair :] = value
        keys = [k.astype(jnp.bfloat16) for k in doubled(key.astype(jnp.float32), half)]
        values = [v.astype(jnp.bfloat16) for v in doubled(value.astype(jnp.float32), half)]
        for number in range(pairs):
            spot = slice(number * pair, (number + 1) * pair)
            query = turned(qkv_ref[:, spot], cos_val, sin_val, False).astype(jnp.bfloat16)
            low_ref[:, spot] = query
            group = number * KVH // pairs
            results = []
            for first in (True, False):
                scores = masked_dot(query, half, first, keys[group])
                probs = softmax_rows(scores, can).astype(jnp.bfloat16)
                results.append(matmul_plain(probs, values[group]))
            out_ref[:, spot] = pick(half, *results).astype(jnp.bfloat16)

    return call_whole(
        body,
        (shape(qkv.shape, jnp.bfloat16), shape((extent, pairs * pair), jnp.bfloat16)),
        (qkv, cosine, sine, allowed),
        QH * 8 * extent**3,
        name="attention_front",
    )


def attention_back(low, heads_grad, cosine, sine, allowed):
    extent = low.shape[0]
    pair = 2 * ATTENTION_HEAD
    pairs = QH // 2
    scale = ATTENTION_HEAD ** (-0.5)

    def body(low_ref, grad_ref, cos_ref, sin_ref, allowed_ref, out_ref):
        half = lane_half(extent)
        can = allowed_ref[...] > 0.0
        cos_val, sin_val = cos_ref[...], sin_ref[...]
        key = low_ref[:, pairs * pair : (pairs + 1) * pair].astype(jnp.float32)
        value = low_ref[:, (pairs + 1) * pair :].astype(jnp.float32)
        keys = [k.astype(jnp.bfloat16) for k in doubled(key, half)]
        values = [v.astype(jnp.bfloat16) for v in doubled(value, half)]
        key_sums = [jnp.zeros((extent, pair), jnp.float32) for _ in range(KVH)]
        value_sums = [jnp.zeros((extent, pair), jnp.float32) for _ in range(KVH)]
        for number in range(pairs):
            spot = slice(number * pair, (number + 1) * pair)
            query = low_ref[:, spot]
            grad = grad_ref[:, spot]
            group = number * KVH // pairs
            q_parts, k_parts, v_parts = [], [], []
            for first in (True, False):
                probs = softmax_rows(masked_dot(query, half, first, keys[group]), can)
                prob_grad = masked_dot(grad, half, first, values[group])
                v_parts.append(matmul_left(probs.astype(jnp.bfloat16), grad))
                inner = jnp.sum(probs * prob_grad, axis=-1, keepdims=True)
                score_grad = (probs * (prob_grad - inner)).astype(jnp.bfloat16)
                q_parts.append(matmul_plain(score_grad, keys[group]))
                k_parts.append(matmul_left(score_grad, query))
            key_sums[group] = key_sums[group] + pick(half, *k_parts)
            value_sums[group] = value_sums[group] + pick(half, *v_parts)
            query_grad = turned(pick(half, *q_parts) * scale, cos_val, sin_val, True)
            out_ref[:, spot] = query_grad.astype(jnp.bfloat16)

        def both(sums):
            return pick(half, *[s + pltpu.roll(s, ATTENTION_HEAD, 1) for s in sums])

        key_grad = turned(both(key_sums) * scale, cos_val, sin_val, True)
        out_ref[:, pairs * pair : (pairs + 1) * pair] = key_grad.astype(jnp.bfloat16)
        out_ref[:, (pairs + 1) * pair :] = both(value_sums).astype(jnp.bfloat16)

    (out,) = call_whole(
        body,
        (shape(low.shape, jnp.bfloat16),),
        (low, heads_grad, cosine, sine, allowed),
        QH * 14 * extent**3,
        name="attention_back",
    )
    return out


def conv_sum(conv_ref, taps_ref, bias_ref, moves_ref, spot):
    value = conv_ref[:, spot]
    total = bias_ref[:, spot] + taps_ref[CONV_K - 1 : CONV_K, spot] * value
    for offset in range(1, CONV_K):
        moved = pltpu.roll(value, offset, 0) * moves_ref[:, offset : offset + 1]
        total = total + taps_ref[CONV_K - 1 - offset : CONV_K - offset, spot] * moved
    return total


def steps_of(raw_ref, shift_ref, rate_ref):
    moved = raw_ref[...] + shift_ref[...]
    step = jnp.maximum(moved, 0.0) + jnp.log1p(jnp.exp(-jnp.abs(moved)))
    rate = -jnp.exp(rate_ref[...])
    return moved, step, rate


def decay_sums(decay, extent):
    row = lax.broadcasted_iota(jnp.int32, (extent, extent), 0)
    column = lax.broadcasted_iota(jnp.int32, (extent, extent), 1)
    lower = jnp.where(row >= column, 1.0, 0.0)
    by_column = dot_exact(lower, decay, ((1,), (0,)))
    by_row = dot_exact(decay, lower, ((0,), (1,)))
    return by_column, by_row, lower


def decay_of(by_column, by_row, head, can):
    spread = by_column[:, head : head + 1] - by_row[head : head + 1, :]
    return jnp.where(can, jnp.exp(jnp.where(can, spread, 0.0)), 0.0)


def mixer_front(conv_in, raw_step, gate_z, taps, bias, shift, rate, skip, gain, moves, allowed):
    extent = conv_in.shape[0]
    width = MH * HD
    pair = 2 * HD

    def body(
        conv_ref,
        raw_ref,
        gate_ref,
        taps_ref,
        bias_ref,
        shift_ref,
        rate_ref,
        skip_ref,
        gain_ref,
        moves_ref,
        allowed_ref,
        act_ref,
        scan_ref,
        gated_ref,
    ):
        half = lane_half(extent)
        can = allowed_ref[...] > 0.0
        for at in range(0, width + 2 * NS, 256):
            spot = slice(at, at + 256)
            total = conv_sum(conv_ref, taps_ref, bias_ref, moves_ref, spot)
            act_ref[:, spot] = (total * sigmoid(total)).astype(jnp.bfloat16)
        _, step, step_rate = steps_of(raw_ref, shift_ref, rate_ref)
        by_column, by_row, _ = decay_sums(step * step_rate, extent)
        inner = matmul_right(act_ref[:, width + NS :], act_ref[:, width : width + NS])
        squares = jnp.zeros((extent, 1), jnp.float32)
        for number in range(MH // 2):
            spot = slice(number * pair, (number + 1) * pair)
            heads = act_ref[:, spot].astype(jnp.float32)
            steps = pick(half, step[:, 2 * number : 2 * number + 1], step[:, 2 * number + 1 : 2 * number + 2])
            scaled = (heads * steps).astype(jnp.bfloat16)
            results = []
            for head in (2 * number, 2 * number + 1):
                weights = (decay_of(by_column, by_row, head, can) * inner).astype(jnp.bfloat16)
                results.append(matmul_plain(weights, scaled))
            scan = pick(half, *results) + skip_ref[:, spot] * heads
            scan_ref[:, spot] = scan
            gate = gate_ref[:, spot]
            value = scan * (gate * sigmoid(gate))
            squares = squares + jnp.sum(value * value, axis=-1, keepdims=True)
        scale = lax.rsqrt(squares / width + EPSILON)
        for number in range(MH // 2):
            spot = slice(number * pair, (number + 1) * pair)
            gate = gate_ref[:, spot]
            value = scan_ref[:, spot] * (gate * sigmoid(gate))
            gated_ref[:, spot] = (value * scale * gain_ref[:, spot]).astype(jnp.bfloat16)

    return call_whole(
        body,
        (
            shape((extent, width + 2 * NS), jnp.bfloat16),
            shape((extent, width)),
            shape((extent, width), jnp.bfloat16),
        ),
        (conv_in, raw_step, gate_z, taps, bias, shift, rate, skip, gain, moves, allowed),
        MH * 16 * extent**3,
        name="mixer_front",
    )


def mixed_columns(z_ref, low_ref, qkv_ref, at):
    for ref in (z_ref, low_ref, qkv_ref):
        if at < ref.shape[1]:
            return ref[:, at : at + 256]
        at -= ref.shape[1]


def mixer_back(
    side,
    qkv_low,
    gated_grad,
    scan,
    act,
    conv_in,
    raw_step,
    gate_z,
    taps,
    bias,
    shift,
    rate,
    skip,
    gain,
    moves,
    allowed,
):
    extent = conv_in.shape[0]
    width = MH * HD
    channels = width + 2 * NS
    pair = 2 * HD

    def body(
        side_ref,
        qkv_ref,
        grad_ref,
        scan_ref,
        act_ref,
        conv_ref,
        raw_ref,
        gate_ref,
        taps_ref,
        bias_ref,
        shift_ref,
        rate_ref,
        skip_ref,
        gain_ref,
        moves_ref,
        allowed_ref,
        z_ref,
        low_ref,
        raw_low_ref,
        mine_ref,
        theirs_ref,
        gain_out,
        taps_out,
        bias_out,
        skip_out,
        shift_out,
        rate_out,
        scan_grad_ref,
        act_grad_ref,
        row_ref,
    ):
        half = lane_half(extent)
        can = allowed_ref[...] > 0.0
        squares = jnp.zeros((extent, 1), jnp.float32)
        dots = jnp.zeros((extent, 1), jnp.float32)
        for at in range(0, width, 256):
            spot = slice(at, at + 256)
            gate = gate_ref[:, spot]
            value = scan_ref[:, spot] * (gate * sigmoid(gate))
            squares = squares + jnp.sum(value * value, axis=-1, keepdims=True)
            dots = dots + jnp.sum(value * gain_ref[:, spot] * grad_ref[:, spot], axis=-1, keepdims=True)
        scale = lax.rsqrt(squares / width + EPSILON)
        common = scale * scale * scale * (dots / width)
        for at in range(0, width, 256):
            spot = slice(at, at + 256)
            gate = gate_ref[:, spot]
            sig = sigmoid(gate)
            silu = gate * sig
            scanned = scan_ref[:, spot]
            value = scanned * silu
            grad = grad_ref[:, spot]
            gain_out[:, spot] = jnp.sum(grad * value * scale, axis=0, keepdims=True)
            value_grad = scale * (gain_ref[:, spot] * grad) - value * common
            z_ref[:, spot] = (value_grad * scanned * (sig * (1.0 + gate * (1.0 - sig)))).astype(
                jnp.bfloat16
            )
            scan_grad_ref[:, spot] = (value_grad * silu).astype(jnp.bfloat16)
        moved, step, step_rate = steps_of(raw_ref, shift_ref, rate_ref)
        by_column, by_row, lower = decay_sums(step * step_rate, extent)
        b_state = act_ref[:, width : width + NS]
        c_state = act_ref[:, width + NS :]
        inner = matmul_right(c_state, b_state)
        inner_grad = jnp.zeros((extent, extent), jnp.float32)
        lane = lax.broadcasted_iota(jnp.int32, (extent, MH), 1)
        by_column_grad = jnp.zeros((extent, MH), jnp.float32)
        step_grad = jnp.zeros((extent, MH), jnp.float32)
        for number in range(MH // 2):
            spot = slice(number * pair, (number + 1) * pair)
            heads = act_ref[:, spot].astype(jnp.float32)
            steps = pick(half, step[:, 2 * number : 2 * number + 1], step[:, 2 * number + 1 : 2 * number + 2])
            scaled = (heads * steps).astype(jnp.bfloat16)
            grad = scan_grad_ref[:, spot]
            results = []
            for first in (True, False):
                head = 2 * number + (0 if first else 1)
                decay = decay_of(by_column, by_row, head, can)
                weight_grad = masked_dot(grad, half, first, scaled)
                mixed = decay * inner
                results.append(matmul_left(mixed.astype(jnp.bfloat16), grad))
                inner_grad = inner_grad + weight_grad * decay
                spread_grad = weight_grad * mixed
                column = jnp.sum(spread_grad, axis=1, keepdims=True)
                by_column_grad = by_column_grad + jnp.where(lane == head, column, 0.0)
                row_ref[head : head + 1, :] = jnp.sum(spread_grad, axis=0, keepdims=True)
            scaled_grad = pick(half, *results)
            grad = grad.astype(jnp.float32)
            act_grad_ref[:, spot] = scaled_grad * steps + skip_ref[:, spot] * grad
            product = scaled_grad * heads
            for first in (True, False):
                head = 2 * number + (0 if first else 1)
                chosen = jnp.where(half, product, 0.0) if first else jnp.where(half, 0.0, product)
                column = jnp.sum(chosen, axis=1, keepdims=True)
                step_grad = step_grad + jnp.where(lane == head, column, 0.0)
            skip_out[:, spot] = jnp.sum(grad * heads, axis=0, keepdims=True)
        inner_low = inner_grad.astype(jnp.bfloat16)
        act_grad_ref[:, width : width + NS] = matmul_left(inner_low, c_state)
        act_grad_ref[:, width + NS :] = matmul_plain(inner_low, b_state)
        decay_grad = dot_exact(lower, by_column_grad, ((0,), (0,))) - dot_exact(
            lower, row_ref[...], ((0,), (1,))
        )
        rate_out[...] = jnp.sum(decay_grad * step * step_rate, axis=0, keepdims=True)
        raw_grad = (step_grad + decay_grad * step_rate) * sigmoid(moved)
        shift_out[...] = jnp.sum(raw_grad, axis=0, keepdims=True)
        raw_low_ref[...] = raw_grad.astype(jnp.bfloat16)
        for at in range(0, channels, 256):
            spot = slice(at, at + 256)
            total = conv_sum(conv_ref, taps_ref, bias_ref, moves_ref, spot)
            sig = sigmoid(total)
            grad = act_grad_ref[:, spot] * (sig * (1.0 + total * (1.0 - sig)))
            bias_out[:, spot] = jnp.sum(grad, axis=0, keepdims=True)
            value = conv_ref[:, spot]
            taps_out[CONV_K - 1 : CONV_K, spot] = jnp.sum(grad * value, axis=0, keepdims=True)
            sums = taps_ref[CONV_K - 1 : CONV_K, spot] * grad
            for offset in range(1, CONV_K):
                kept = grad * moves_ref[:, offset : offset + 1]
                tap = slice(CONV_K - 1 - offset, CONV_K - offset)
                taps_out[tap, spot] = jnp.sum(
                    kept * pltpu.roll(value, offset, 0), axis=0, keepdims=True
                )
                sums = sums + taps_ref[tap, spot] * pltpu.roll(kept, extent - offset, 0)
            low_ref[:, spot] = sums.astype(jnp.bfloat16)
        first = side_ref[0] == 0
        for at in range(0, MIXED // 2, 256):
            spot = slice(at, at + 256)
            near = mixed_columns(z_ref, low_ref, qkv_ref, at)
            far = mixed_columns(z_ref, low_ref, qkv_ref, at + MIXED // 2)
            mine_ref[:, spot] = jnp.where(first, near, far)
            theirs_ref[:, spot] = jnp.where(first, far, near)

    return call_whole(
        body,
        (
            shape((extent, width), jnp.bfloat16),
            shape((extent, channels), jnp.bfloat16),
            shape((extent, MH), jnp.bfloat16),
            shape((extent, MIXED // 2), jnp.bfloat16),
            shape((extent, MIXED // 2), jnp.bfloat16),
            shape((1, width)),
            shape((CONV_K, channels)),
            shape((1, channels)),
            shape((1, width)),
            shape((1, MH)),
            shape((1, MH)),
        ),
        (
            side,
            qkv_low,
            gated_grad,
            scan,
            act,
            conv_in,
            raw_step,
            gate_z,
            taps,
            bias,
            shift,
            rate,
            skip,
            gain,
            moves,
            allowed,
        ),
        MH * 24 * extent**3,
        scratch=(
            pltpu.VMEM((extent, width), jnp.bfloat16),
            pltpu.VMEM((extent, channels), jnp.float32),
            pltpu.VMEM((MH, extent), jnp.float32),
        ),
        name="mixer_back",
    )


def middle(side, pack, spans, tokens, gated, heads, cotangent, valid, gain):
    extent, model = tokens.shape
    width = gated.shape[1]
    q_cols = heads.shape[1]
    groups = pack.shape[0]
    half_ff = FF // 2

    def body(
        side_ref,
        pack_ref,
        tokens_ref,
        gated_ref,
        heads_ref,
        cot_ref,
        valid_ref,
        gain_ref,
        result_ref,
        normed_ref,
        hidden_ref,
        feed_mine,
        feed_theirs,
        gu_mine,
        gu_theirs,
        branch_mine,
        branch_theirs,
        grad_ref,
        gain_out,
        gated_out,
        heads_out,
        *rest,
    ):
        held, sems = rest[:-1], rest[-1]
        loads = []
        for number, (start, count) in enumerate(spans):
            load = pltpu.make_async_copy(
                pack_ref.at[:, pl.ds(start, count), :], held[number], sems.at[number]
            )
            load.start()
            loads.append(load)

        def matrix(number):
            return held[number][...].reshape(groups * spans[number][1], BLOCK)

        first = side_ref[0] == 0

        def split(value, mine, theirs, at):
            half = value.shape[1] // 2
            low, high = value[:, :half], value[:, half:]
            mine[:, at : at + half] = jnp.where(first, low, high)
            theirs[:, at : at + half] = jnp.where(first, high, low)

        is_valid = valid_ref[...] > 0.0
        out_grad = jnp.where(is_valid, cot_ref[...].astype(jnp.float32), 0.0)
        feed_grad = out_grad.astype(jnp.bfloat16)
        split(feed_grad, feed_mine, feed_theirs, 0)
        loads[0].wait()
        loads[1].wait()
        residual = tokens_ref[...].astype(jnp.float32) + (
            matmul_plain(gated_ref[...], matrix(0)) + matmul_plain(heads_ref[...], matrix(1))
        )
        scale = lax.rsqrt(jnp.mean(residual * residual, axis=-1, keepdims=True) + EPSILON)
        gain_val = gain_ref[...]
        normed = (residual * scale * gain_val).astype(jnp.bfloat16)
        normed_ref[...] = normed
        loads[6].wait()
        hidden_grad = matmul_right(feed_grad, matrix(6))
        normed_grad = jnp.zeros((extent, model), jnp.float32)
        feed_out = jnp.zeros((extent, model), jnp.float32)
        gates, ups = [], []
        for part in range(2):
            loads[2 + part].wait()
            loads[4 + part].wait()
            columns = slice(part * half_ff, (part + 1) * half_ff)
            gate = matmul_plain(normed, matrix(2 + part))
            up = matmul_plain(normed, matrix(4 + part))
            sig = sigmoid(gate)
            silu = gate * sig
            hidden = (silu * up).astype(jnp.bfloat16)
            hidden_ref[:, columns] = hidden
            grad = hidden_grad[:, columns]
            gate_low = (grad * up * (sig * (1.0 + gate * (1.0 - sig)))).astype(jnp.bfloat16)
            up_low = (grad * silu).astype(jnp.bfloat16)
            gates.append(gate_low)
            ups.append(up_low)
            normed_grad = normed_grad + (
                matmul_right(gate_low, matrix(2 + part)) + matmul_right(up_low, matrix(4 + part))
            )
            feed_out = feed_out + matmul_plain(hidden, matrix(6)[columns])
        gu_mine[:, :half_ff] = jnp.where(first, gates[0], gates[1])
        gu_theirs[:, :half_ff] = jnp.where(first, gates[1], gates[0])
        gu_mine[:, half_ff:] = jnp.where(first, ups[0], ups[1])
        gu_theirs[:, half_ff:] = jnp.where(first, ups[1], ups[0])
        result_ref[...] = jnp.where(is_valid, residual + feed_out, 0.0).astype(jnp.bfloat16)
        gain_out[...] = jnp.sum(normed_grad * residual * scale, axis=0, keepdims=True)
        scaled = gain_val * normed_grad
        dots = jnp.mean(scaled * residual, axis=-1, keepdims=True)
        residual_grad = out_grad + (scale * scaled - residual * (scale * scale * scale * dots))
        grad_ref[...] = residual_grad
        branch = residual_grad.astype(jnp.bfloat16)
        split(branch, branch_mine, branch_theirs, 0)
        gated_out[...] = matmul_right(branch, matrix(0))
        heads_out[...] = matmul_right(branch, matrix(1)).astype(jnp.bfloat16)

    low = jnp.bfloat16
    outs = (
        shape((extent, model), low),
        shape((extent, model), low),
        shape((extent, FF), low),
        shape((extent, model // 2), low),
        shape((extent, model // 2), low),
        shape((extent, FF), low),
        shape((extent, FF), low),
        shape((extent, model // 2), low),
        shape((extent, model // 2), low),
        shape((extent, model)),
        shape((1, model)),
        shape((extent, width)),
        shape((extent, q_cols), low),
    )
    args = (side, pack, tokens, gated, heads, cotangent, valid, gain)
    spaces = [pltpu.SMEM, pl.ANY] + [pltpu.VMEM] * 6
    return pl.pallas_call(
        body,
        out_shape=outs,
        in_specs=[pl.BlockSpec(memory_space=space) for space in spaces],
        out_specs=[pl.BlockSpec(memory_space=pltpu.VMEM)] * len(outs),
        scratch_shapes=[pltpu.VMEM((groups, count, BLOCK), low) for _, count in spans]
        + [pltpu.SemaphoreType.DMA((len(spans),))],
        compiler_params=pltpu.CompilerParams(vmem_limit_bytes=52 * 1024 * 1024),
        cost_estimate=pl.CostEstimate(
            flops=4 * extent * pack.size, bytes_accessed=2 * pack.size, transcendentals=0
        ),
        name="middle",
    )(*args)


def outer(spots, lefts, rights, segments, z_size):
    widths = [group[0].shape[1] for group in lefts]
    rows = [width // (2 * z_size) for width in widths]
    columns = sum(width for _, width in segments)
    total = len(rights)
    count = len(lefts)

    def body(spots_ref, *refs):
        left_refs = [refs[at * total : (at + 1) * total] for at in range(count)]
        right_refs = refs[count * total : (count + 1) * total]
        mine_ref, theirs_ref = refs[-2], refs[-1]
        first = spots_ref[0] == 0
        quarter = spots_ref[1]
        right = jnp.concatenate(
            [
                jnp.concatenate(
                    [
                        ref[:, pl.ds(pl.multiple_of(start + quarter * size, 128), size)]
                        for start, size in segments
                    ],
                    axis=1,
                )
                for ref in right_refs
            ],
            axis=0,
        )
        at = 0
        for group, size in zip(left_refs, rows):
            for z in range(z_size):
                left = jnp.concatenate(
                    [ref[:, 2 * z * size : 2 * (z + 1) * size] for ref in group], axis=0
                )
                both = matmul_left(left, right).astype(jnp.bfloat16)
                near, far = both[:size], both[size:]
                mine_ref[z, at : at + size, :] = jnp.where(first, near, far)
                theirs_ref[z, at : at + size, :] = jnp.where(first, far, near)
            at += size

    out = shape((z_size, sum(rows), columns), jnp.bfloat16)
    args = (spots,) + tuple(ref for group in lefts for ref in group) + tuple(rights)
    tokens = total * rights[0].shape[0]
    return call_whole(
        body, (out, out), args, 2 * tokens * sum(widths) * columns, name="outer"
    )


def finish(spots, pieces, outs, extra=None):
    size = pieces[0].shape[1]

    def body(spots_ref, *refs):
        pieces_ref = refs[:4]
        out_refs = refs[4 + (extra is not None) :]
        y, c = spots_ref[0], spots_ref[1]
        for quarter in range(4):
            same_y = y == quarter // 2
            same_c = c == quarter % 2
            for out_ref, (_, _, moves) in zip(out_refs, outs):
                for source, rows, column, count in moves[quarter]:
                    own, by_c, by_y, by_yc = [
                        ref[rows, source : source + count] for ref in pieces_ref
                    ]
                    value = jnp.where(
                        same_y,
                        jnp.where(same_c, own, by_c),
                        jnp.where(same_c, by_y, by_yc),
                    )
                    out_ref[:, column : column + count] = value.astype(jnp.float32)
        if extra is not None:
            out_refs[0][:, outs[0][1] - extra.shape[1] :] = refs[4][...]

    args = (spots,) + tuple(pieces) + (() if extra is None else (extra,))
    return call_whole(
        body, tuple(shape((rows, columns)) for rows, columns, _ in outs), args, 0, name="finish"
    )


def block_masks(segment, position):
    extent = segment.shape[0]
    slot = jnp.arange(extent, dtype=jnp.int32)
    moves = [jnp.ones((extent,), jnp.bool_)]
    for offset in range(1, CONV_K):
        moves.append((slot >= offset) & (jnp.roll(segment, offset) == segment))
    half = ATTENTION_HEAD // 2
    inverse = ROPE_BASE ** (-jnp.arange(half, dtype=jnp.float32) / half)
    angle = position.astype(jnp.float32)[:, None] * inverse[None, :]
    return (
        jnp.stack(moves, axis=1).astype(jnp.float32),
        causal_allowed(segment).astype(jnp.float32),
        jnp.tile(jnp.cos(angle), (1, 4)),
        jnp.tile(jnp.sin(angle), (1, 4)),
    )


def forward_pass(tokens_f, gains, mats, a_log, dt_bias, skip_d, segment, position):
    in_gain, conv_w, conv_b, ssm_gain, _, w_raw = gains
    w_conv, w_z, w_qkv = mats
    moves, allowed, cosine, sine = block_masks(segment, position)
    normed_f, pull_norm_one = jax.vjp(rms_scale, tokens_f, in_gain.astype(jnp.float32))
    normed = normed_f.astype(jnp.bfloat16)
    qkv = matmul_plain(normed, w_qkv)
    low, heads_out = attention_front(qkv, cosine, sine, allowed)
    conv_in = matmul_plain(normed, w_conv)
    raw_step = matmul_right(normed, w_raw)
    gate_z = matmul_plain(normed, w_z)
    mixer_args = (
        conv_in,
        raw_step,
        gate_z,
        conv_w.astype(jnp.float32),
        conv_b.astype(jnp.float32)[None],
        dt_bias[None],
        a_log[None],
        jnp.repeat(skip_d, HD)[None],
        ssm_gain.astype(jnp.float32)[None],
        moves,
        allowed,
    )
    act, scan, gated = mixer_front(*mixer_args)
    kept = (pull_norm_one, normed, mixer_args, act, scan, low, (cosine, sine, allowed))
    return (gated, heads_out, kept)


def backward_pass(side, grads, w_raw, mats, kept):
    w_conv, w_z, w_qkv = mats
    pull_norm_one, normed, mixer_args, act, scan, low, turn_args = kept
    residual_grad, gated_grad, heads_grad = grads
    qkv_low = attention_back(low, heads_grad, *turn_args)
    (
        z_low,
        conv_low,
        raw_low,
        mixed_mine,
        mixed_theirs,
        grad_ssm_gain,
        grad_conv_w,
        grad_conv_b,
        skip_lanes,
        grad_dt_bias,
        grad_a_log,
    ) = mixer_back(side, qkv_low, gated_grad, scan, act, *mixer_args)
    grad_skip = jnp.sum(skip_lanes.reshape(MH, HD), axis=1)
    normed_grad = (
        matmul_right(qkv_low, w_qkv)
        + matmul_right(z_low, w_z)
        + matmul_right(conv_low, w_conv)
        + matmul_plain(raw_low, w_raw)
    )
    token_part, grad_in_gain = pull_norm_one(normed_grad)
    tokens_grad = (residual_grad + token_part).astype(jnp.bfloat16)
    raw_rows = matmul_left(raw_low, normed)
    small = (
        grad_in_gain,
        grad_conv_w,
        grad_conv_b[0],
        grad_ssm_gain[0],
        raw_rows,
        grad_a_log[0],
        grad_dt_bias[0],
        grad_skip,
    )
    return (tokens_grad, (mixed_mine, mixed_theirs), small)


AXES = ("shard", "replica")


def place(pieces, positions, dim, count):
    shape = list(pieces[0].shape)
    shape[dim] = count
    total = len(pieces)

    def body(where, *refs):
        out, held, sems = refs[total], refs[total + 1 : 2 * total + 1], refs[-1]
        loads, stores = [], []
        for number in range(total):
            spot = (slice(None),) * dim + (pl.ds(where[number], 1),)
            loads.append(
                pltpu.make_async_copy(refs[number], held[number], sems.at[0, number])
            )
            stores.append(
                pltpu.make_async_copy(held[number], out.at[spot], sems.at[1, number])
            )
        for load in loads:
            load.start()
        for load, store in zip(loads, stores):
            load.wait()
            store.start()
        for store in stores:
            store.wait()

    moved = 2 * sum(piece.size * piece.dtype.itemsize for piece in pieces)
    return pl.pallas_call(
        body,
        out_shape=jax.ShapeDtypeStruct(tuple(shape), pieces[0].dtype),
        in_specs=[pl.BlockSpec(memory_space=pltpu.SMEM)]
        + [pl.BlockSpec(memory_space=pl.ANY)] * total,
        out_specs=pl.BlockSpec(memory_space=pl.ANY),
        scratch_shapes=[pltpu.VMEM(piece.shape, piece.dtype) for piece in pieces]
        + [pltpu.SemaphoreType.DMA((2, total))],
        compiler_params=pltpu.CompilerParams(vmem_limit_bytes=24 * 1024 * 1024),
        cost_estimate=pl.CostEstimate(flops=0, bytes_accessed=moved, transcendentals=0),
        name="place",
    )(jnp.stack(positions).astype(jnp.int32), *pieces)


class Links:
    def __init__(self, shards_of, copies):
        self.z_size = shards_of // 2
        shard = lax.axis_index("shard")
        replica = lax.axis_index("replica")
        self.z, self.x = shard // 2, shard % 2
        self.y, self.c = replica // 2, replica % 2
        everyone = [(s, r) for s in range(shards_of) for r in range(copies)]

        def table(step):
            return [(s * copies + r, step(s, r)) for s, r in everyone]

        self.tables = {
            "x": table(lambda s, r: (s ^ 1) * copies + r),
            "y": table(lambda s, r: s * copies + (r ^ 2)),
            "c": table(lambda s, r: s * copies + (r ^ 1)),
            "z": table(lambda s, r: ((s + 2) % shards_of) * copies + r),
            "z_one": table(lambda s, r: (s ^ 2) * copies + r),
            "z_two": table(lambda s, r: (s ^ 4) * copies + r),
        }

    def send(self, value, axis):
        return lax.ppermute(value, AXES, self.tables[axis])

    def spread(self, value, axis):
        if axis == "z":
            pieces, spots = [value], [self.z]
            for step in range(1, self.z_size):
                pieces.append(self.send(pieces[-1], "z"))
                spots.append((self.z + self.z_size - step) % self.z_size)
            return place(pieces, spots, 0, self.z_size)
        spot = {"x": self.x, "y": self.y, "c": self.c}[axis]
        return place([value, self.send(value, axis)], [spot, 1 - spot], "zxyc".index(axis), 2)

    def gather(self, own, order):
        rows, columns = own.shape
        cut = own.reshape(1, 1, 2, 2, rows // 4, columns)
        cut = lax.dynamic_slice_in_dim(cut, self.c, 1, 3)
        if "y" in order:
            cut = lax.dynamic_slice_in_dim(cut, self.y, 1, 2)
        for axis in order:
            cut = self.spread(cut, axis)
        return cut.reshape(-1, columns)

    def gather_small(self, own):
        other = self.send(own, "x")
        pair = jnp.stack(
            [jnp.where(self.x == 0, own, other), jnp.where(self.x == 0, other, own)]
        )
        pieces = [pair]
        for _ in range(1, self.z_size):
            pieces.append(self.send(pieces[-1], "z"))
        stacked = jnp.stack(pieces)
        return jnp.concatenate(
            [
                lax.dynamic_index_in_dim(stacked, (self.z + self.z_size - at) % self.z_size, 0, False)
                for at in range(self.z_size)
            ]
        )

    def exchange(self, lefts, mine, theirs, segments):
        rights = [mine, self.send(theirs, "y")]
        rights = rights + [self.send(value, "c") for value in rights]
        groups = []
        for left in lefts:
            group = [left, self.send(left, "y")]
            groups.append(group + [self.send(value, "c") for value in group])
        spots = jnp.stack([self.x, self.c]).astype(jnp.int32)
        return outer(spots, groups, rights, segments, self.z_size)

    def reduce(self, mine, theirs):
        moved = self.send(theirs, "x")

        def block(step):
            at = (self.z + 2 * self.z_size - 1 - step) % self.z_size
            return lax.dynamic_index_in_dim(mine, at, 0, False).astype(
                jnp.float32
            ) + lax.dynamic_index_in_dim(moved, at, 0, False).astype(jnp.float32)

        total = block(0).astype(jnp.bfloat16)
        for step in range(1, self.z_size):
            arrived = self.send(total, "z")
            total = (arrived.astype(jnp.float32) + block(step)).astype(jnp.bfloat16)
        by_y = self.send(total, "y")
        return (total, self.send(total, "c"), by_y, self.send(by_y, "c"))

    def total(self, value):
        for axis in ("c", "y", "x", "z_one", "z_two"):
            value = value + self.send(value, axis)
        return value


def pack_small(in_gain, conv_w, conv_b, ssm_gain, ff_gain, raw):
    def rows(value):
        flat = value.reshape(-1)
        return jnp.pad(flat, (0, -flat.shape[0] % 128)).reshape(-1, 128)

    packed = jnp.concatenate([rows(v) for v in (raw.T, in_gain, conv_w, conv_b, ssm_gain, ff_gain)])
    return jnp.pad(packed, ((0, -packed.shape[0] % 16), (0, 0)))


def unpack_small(gathered, own):
    in_gain, conv_w, conv_b, ssm_gain, ff_gain, raw = own
    parts = gathered.shape[0]
    at = 0
    out = []
    for value in (raw.T, in_gain, conv_w, conv_b, ssm_gain, ff_gain):
        count = -(-value.size // 128)
        flat = gathered[:, at : at + count].reshape(parts, -1)[:, : value.size]
        at += count
        shaped = flat.reshape((parts,) + value.shape)
        if value.ndim == 1:
            out.append(shaped.reshape(-1))
        else:
            out.append(shaped.transpose(1, 0, 2).reshape(value.shape[0], -1))
    return tuple(out[1:]) + (out[0],)


def shards(
    copies,
    tokens,
    cotangent,
    seq_lengths,
    seq_starts,
    in_gain,
    w_in,
    conv_w,
    conv_b,
    a_log,
    dt_bias,
    skip_d,
    ssm_gain,
    w_out,
    w_query,
    w_key,
    w_value,
    w_attn_out,
    ff_gain,
    w_gate,
    w_up,
    w_down,
):
    parts = MH * HD // w_out.shape[0]
    width = MH * HD
    channels = width + 2 * NS
    quick = parts == 8 and copies == 4
    links = Links(parts, copies)
    own_small = (in_gain, conv_w, conv_b, ssm_gain, ff_gain, w_in[:, width + channels :])
    own = (
        w_in[:, width : width + channels],
        w_in[:, :width],
        jnp.concatenate([w_query, w_key, w_value], axis=1),
    )
    blocks = (
        w_out,
        w_attn_out,
        w_gate[:, :BLOCK],
        w_gate[:, BLOCK:],
        w_up[:, :BLOCK],
        w_up[:, BLOCK:],
        w_down,
    )
    pieces = 4 if quick else 1
    turn = links.y * 2 + links.c if quick else 0
    cuts, spans, at = [], [], 0
    for value in blocks:
        count = value.shape[0] // pieces
        cuts.append(lax.dynamic_slice_in_dim(value, turn * count, count, 0))
        spans.append((at, count))
        at += count
    pack = jnp.concatenate(cuts, axis=0)
    if quick:
        orders = ("zxyc", "zyxc", "xzc")
        small_all = links.gather_small(pack_small(*own_small))
        mats = tuple(links.gather(value, order) for value, order in zip(own, orders))
        pack = lax.all_gather(pack, AXES, axis=0)
    else:
        small_all = lax.all_gather(pack_small(*own_small), "shard", axis=0)
        mats = tuple(lax.all_gather(value, "shard", axis=0, tiled=True) for value in own)
        pack = lax.all_gather(pack, "shard", axis=0)
    gains = unpack_small(small_all, own_small)
    segment, position = layout(seq_lengths[0], seq_starts[0], tokens.shape[0])
    gated, heads_out, kept = forward_pass(
        tokens.astype(jnp.float32), gains, mats, a_log, dt_bias, skip_d, segment, position
    )
    side = jnp.stack([links.y if quick else jnp.int32(0)]).astype(jnp.int32)
    valid = (segment >= 0).astype(jnp.float32)[:, None]
    (
        result,
        normed_two,
        hidden,
        feed_mine,
        feed_theirs,
        gu_mine,
        gu_theirs,
        branch_mine,
        branch_theirs,
        residual_grad,
        grad_ff_gain,
        gated_grad,
        heads_grad,
    ) = middle(
        side, pack, spans, tokens, gated, heads_out, cotangent, valid, gains[4].astype(jnp.float32)[None]
    )
    tokens_grad, (mixed_mine, mixed_theirs), small = backward_pass(
        side, (residual_grad, gated_grad, heads_grad), gains[5], mats, kept
    )
    small = small + (grad_ff_gain[0],)
    normed = kept[1]
    flat = jnp.concatenate([value.reshape(-1) for value in small])
    flat = jnp.pad(flat, (0, -flat.shape[0] % 1024)).reshape(-1, 128)
    flat = (links.total(flat) if quick else lax.psum(flat, AXES)).reshape(-1)
    totals = []
    at = 0
    for value in small:
        totals.append(flat[at : at + value.size].reshape(value.shape))
        at += value.size
    here = lax.axis_index("shard")

    def mine(value):
        size = value.shape[-1] // parts
        return lax.dynamic_slice_in_dim(value, here * size, size, value.ndim - 1)

    raw_part = mine(totals[4]).T
    q_cols = QH * ATTENTION_HEAD
    k_cols = KVH * ATTENTION_HEAD
    out_rows, attn_rows = w_out.shape[0], w_attn_out.shape[0]
    down_rows, model_rows = w_down.shape[0], w_in.shape[0]
    if quick:
        quarter = BLOCK // 4
        whole = slice(None)

        def plain(rows):
            return [[(0, rows, number * quarter, quarter)] for number in range(4)]

        half_ff, quarter_ff = FF // 2, FF // 4
        edges = (0, width + channels, width + channels + q_cols, MIXED - k_cols, MIXED)
        mixed_moves = [[[] for _ in range(4)] for _ in range(4)]
        for number in range(4):
            for index in range(4):
                low = max(edges[index], number * BLOCK)
                high = min(edges[index + 1], (number + 1) * BLOCK)
                if low < high:
                    mixed_moves[index][number].append(
                        (low - number * BLOCK, whole, low - edges[index], high - low)
                    )
        spots = jnp.stack([links.y, links.c]).astype(jnp.int32)
        down_parts = links.exchange([hidden], feed_mine, feed_theirs, [(0, quarter)])
        feed_parts = links.exchange(
            [normed_two], gu_mine, gu_theirs, [(0, quarter_ff), (half_ff, quarter_ff)]
        )
        out_parts = links.exchange([gated, heads_out], branch_mine, branch_theirs, [(0, quarter)])
        mixed_parts = links.exchange([normed], mixed_mine, mixed_theirs, [(0, BLOCK)])
        (down,) = finish(
            spots, links.reduce(*down_parts), [(down_rows, BLOCK, plain(whole))]
        )
        gate, up = finish(
            spots,
            links.reduce(*feed_parts),
            [
                (
                    model_rows,
                    FF,
                    [[(at, whole, number * quarter_ff, quarter_ff)] for number in range(4)],
                )
                for at in (0, quarter_ff)
            ],
        )
        out, attn = finish(
            spots,
            links.reduce(*out_parts),
            [
                (out_rows, BLOCK, plain(slice(0, out_rows))),
                (attn_rows, BLOCK, plain(slice(out_rows, out_rows + attn_rows))),
            ],
        )
        projection, query, key, value = finish(
            spots,
            links.reduce(*mixed_parts),
            [
                (model_rows, columns, moves)
                for columns, moves in zip(
                    (width + channels + MH, q_cols, k_cols, k_cols), mixed_moves
                )
            ],
            raw_part,
        )
    else:

        def joined(first, second):
            return jnp.concatenate([first, second], axis=1)

        def share(left, right):
            part = lax.psum_scatter(
                matmul_left(left, right).astype(jnp.bfloat16),
                "shard",
                scatter_dimension=0,
                tiled=True,
            )
            return lax.psum(part, "replica").astype(jnp.float32)

        half_ff = FF // 2
        branch = joined(branch_mine, branch_theirs)
        mixed = share(normed, joined(mixed_mine, mixed_theirs))
        down = share(hidden, joined(feed_mine, feed_theirs))
        gate = share(normed_two, joined(gu_mine[:, :half_ff], gu_theirs[:, :half_ff]))
        up = share(normed_two, joined(gu_mine[:, half_ff:], gu_theirs[:, half_ff:]))
        out = share(gated, branch)
        attn = share(heads_out, branch)
        at = width + channels
        projection = joined(mixed[:, :at], raw_part)
        query = mixed[:, at : at + q_cols]
        key = mixed[:, at + q_cols : at + q_cols + k_cols]
        value = mixed[:, at + q_cols + k_cols :]
    return (
        result,
        tokens_grad,
        mine(totals[0]),
        projection,
        mine(totals[1]),
        mine(totals[2]),
        totals[5],
        totals[6],
        totals[7],
        mine(totals[3]),
        out,
        query,
        key,
        value,
        attn,
        mine(totals[8]),
        gate,
        up,
        down,
    )


def solution(mesh):
    in_specs = (
        P(("shard", "replica"), None),
        P(("shard", "replica"), None),
        P(("shard", "replica"), None),
        P(("shard", "replica"), None),
        P("shard"),
        P("shard", None),
        P(None, "shard"),
        P("shard"),
        P(),
        P(),
        P(),
        P("shard"),
        P("shard", None),
        P("shard", None),
        P("shard", None),
        P("shard", None),
        P("shard", None),
        P("shard"),
        P("shard", None),
        P("shard", None),
        P("shard", None),
    )
    out_specs = (
        P(("shard", "replica"), None),
        P(("shard", "replica"), None),
        P("shard"),
        P("shard", None),
        P(None, "shard"),
        P("shard"),
        P(),
        P(),
        P(),
        P("shard"),
        P("shard", None),
        P("shard", None),
        P("shard", None),
        P("shard", None),
        P("shard", None),
        P("shard"),
        P("shard", None),
        P("shard", None),
        P("shard", None),
    )

    def local(*args):
        return shards(mesh.shape["replica"], *args)

    return jax.shard_map(local, mesh=mesh, in_specs=in_specs, out_specs=out_specs, check_vma=False)
```

time: 1960 us -> 424 us (0.22)
  Pallas kernels: 1430 us -> 75.9 us
  waiting for transfers between devices: 257 us -> 182 us
  matrix products: 66.5 us -> 6.66 us
  other arithmetic: 56.1 us -> 17.2 us
    pallas_call x26 -> x11, Pallas kernels: 1430 us -> 21.2 us  [place(): pl.pallas_call(body, out_shape=jax.ShapeDtypeStruct(tuple(shape), pieces[...]
    psum x1 -> x0, waiting for transfers between devices: 106 us -> none  [shards(): flat = lax.psum(flat, AXES).reshape(-1)]
    pallas_call x0 -> x13, Pallas kernels: none -> 54.7 us  [the longest x12 38.9 us: call_whole(): pl.pallas_call(body, out_shape=outs, in_specs=[pl.BlockSpec(memory_space=...]
    ppermute x97 -> x81, waiting for transfers between devices: 151 us -> 181 us  [send(): return lax.ppermute(value, AXES, self.tables[axis])]
    dot_general x9 -> x4, matrix products: 24.1 us -> 1.81 us  [matmul_plain(): return jnp.dot(left, right, preferred_element_type=jnp.float32)]
    ppermute x97 -> x81, starting transfers between devices: 57.8 us -> 69.4 us  [send(): return lax.ppermute(value, AXES, self.tables[axis])]
  transfers between devices with their start and end apart: 98 -> 82, of which waited for: 31 -> 31; matrix products, arithmetic and copies ran while one was open for 9% -> 9% of each run, Pallas kernels for 73% -> 18%
where the time goes in v2:
time: 424 us; the launch traced here: 415 us
  waiting for transfers between devices  182 us (43%)
  Pallas kernels  75.9 us (18%)
  starting transfers between devices  69.5 us (16%)
  local copies, waits for them, and re-layouts  48.1 us (11%)
  other arithmetic  17.2 us (4%)
  between operations  16.5 us (4%)
  matrix products  6.66 us (2%)
    ppermute x81, waiting for transfers between devices, send(): return lax.ppermute(value, AXES, self.tables[axis])  181 us
    ppermute x81, starting transfers between devices, send(): return lax.ppermute(value, AXES, self.tables[axis])  69.4 us
    pallas_call x12, Pallas kernels, call_whole(): pl.pallas_call(body, out_shape=outs, in_specs=[pl.BlockSpec(memory_space=...  38.9 us
    unnamed x263, local copies, waits for them, and re-layouts  32 us
    pallas_call x11, Pallas kernels, place(): pl.pallas_call(body, out_shape=jax.ShapeDtypeStruct(tuple(shape), pieces[...  21.2 us
    pallas_call x1, Pallas kernels, middle(): pl.pallas_call(body, out_shape=outs, in_specs=[pl.BlockSpec(memory_space=...  15.7 us
  transfers between devices with their start and end apart: 82, of which 31 were waited for; matrix products, arithmetic and copies ran while one was open for 9% of the time, Pallas kernels for 18%

profile of v2, /device:TPU:0, one launch (start us, length us, event | category | flops | bytes accessed | tf_op | source)
XLA Modules:
  0.0 415.3 jit_solution(1294558830989215496)
XLA Ops:
  14.8 2.9 collective-permute-start.16
  25.1 2.9 collective-permute-done.4.refs_1_
  28.1 9.6 %collective-permute-done.5.refs_2_ = bf16[1,1,1,1,32,1792]{5,4,3,2,1,0:T(8,128)(2,1)S(1)} collective-permute-done((bf16[1,1,1,1,32,1792]{5,4,3,2,1,0:T(8,128)(2,1)S(1)}, bf16[1,1,1,1,32,1792]{5,4,3,2,1,0:T(8,128)(2,1)S(1)}, u32[]{:S(2)}, u32[]{:S(2)}) %collective-permute-start.5) | collective-permute-done | bytes 114720 | tf_op jit(solution)/shard_map/ppermute | solution.py:887
  40.7 5.9 %collective-permute-done.6.refs_3_ = bf16[1,1,1,1,32,1792]{5,4,3,2,1,0:T(8,128)(2,1)S(1)} collective-permute-done((bf16[1,1,1,1,32,1792]{5,4,3,2,1,0:T(8,128)(2,1)S(1)}, bf16[1,1,1,1,32,1792]{5,4,3,2,1,0:T(8,128)(2,1)S(1)}, u32[]{:S(2)}, u32[]{:S(2)}) %collective-permute-start.6) | collective-permute-done | bytes 114720 | tf_op jit(solution)/shard_map/ppermute | solution.py:887
  51.4 8.4 %collective-permute-done.12.refs_3_ = bf16[1,1,1,1,32,1536]{5,4,3,2,1,0:T(8,128)(2,1)S(1)} collective-permute-done((bf16[1,1,1,1,32,1536]{5,4,3,2,1,0:T(8,128)(2,1)S(1)}, bf16[1,1,1,1,32,1536]{5,4,3,2,1,0:T(8,128)(2,1)S(1)}, u32[]{:S(2)}, u32[]{:S(2)}) %collective-permute-start.12) | collective-permute-done | bytes 98336 | tf_op jit(solution)/shard_map/ppermute | solution.py:887
  63.1 5.3 %collective-permute-done.7.refs_1_ = bf16[4,1,1,1,32,1792]{5,4,3,2,1,0:T(8,128)(2,1)S(1)} collective-permute-done((bf16[4,1,1,1,32,1792]{5,4,3,2,1,0:T(8,128)(2,1)S(1)}, bf16[4,1,1,1,32,1792]{5,4,3,2,1,0:T(8,128)(2,1)S(1)}, u32[]{:S(2)}, u32[]{:S(2)}) %collective-permute-start.7) | collective-permute-done | bytes 458784 | tf_op jit(solution)/shard_map/ppermute | solution.py:887
  78.4 6.0 %collective-permute-done.1 = bf16[2,48,128]{2,1,0:T(8,128)(2,1)S(1)} collective-permute-done((bf16[2,48,128]{2,1,0:T(8,128)(2,1)S(1)}, bf16[2,48,128]{2,1,0:T(8,128)(2,1)S(1)}, u32[]{:S(2)}, u32[]{:S(2)}) %collective-permute-start.1) | collective-permute-done | bytes 24608 | tf_op jit(solution)/shard_map/ppermute | solution.py:887
  85.0 5.2 %collective-permute-done.2 = bf16[2,48,128]{2,1,0:T(8,128)(2,1)} collective-permute-done((bf16[2,48,128]{2,1,0:T(8,128)(2,1)S(1)}, bf16[2,48,128]{2,1,0:T(8,128)(2,1)}, u32[]{:S(2)}, u32[]{:S(2)}) %collective-permute-start.2) | collective-permute-done | bytes 24608 | tf_op jit(solution)/shard_map/ppermute | solution.py:887
  96.0 3.3 place.13.refs_0_
  102.9 13.5 %collective-permute-done.17.refs_1_ = bf16[1,2,2,1,32,768]{5,4,3,2,1,0:T(8,128)(2,1)S(1)} collective-permute-done((bf16[1,2,2,1,32,768]{5,4,3,2,1,0:T(8,128)(2,1)S(1)}, bf16[1,2,2,1,32,768]{5,4,3,2,1,0:T(8,128)(2,1)S(1)}, u32[]{:S(2)}, u32[]{:S(2)}) %collective-permute-start.17) | collective-permute-done | bytes 196640 | tf_op jit(solution)/shard_map/ppermute | solution.py:887
  117.5 16.8 %collective-permute-done.18.refs_2_ = bf16[1,2,2,1,32,768]{5,4,3,2,1,0:T(8,128)(2,1)S(1)} collective-permute-done((bf16[1,2,2,1,32,768]{5,4,3,2,1,0:T(8,128)(2,1)S(1)}, bf16[1,2,2,1,32,768]{5,4,3,2,1,0:T(8,128)(2,1)S(1)}, u32[]{:S(2)}, u32[]{:S(2)}) %collective-permute-start.18) | collective-permute-done | bytes 196640 | tf_op jit(solution)/shard_map/ppermute | solution.py:887
  134.3 2.8 collective-permute-start.19
  137.3 11.5 %collective-permute-done.19.refs_3_ = bf16[1,2,2,1,32,768]{5,4,3,2,1,0:T(8,128)(2,1)S(1)} collective-permute-done((bf16[1,2,2,1,32,768]{5,4,3,2,1,0:T(8,128)(2,1)S(1)}, bf16[1,2,2,1,32,768]{5,4,3,2,1,0:T(8,128)(2,1)S(1)}, u32[]{:S(2)}, u32[]{:S(2)}) %collective-permute-start.19) | collective-permute-done | bytes 196640 | tf_op jit(solution)/shard_map/ppermute | solution.py:887
  161.0 5.2 %mixer_front.1 = (bf16[128,1792]{1,0:T(8,128)(2,1)S(1)}, f32[128,1536]{1,0:T(8,128)S(1)}, bf16[128,1536]{1,0:T(8,128)(2,1)}) custom-call(f32[128,1792]{1,0:T(8,128)S(1)} %fusion.43.conv_ref, f32[128,24]{1,0:T(8,128)S(1)} %fusion.30.raw_ref, f32[128,1536]{1,0:T(8,128)S(1)} %fusion.44.gate_ref, f32[4,1792]{1,0:T(4,128)S(1)} %reshape.481.taps_ref, ...), custom_call_target="tpu_custom_call" | custom-call | flops 805306368 | bytes 3470528 | tf_op jit(solution)/shard_map/mixer_front/pallas_call | solution.py:89
  176.2 2.9 attention_front.1
  184.1 15.7 %middle.1 = (bf16[128,1024]{1,0:T(8,128)(2,1)}, bf16[128,1024]{1,0:T(8,128)(2,1)S(1)}, bf16[128,2048]{1,0:T(8,128)(2,1)}, bf16[128,512]{1,0:T(8,128)(2,1)S(1)}, ...) custom-call(s32[1]{0:T(128)} %bitcast.side_ref, ...), custom_call_target="tpu_custom_call" | custom-call | flops 4294967296 | bytes 16777216 | tf_op jit(solution)/shard_map/middle/pallas_call | solution.py:645
  200.0 3.7 attention_back.1.qkv_ref
  204.9 11.0 %mixer_back.1 = (bf16[128,1536]{1,0:T(8,128)(2,1)S(1)}, bf16[128,1792]{1,0:T(8,128)(2,1)S(1)}, bf16[128,24]{1,0:T(8,128)(2,1)S(1)}, bf16[128,2048]{1,0:T(8,128)(...) custom-call(s32[1]{0:T(128)} %bitcast.side_ref, ...), custom_call_target="tpu_custom_call" | custom-call | flops 1207959552 | bytes 6015364 | tf_op jit(solution)/shard_map/mixer_back/pallas_call | solution.py:89
  226.9 2.8 collective-permute-done.45.refs_9_
  237.2 12.7 %collective-permute-done.22 = f32[296,128]{1,0:T(8,128)S(1)} collective-permute-done((f32[296,128]{1,0:T(8,128)S(1)}, f32[296,128]{1,0:T(8,128)S(1)}, u32[]{:S(2)}, u32[]{:S(2)}) %collective-permute-start.22) | collective-permute-done | bytes 151584 | tf_op jit(solution)/shard_map/ppermute | solution.py:887
  261.6 3.1 collective-permute-done.24
  280.5 3.6 collective-permute-done.71.refs_5_
  297.6 3.2 collective-permute-done.51
  302.6 8.8 %collective-permute-done.61 = bf16[4,128,1024]{2,1,0:T(8,128)(2,1)S(1)} collective-permute-done((bf16[4,128,1024]{2,1,0:T(8,128)(2,1)S(1)}, bf16[4,128,1024]{2,1,0:T(8,128)(2,1)S(1)}, u32[]{:S(2)}, u32[]{:S(2)}) %collective-permute-start.61) | collective-permute-done | bytes 1048608 | tf_op jit(solution)/shard_map/ppermute | solution.py:887
  315.0 18.9 %collective-permute-done.32 = bf16[4,128,1024]{2,1,0:T(8,128)(2,1)S(1)} collective-permute-done((bf16[4,128,1024]{2,1,0:T(8,128)(2,1)S(1)}, bf16[4,128,1024]{2,1,0:T(8,128)(2,1)S(1)}, u32[]{:S(2)}, u32[]{:S(2)}) %collective-permute-start.32) | collective-permute-done | bytes 1048608 | tf_op jit(solution)/shard_map/ppermute | solution.py:887
  336.3 8.0 %collective-permute-done.74 = bf16[4,256,256]{2,1,0:T(8,128)(2,1)S(1)} collective-permute-done((bf16[4,256,256]{2,1,0:T(8,128)(2,1)S(1)}, bf16[4,256,256]{2,1,0:T(8,128)(2,1)S(1)}, u32[]{:S(2)}, u32[]{:S(2)}) %collective-permute-start.74) | collective-permute-done | bytes 524320 | tf_op jit(solution)/shard_map/ppermute | solution.py:887
  349.1 2.9 collective-permute-done.75
  353.2 4.7 %collective-permute-done.63 = bf16[128,1024]{1,0:T(8,128)(2,1)S(1)} collective-permute-done((bf16[128,1024]{1,0:T(8,128)(2,1)S(1)}, bf16[128,1024]{1,0:T(8,128)(2,1)S(1)}, u32[]{:S(2)}, u32[]{:S(2)}) %collective-permute-start.63) | collective-permute-done | bytes 262176 | tf_op jit(solution)/shard_map/ppermute | solution.py:887
  358.9 4.7 %collective-permute-done.34 = bf16[128,1024]{1,0:T(8,128)(2,1)S(1)} collective-permute-done((bf16[128,1024]{1,0:T(8,128)(2,1)S(1)}, bf16[128,1024]{1,0:T(8,128)(2,1)S(1)}, u32[]{:S(2)}, u32[]{:S(2)}) %collective-permute-start.34) | collective-permute-done | bytes 262176 | tf_op jit(solution)/shard_map/ppermute | solution.py:887
  367.3 4.7 %collective-permute-done.64 = bf16[128,1024]{1,0:T(8,128)(2,1)S(1)} collective-permute-done((bf16[128,1024]{1,0:T(8,128)(2,1)S(1)}, bf16[128,1024]{1,0:T(8,128)(2,1)S(1)}, u32[]{:S(2)}, u32[]{:S(2)}) %collective-permute-start.64) | collective-permute-done | bytes 262176 | tf_op jit(solution)/shard_map/ppermute | solution.py:887
  373.9 3.7 collective-permute-done.35
  382.8 4.2 %collective-permute-done.79.refs_2_ = bf16[256,256]{1,0:T(8,128)(2,1)S(1)} collective-permute-done((bf16[256,256]{1,0:T(8,128)(2,1)S(1)}, bf16[256,256]{1,0:T(8,128)(2,1)S(1)}, u32[]{:S(2)}, u32[]{:S(2)}) %collective-permute-start.79) | collective-permute-done | bytes 131104 | tf_op jit(solution)/shard_map/ppermute | solution.py:887
  (543 shorter events, 180.3 us)
Async XLA Ops:
  7.3 174.0 %all-gather.3.cloned.1.call-start = ((), (), s32[]{:S(2)}) async-start(), calls=%async_computation | async-start | bytes 17301504 | tf_op jit(solution)/shard_map/all_gather | solution.py:1040
  14.8 86.3 %collective-permute-start.16 = (bf16[1,1,2,1,32,768]{5,4,3,2,1,0:T(8,128)(2,1)}, bf16[1,1,2,1,32,768]{5,4,3,2,1,0:T(8,128)(2,1)}, u32[]{:S(2)}, u32[]{:S(2)}) collective-permute-start(bf16[1,1,2,1,32,768]{5,4,3,2,1,0:T(8,128)(2,1)} %constant_dynamic-slice_fusion.2.refs_0_), channel_id=1, source_target_pairs={{0,4},{1,5},{2,6},{3,7},{4,0},{5,1},{6,2},{7,3},{8,12},{9,13},{10,... | collective-permute-start | bytes 294920 | tf_op jit(solution)/shard_map/ppermute | solution.py:887
  18.6 58.4 %collective-permute-start = (bf16[48,128]{1,0:T(8,128)(2,1)}, bf16[48,128]{1,0:T(8,128)(2,1)}, u32[]{:S(2)}, u32[]{:S(2)}) collective-permute-start(bf16[48,128]{1,0:T(8,128)(2,1)} %pad.18), channel_id=1, source_target_pairs={{0,4},{1,5},{2,6},{3,7},{4,0},{5,1},{6,2},{7,3},{8,12},{9,13},{10,... | collective-permute-start | bytes 36872 | tf_op jit(solution)/shard_map/ppermute | solution.py:887
  18.8 19.5 %collective-permute-start.10 = (bf16[1,1,1,1,32,1536]{5,4,3,2,1,0:T(8,128)(2,1)S(1)}, bf16[1,1,1,1,32,1536]{5,4,3,2,1,0:T(8,128)(2,1)S(1)}, u32[]{:S(2)}, u32[]{:S(2)}) collective-permute-start(bf16[1,1,1,1,32,1536]{5,4,3,2,1,0:T(8,128)(2,1)S(1)} %constant_dynamic-slice_fusion.3.refs_0_), channel_id=1, source_target_pairs={{0,8},{1,9},{2,10},{3,11},{4,12},{5,13},{6,14},{7,15},{8,16},{9,17... | collective-permute-start | bytes 294920 | tf_op jit(solution)/shard_map/ppermute | solution.py:887
  48.4 19.9 %collective-permute-start.7 = (bf16[4,1,1,1,32,1792]{5,4,3,2,1,0:T(8,128)(2,1)S(1)}, bf16[4,1,1,1,32,1792]{5,4,3,2,1,0:T(8,128)(2,1)S(1)}, u32[]{:S(2)}, u32[]{:S(2)}) collective-permute-start(bf16[4,1,1,1,32,1792]{5,4,3,2,1,0:T(8,128)(2,1)S(1)} %place.11.refs_0_), channel_id=1, source_target_pairs={{0,4},{1,5},{2,6},{3,7},{4,0},{5,1},{6,2},{7,3},{8,12},{9,13},{10,... | collective-permute-start | bytes 1376264 | tf_op jit(solution)/shard_map/ppermute | solution.py:887
  69.6 26.3 %collective-permute-start.8 = (bf16[4,2,1,1,32,1792]{5,4,3,2,1,0:T(8,128)(2,1)S(1)}, bf16[4,2,1,1,32,1792]{5,4,3,2,1,0:T(8,128)(2,1)}, u32[]{:S(2)}, u32[]{:S(2)}) collective-permute-start(bf16[4,2,1,1,32,1792]{5,4,3,2,1,0:T(8,128)(2,1)S(1)} %place.12.refs_0_), channel_id=1, source_target_pairs={{0,2},{1,3},{2,0},{3,1},{4,6},{5,7},{6,4},{7,5},{8,10},{9,11},{10,... | collective-permute-start | bytes 2752520 | tf_op jit(solution)/shard_map/ppermute | solution.py:887
  75.9 17.1 %collective-permute-start.14 = (bf16[4,1,2,1,32,1536]{5,4,3,2,1,0:T(8,128)(2,1)S(1)}, bf16[4,1,2,1,32,1536]{5,4,3,2,1,0:T(8,128)(2,1)S(1)}, u32[]{:S(2)}, u32[]{:S(2)}) collective-permute-start(bf16[4,1,2,1,32,1536]{5,4,3,2,1,0:T(8,128)(2,1)S(1)} %place.16.refs_0_), channel_id=1, source_target_pairs={{0,4},{1,5},{2,6},{3,7},{4,0},{5,1},{6,2},{7,3},{8,12},{9,13},{10,... | collective-permute-start | bytes 2359304 | tf_op jit(solution)/shard_map/ppermute | solution.py:887
  95.9 55.5 %collective-permute-start.15 = (bf16[4,2,2,1,32,1536]{5,4,3,2,1,0:T(8,128)(2,1)S(1)}, bf16[4,2,2,1,32,1536]{5,4,3,2,1,0:T(8,128)(2,1)}, u32[]{:S(2)}, u32[]{:S(2)}) collective-permute-start(bf16[4,2,2,1,32,1536]{5,4,3,2,1,0:T(8,128)(2,1)S(1)} %place.17.refs_0_), channel_id=1, source_target_pairs={{0,1},{1,0},{2,3},{3,2},{4,5},{5,4},{6,7},{7,6},{8,9},{9,8},{10,11... | collective-permute-start | bytes 4718600 | tf_op jit(solution)/shard_map/ppermute | solution.py:887
  99.2 56.3 %collective-permute-start.9 = (bf16[4,2,2,1,32,1792]{5,4,3,2,1,0:T(8,128)(2,1)}, bf16[4,2,2,1,32,1792]{5,4,3,2,1,0:T(8,128)(2,1)}, u32[]{:S(2)}, u32[]{:S(2)}) collective-permute-start(bf16[4,2,2,1,32,1792]{5,4,3,2,1,0:T(8,128)(2,1)} %place.13.refs_0_), channel_id=1, source_target_pairs={{0,1},{1,0},{2,3},{3,2},{4,5},{5,4},{6,7},{7,6},{8,9},{9,8},{10,11... | collective-permute-start | bytes 5505032 | tf_op jit(solution)/shard_map/ppermute | solution.py:887
  116.4 17.9 %collective-permute-start.18 = (bf16[1,2,2,1,32,768]{5,4,3,2,1,0:T(8,128)(2,1)S(1)}, bf16[1,2,2,1,32,768]{5,4,3,2,1,0:T(8,128)(2,1)S(1)}, u32[]{:S(2)}, u32[]{:S(2)}) collective-permute-start(bf16[1,2,2,1,32,768]{5,4,3,2,1,0:T(8,128)(2,1)S(1)} %collective-permute-done.17.refs_1_), channel_id=1, source_target_pairs={{0,8},{1,9},{2,10},{3,11},{4,12},{5,13},{6,14},{7,15},{8,16},{9,17... | collective-permute-start | bytes 589832 | tf_op jit(solution)/shard_map/ppermute | solution.py:887
  151.2 20.4 %collective-permute-start.20 = (bf16[4,2,2,1,32,768]{5,4,3,2,1,0:T(8,128)(2,1)}, bf16[4,2,2,1,32,768]{5,4,3,2,1,0:T(8,128)(2,1)}, u32[]{:S(2)}, u32[]{:S(2)}) collective-permute-start(bf16[4,2,2,1,32,768]{5,4,3,2,1,0:T(8,128)(2,1)} %place.20.refs_0_), channel_id=1, source_target_pairs={{0,1},{1,0},{2,3},{3,2},{4,5},{5,4},{6,7},{7,6},{8,9},{9,8},{10,11... | collective-permute-start | bytes 2359304 | tf_op jit(solution)/shard_map/ppermute | solution.py:887
  179.8 43.5 %collective-permute-start.42 = (bf16[128,512]{1,0:T(8,128)(2,1)S(1)}, bf16[128,512]{1,0:T(8,128)(2,1)}, u32[]{:S(2)}, u32[]{:S(2)}) collective-permute-start(bf16[128,512]{1,0:T(8,128)(2,1)S(1)} %get-tuple-element.65.heads_ref.refs_4_), channel_id=1, source_target_pairs={{0,2},{1,3},{2,0},{3,1},{4,6},{5,7},{6,4},{7,5},{8,10},{9,11},{10,... | collective-permute-start | bytes 393224 | tf_op jit(solution)/shard_map/ppermute | solution.py:887
  180.6 42.9 %collective-permute-start.43 = (bf16[128,512]{1,0:T(8,128)(2,1)S(1)}, bf16[128,512]{1,0:T(8,128)(2,1)}, u32[]{:S(2)}, u32[]{:S(2)}) collective-permute-start(bf16[128,512]{1,0:T(8,128)(2,1)S(1)} %get-tuple-element.65.heads_ref.refs_4_), channel_id=1, source_target_pairs={{0,1},{1,0},{2,3},{3,2},{4,5},{5,4},{6,7},{7,6},{8,9},{9,8},{10,11... | collective-permute-start | bytes 393224 | tf_op jit(solution)/shard_map/ppermute | solution.py:887
  180.7 45.4 %collective-permute-start.40 = (bf16[128,1536]{1,0:T(8,128)(2,1)}, bf16[128,1536]{1,0:T(8,128)(2,1)}, u32[]{:S(2)}, u32[]{:S(2)}) collective-permute-start(bf16[128,1536]{1,0:T(8,128)(2,1)} %get-tuple-element.64.gated_ref.refs_0_), channel_id=1, source_target_pairs={{0,1},{1,0},{2,3},{3,2},{4,5},{5,4},{6,7},{7,6},{8,9},{9,8},{10,11... | collective-permute-start | bytes 1179656 | tf_op jit(solution)/shard_map/ppermute | solution.py:887
  181.1 45.0 %collective-permute-start.41 = (bf16[128,1536]{1,0:T(8,128)(2,1)}, bf16[128,1536]{1,0:T(8,128)(2,1)}, u32[]{:S(2)}, u32[]{:S(2)}) collective-permute-start(bf16[128,1536]{1,0:T(8,128)(2,1)} %collective-permute-done.39.refs_1_), channel_id=1, source_target_pairs={{0,1},{1,0},{2,3},{3,2},{4,5},{5,4},{6,7},{7,6},{8,9},{9,8},{10,11... | collective-permute-start | bytes 1179656 | tf_op jit(solution)/shard_map/ppermute | solution.py:887
  226.1 30.9 %collective-permute-start.58 = (bf16[128,2048]{1,0:T(8,128)(2,1)}, bf16[128,2048]{1,0:T(8,128)(2,1)S(1)}, u32[]{:S(2)}, u32[]{:S(2)}) collective-permute-start(bf16[128,2048]{1,0:T(8,128)(2,1)} %get-tuple-element.99), channel_id=1, source_target_pairs={{0,2},{1,3},{2,0},{3,1},{4,6},{5,7},{6,4},{7,5},{8,10},{9,11},{10,... | collective-permute-start | bytes 1572872 | tf_op jit(solution)/shard_map/ppermute | solution.py:887
  231.1 18.7 %collective-permute-start.22 = (f32[296,128]{1,0:T(8,128)S(1)}, f32[296,128]{1,0:T(8,128)S(1)}, u32[]{:S(2)}, u32[]{:S(2)}) collective-permute-start(f32[296,128]{1,0:T(8,128)S(1)} %fusion.39), channel_id=1, source_target_pairs={{0,2},{1,3},{2,0},{3,1},{4,6},{5,7},{6,4},{7,5},{8,10},{9,11},{10,... | collective-permute-start | bytes 454664 | tf_op jit(solution)/shard_map/ppermute | solution.py:887
  234.6 23.6 %collective-permute-start.48 = (bf16[4,256,256]{2,1,0:T(8,128)(2,1)S(1)}, bf16[4,256,256]{2,1,0:T(8,128)(2,1)S(1)}, u32[]{:S(2)}, u32[]{:S(2)}) collective-permute-start(bf16[4,256,256]{2,1,0:T(8,128)(2,1)S(1)} %get-tuple-element.91), channel_id=1, source_target_pairs={{0,4},{1,5},{2,6},{3,7},{4,0},{5,1},{6,2},{7,3},{8,12},{9,13},{10,... | collective-permute-start | bytes 1572872 | tf_op jit(solution)/shard_map/ppermute | solution.py:887
  236.8 18.2 %collective-permute-start.55 = (bf16[128,1024]{1,0:T(8,128)(2,1)S(1)}, bf16[128,1024]{1,0:T(8,128)(2,1)}, u32[]{:S(2)}, u32[]{:S(2)}) collective-permute-start(bf16[128,1024]{1,0:T(8,128)(2,1)S(1)} %copy-done.71), channel_id=1, source_target_pairs={{0,2},{1,3},{2,0},{3,1},{4,6},{5,7},{6,4},{7,5},{8,10},{9,11},{10,... | collective-permute-start | bytes 786440 | tf_op jit(solution)/shard_map/ppermute | solution.py:887
  260.7 23.5 %collective-permute-start.68 = (bf16[128,2048]{1,0:T(8,128)(2,1)}, bf16[128,2048]{1,0:T(8,128)(2,1)S(1)}, u32[]{:S(2)}, u32[]{:S(2)}) collective-permute-start(bf16[128,2048]{1,0:T(8,128)(2,1)} %get-tuple-element.104.refs_0_), channel_id=1, source_target_pairs={{0,2},{1,3},{2,0},{3,1},{4,6},{5,7},{6,4},{7,5},{8,10},{9,11},{10,... | collective-permute-start | bytes 1572872 | tf_op jit(solution)/shard_map/ppermute | solution.py:887
  267.6 16.5 %collective-permute-start.71 = (bf16[128,512]{1,0:T(8,128)(2,1)}, bf16[128,512]{1,0:T(8,128)(2,1)S(1)}, u32[]{:S(2)}, u32[]{:S(2)}) collective-permute-start(bf16[128,512]{1,0:T(8,128)(2,1)} %copy-done.83), channel_id=1, source_target_pairs={{0,2},{1,3},{2,0},{3,1},{4,6},{5,7},{6,4},{7,5},{8,10},{9,11},{10,... | collective-permute-start | bytes 393224 | tf_op jit(solution)/shard_map/ppermute | solution.py:887
  270.6 17.3 %collective-permute-start.30 = (bf16[128,2048]{1,0:T(8,128)(2,1)S(1)}, bf16[128,2048]{1,0:T(8,128)(2,1)S(1)}, u32[]{:S(2)}, u32[]{:S(2)}) collective-permute-start(bf16[128,2048]{1,0:T(8,128)(2,1)S(1)} %copy-done.63), channel_id=1, source_target_pairs={{0,1},{1,0},{2,3},{3,2},{4,5},{5,4},{6,7},{7,6},{8,9},{9,8},{10,11... | collective-permute-start | bytes 1572872 | tf_op jit(solution)/shard_map/ppermute | solution.py:887
  271.7 16.3 %collective-permute-start.31 = (bf16[128,2048]{1,0:T(8,128)(2,1)}, bf16[128,2048]{1,0:T(8,128)(2,1)S(1)}, u32[]{:S(2)}, u32[]{:S(2)}) collective-permute-start(bf16[128,2048]{1,0:T(8,128)(2,1)} %collective-permute-done.29.refs_5_), channel_id=1, source_target_pairs={{0,1},{1,0},{2,3},{3,2},{4,5},{5,4},{6,7},{7,6},{8,9},{9,8},{10,11... | collective-permute-start | bytes 1572872 | tf_op jit(solution)/shard_map/ppermute | solution.py:887
  285.4 26.0 %collective-permute-start.61 = (bf16[4,128,1024]{2,1,0:T(8,128)(2,1)S(1)}, bf16[4,128,1024]{2,1,0:T(8,128)(2,1)S(1)}, u32[]{:S(2)}, u32[]{:S(2)}) collective-permute-start(bf16[4,128,1024]{2,1,0:T(8,128)(2,1)S(1)} %get-tuple-element.101), channel_id=1, source_target_pairs={{0,4},{1,5},{2,6},{3,7},{4,0},{5,1},{6,2},{7,3},{8,12},{9,13},{10,... | collective-permute-start | bytes 3145736 | tf_op jit(solution)/shard_map/ppermute | solution.py:887
  292.3 41.5 %collective-permute-start.32 = (bf16[4,128,1024]{2,1,0:T(8,128)(2,1)S(1)}, bf16[4,128,1024]{2,1,0:T(8,128)(2,1)S(1)}, u32[]{:S(2)}, u32[]{:S(2)}) collective-permute-start(bf16[4,128,1024]{2,1,0:T(8,128)(2,1)S(1)} %get-tuple-element.86), channel_id=1, source_target_pairs={{0,4},{1,5},{2,6},{3,7},{4,0},{5,1},{6,2},{7,3},{8,12},{9,13},{10,... | collective-permute-start | bytes 3145736 | tf_op jit(solution)/shard_map/ppermute | solution.py:887
  296.6 47.7 %collective-permute-start.74 = (bf16[4,256,256]{2,1,0:T(8,128)(2,1)S(1)}, bf16[4,256,256]{2,1,0:T(8,128)(2,1)S(1)}, u32[]{:S(2)}, u32[]{:S(2)}) collective-permute-start(bf16[4,256,256]{2,1,0:T(8,128)(2,1)S(1)} %get-tuple-element.108), channel_id=1, source_target_pairs={{0,4},{1,5},{2,6},{3,7},{4,0},{5,1},{6,2},{7,3},{8,12},{9,13},{10,... | collective-permute-start | bytes 1572872 | tf_op jit(solution)/shard_map/ppermute | solution.py:887
  311.4 35.3 %collective-permute-start.62 = (bf16[128,1024]{1,0:T(8,128)(2,1)S(1)}, bf16[128,1024]{1,0:T(8,128)(2,1)S(1)}, u32[]{:S(2)}, u32[]{:S(2)}) collective-permute-start(bf16[128,1024]{1,0:T(8,128)(2,1)S(1)} %fusion.17), channel_id=1, source_target_pairs={{0,8},{1,9},{2,10},{3,11},{4,12},{5,13},{6,14},{7,15},{8,16},{9,17... | collective-permute-start | bytes 786440 | tf_op jit(solution)/shard_map/ppermute | solution.py:887
  314.5 66.5 %collective-permute-start.52 = (bf16[256,256]{1,0:T(8,128)(2,1)S(1)}, bf16[256,256]{1,0:T(8,128)(2,1)S(1)}, u32[]{:S(2)}, u32[]{:S(2)}) collective-permute-start(bf16[256,256]{1,0:T(8,128)(2,1)S(1)} %fusion.21.refs_0_), channel_id=1, source_target_pairs={{0,1},{1,0},{2,3},{3,2},{4,5},{5,4},{6,7},{7,6},{8,9},{9,8},{10,11... | collective-permute-start | bytes 393224 | tf_op jit(solution)/shard_map/ppermute | solution.py:887
  314.5 67.2 %collective-permute-start.54 = (bf16[256,256]{1,0:T(8,128)(2,1)S(1)}, bf16[256,256]{1,0:T(8,128)(2,1)S(1)}, u32[]{:S(2)}, u32[]{:S(2)}) collective-permute-start(bf16[256,256]{1,0:T(8,128)(2,1)S(1)} %collective-permute-done.53.refs_2_), channel_id=1, source_target_pairs={{0,1},{1,0},{2,3},{3,2},{4,5},{5,4},{6,7},{7,6},{8,9},{9,8},{10,11... | collective-permute-start | bytes 393224 | tf_op jit(solution)/shard_map/ppermute | solution.py:887
  348.7 14.9 %collective-permute-start.34 = (bf16[128,1024]{1,0:T(8,128)(2,1)S(1)}, bf16[128,1024]{1,0:T(8,128)(2,1)S(1)}, u32[]{:S(2)}, u32[]{:S(2)}) collective-permute-start(bf16[128,1024]{1,0:T(8,128)(2,1)S(1)} %fusion.15), channel_id=1, source_target_pairs={{0,8},{1,9},{2,10},{3,11},{4,12},{5,13},{6,14},{7,15},{8,16},{9,17... | collective-permute-start | bytes 786440 | tf_op jit(solution)/shard_map/ppermute | solution.py:887
  382.3 23.6 %collective-permute-start.65 = (bf16[128,1024]{1,0:T(8,128)(2,1)S(1)}, bf16[128,1024]{1,0:T(8,128)(2,1)S(1)}, u32[]{:S(2)}, u32[]{:S(2)}) collective-permute-start(bf16[128,1024]{1,0:T(8,128)(2,1)S(1)} %fusion.10.refs_0_), channel_id=1, source_target_pairs={{0,1},{1,0},{2,3},{3,2},{4,5},{5,4},{6,7},{7,6},{8,9},{9,8},{10,11... | collective-permute-start | bytes 786440 | tf_op jit(solution)/shard_map/ppermute | solution.py:887
  387.0 18.9 %collective-permute-start.67 = (bf16[128,1024]{1,0:T(8,128)(2,1)S(1)}, bf16[128,1024]{1,0:T(8,128)(2,1)S(1)}, u32[]{:S(2)}, u32[]{:S(2)}) collective-permute-start(bf16[128,1024]{1,0:T(8,128)(2,1)S(1)} %collective-permute-done.66.refs_2_), channel_id=1, source_target_pairs={{0,1},{1,0},{2,3},{3,2},{4,5},{5,4},{6,7},{7,6},{8,9},{9,8},{10,11... | collective-permute-start | bytes 786440 | tf_op jit(solution)/shard_map/ppermute | solution.py:887
  (178 other events, 2166.7 us)
Sparse Core Ops, SparseCore 0:
  13.3 141.4 all-gather.2

commit v3 on v2

--- a/solution.py
+++ b/solution.py
@@ -83,22 +83,28 @@
     return jnp.where(half, first, second)
 
 
-def call_whole(body, outs, args, flops, scratch=(), name="kernel"):
+def call_whole(body, outs, args, flops, scratch=(), name="kernel", after=()):
     moved = sum(arg.size * arg.dtype.itemsize for arg in args)
     moved += sum(out.size * out.dtype.itemsize for out in outs)
+    count = len(args)
+
+    def ordered(*refs):
+        body(*refs[:count], *refs[count + len(after) :])
+
     return pl.pallas_call(
-        body,
+        ordered,
         out_shape=outs,
         in_specs=[
             pl.BlockSpec(memory_space=pltpu.SMEM if arg.dtype == jnp.int32 else pltpu.VMEM)
             for arg in args
-        ],
+        ]
+        + [pl.BlockSpec(memory_space=pl.ANY)] * len(after),
         out_specs=[pl.BlockSpec(memory_space=pltpu.VMEM)] * len(outs),
         scratch_shapes=list(scratch),
         compiler_params=pltpu.CompilerParams(vmem_limit_bytes=40 * 1024 * 1024),
         cost_estimate=pl.CostEstimate(flops=flops, bytes_accessed=moved, transcendentals=0),
         name=name,
-    )(*args)
+    )(*args, *after)
 
 
 def shape(dims, kind=jnp.float32):
@@ -253,12 +259,35 @@
     return jnp.where(can, jnp.exp(jnp.where(can, spread, 0.0)), 0.0)
 
 
-def mixer_front(conv_in, raw_step, gate_z, taps, bias, shift, rate, skip, gain, moves, allowed):
+def mixer_front(
+    side,
+    heads_out,
+    normed,
+    feed_grad,
+    conv_in,
+    raw_step,
+    gate_z,
+    taps,
+    bias,
+    shift,
+    rate,
+    skip,
+    gain,
+    moves,
+    allowed,
+):
     extent = conv_in.shape[0]
+    at_normed = MH * HD + heads_out.shape[1]
+    at_feed = at_normed + normed.shape[1]
+    half_feed = feed_grad.shape[1] // 2
     width = MH * HD
     pair = 2 * HD
 
     def body(
+        side_ref,
+        heads_ref,
+        normed_ref,
+        feed_ref,
         conv_ref,
         raw_ref,
         gate_ref,
@@ -272,8 +301,16 @@
         allowed_ref,
         act_ref,
         scan_ref,
-        gated_ref,
+        mine_ref,
+        theirs_ref,
     ):
+        side_first = side_ref[0] == 0
+        low, high = feed_ref[:, :half_feed], feed_ref[:, half_feed:]
+        for ref in (mine_ref, theirs_ref):
+            ref[:, MH * HD : at_normed] = heads_ref[...]
+            ref[:, at_normed:at_feed] = normed_ref[...]
+        mine_ref[:, at_feed:] = jnp.where(side_first, low, high)
+        theirs_ref[:, at_feed:] = jnp.where(side_first, high, low)
         half = lane_half(extent)
         can = allowed_ref[...] > 0.0
         for at in range(0, width + 2 * NS, 256):
@@ -303,16 +340,19 @@
             spot = slice(number * pair, (number + 1) * pair)
             gate = gate_ref[:, spot]
             value = scan_ref[:, spot] * (gate * sigmoid(gate))
-            gated_ref[:, spot] = (value * scale * gain_ref[:, spot]).astype(jnp.bfloat16)
+            gated = (value * scale * gain_ref[:, spot]).astype(jnp.bfloat16)
+            mine_ref[:, spot] = gated
+            theirs_ref[:, spot] = gated
 
     return call_whole(
         body,
         (
             shape((extent, width + 2 * NS), jnp.bfloat16),
             shape((extent, width)),
-            shape((extent, width), jnp.bfloat16),
+            shape((extent, at_feed + half_feed), jnp.bfloat16),
+            shape((extent, at_feed + half_feed), jnp.bfloat16),
         ),
-        (conv_in, raw_step, gate_z, taps, bias, shift, rate, skip, gain, moves, allowed),
+        (side, heads_out, normed, feed_grad, conv_in, raw_step, gate_z, taps, bias, shift, rate, skip, gain, moves, allowed),
         MH * 16 * extent**3,
         name="mixer_front",
     )
@@ -521,10 +561,10 @@
     )
 
 
-def middle(side, pack, spans, tokens, gated, heads, cotangent, valid, gain):
+def middle(side, pack, spans, tokens, early, cotangent, valid, gain):
     extent, model = tokens.shape
-    width = gated.shape[1]
-    q_cols = heads.shape[1]
+    width = MH * HD
+    q_cols = QH * ATTENTION_HEAD
     groups = pack.shape[0]
     half_ff = FF // 2
 
@@ -532,20 +572,13 @@
         side_ref,
         pack_ref,
         tokens_ref,
-        gated_ref,
-        heads_ref,
+        early_ref,
         cot_ref,
         valid_ref,
         gain_ref,
         result_ref,
-        normed_ref,
-        hidden_ref,
-        feed_mine,
-        feed_theirs,
-        gu_mine,
-        gu_theirs,
-        branch_mine,
-        branch_theirs,
+        mine_ref,
+        theirs_ref,
         grad_ref,
         gain_out,
         gated_out,
@@ -566,25 +599,24 @@
 
         first = side_ref[0] == 0
 
-        def split(value, mine, theirs, at):
-            half = value.shape[1] // 2
-            low, high = value[:, :half], value[:, half:]
-            mine[:, at : at + half] = jnp.where(first, low, high)
-            theirs[:, at : at + half] = jnp.where(first, high, low)
+        def both(at, low, high):
+            mine_ref[:, at : at + low.shape[1]] = jnp.where(first, low, high)
+            theirs_ref[:, at : at + low.shape[1]] = jnp.where(first, high, low)
 
         is_valid = valid_ref[...] > 0.0
         out_grad = jnp.where(is_valid, cot_ref[...].astype(jnp.float32), 0.0)
         feed_grad = out_grad.astype(jnp.bfloat16)
-        split(feed_grad, feed_mine, feed_theirs, 0)
         loads[0].wait()
         loads[1].wait()
         residual = tokens_ref[...].astype(jnp.float32) + (
-            matmul_plain(gated_ref[...], matrix(0)) + matmul_plain(heads_ref[...], matrix(1))
+            matmul_plain(early_ref[:, :width], matrix(0))
+            + matmul_plain(early_ref[:, width : width + q_cols], matrix(1))
         )
         scale = lax.rsqrt(jnp.mean(residual * residual, axis=-1, keepdims=True) + EPSILON)
         gain_val = gain_ref[...]
         normed = (residual * scale * gain_val).astype(jnp.bfloat16)
-        normed_ref[...] = normed
+        mine_ref[:, :model] = normed
+        theirs_ref[:, :model] = normed
         loads[6].wait()
         hidden_grad = matmul_right(feed_grad, matrix(6))
         normed_grad = jnp.zeros((extent, model), jnp.float32)
@@ -599,7 +631,9 @@
             sig = sigmoid(gate)
             silu = gate * sig
             hidden = (silu * up).astype(jnp.bfloat16)
-            hidden_ref[:, columns] = hidden
+            at = model + FF + part * half_ff
+            mine_ref[:, at : at + half_ff] = hidden
+            theirs_ref[:, at : at + half_ff] = hidden
             grad = hidden_grad[:, columns]
             gate_low = (grad * up * (sig * (1.0 + gate * (1.0 - sig)))).astype(jnp.bfloat16)
             up_low = (grad * silu).astype(jnp.bfloat16)
@@ -609,10 +643,8 @@
                 matmul_right(gate_low, matrix(2 + part)) + matmul_right(up_low, matrix(4 + part))
             )
             feed_out = feed_out + matmul_plain(hidden, matrix(6)[columns])
-        gu_mine[:, :half_ff] = jnp.where(first, gates[0], gates[1])
-        gu_theirs[:, :half_ff] = jnp.where(first, gates[1], gates[0])
-        gu_mine[:, half_ff:] = jnp.where(first, ups[0], ups[1])
-        gu_theirs[:, half_ff:] = jnp.where(first, ups[1], ups[0])
+        both(model, *gates)
+        both(model + half_ff, *ups)
         result_ref[...] = jnp.where(is_valid, residual + feed_out, 0.0).astype(jnp.bfloat16)
         gain_out[...] = jnp.sum(normed_grad * residual * scale, axis=0, keepdims=True)
         scaled = gain_val * normed_grad
@@ -620,28 +652,23 @@
         residual_grad = out_grad + (scale * scaled - residual * (scale * scale * scale * dots))
         grad_ref[...] = residual_grad
         branch = residual_grad.astype(jnp.bfloat16)
-        split(branch, branch_mine, branch_theirs, 0)
+        both(model + 2 * FF, branch[:, : model // 2], branch[:, model // 2 :])
         gated_out[...] = matmul_right(branch, matrix(0))
         heads_out[...] = matmul_right(branch, matrix(1)).astype(jnp.bfloat16)
 
     low = jnp.bfloat16
+    late = model + 2 * FF + model // 2
     outs = (
         shape((extent, model), low),
-        shape((extent, model), low),
-        shape((extent, FF), low),
-        shape((extent, model // 2), low),
-        shape((extent, model // 2), low),
-        shape((extent, FF), low),
-        shape((extent, FF), low),
-        shape((extent, model // 2), low),
-        shape((extent, model // 2), low),
+        shape((extent, late), low),
+        shape((extent, late), low),
         shape((extent, model)),
         shape((1, model)),
         shape((extent, width)),
         shape((extent, q_cols), low),
     )
-    args = (side, pack, tokens, gated, heads, cotangent, valid, gain)
-    spaces = [pltpu.SMEM, pl.ANY] + [pltpu.VMEM] * 6
+    args = (side, pack, tokens, early, cotangent, valid, gain)
+    spaces = [pltpu.SMEM, pl.ANY] + [pltpu.VMEM] * 5
     return pl.pallas_call(
         body,
         out_shape=outs,
@@ -657,49 +684,123 @@
     )(*args)
 
 
-def outer(spots, lefts, rights, segments, z_size):
-    widths = [group[0].shape[1] for group in lefts]
-    rows = [width // (2 * z_size) for width in widths]
-    columns = sum(width for _, width in segments)
-    total = len(rights)
-    count = len(lefts)
+def outer(spots, terms, z_size, apart, after=()):
+    rows = [width // (2 * z_size) for _, _, width, _, _ in terms]
+    columns = sum(size for _, size in terms[0][4])
+    arrays = []
+    for lefts, _, _, rights, _ in terms:
+        for value in lefts + rights:
+            if not any(value is held for held in arrays):
+                arrays.append(value)
 
     def body(spots_ref, *refs):
-        left_refs = [refs[at * total : (at + 1) * total] for at in range(count)]
-        right_refs = refs[count * total : (count + 1) * total]
-        mine_ref, theirs_ref = refs[-2], refs[-1]
         first = spots_ref[0] == 0
         quarter = spots_ref[1]
-        right = jnp.concatenate(
-            [
-                jnp.concatenate(
-                    [
-                        ref[:, pl.ds(pl.multiple_of(start + quarter * size, 128), size)]
-                        for start, size in segments
-                    ],
-                    axis=1,
-                )
-                for ref in right_refs
-            ],
-            axis=0,
-        )
+
+        def ref_of(value):
+            return refs[[held is value for held in arrays].index(True)]
+
         at = 0
-        for group, size in zip(left_refs, rows):
+        for (lefts, begin, _, rights, segments), size in zip(terms, rows):
+            right = jnp.concatenate(
+                [
+                    jnp.concatenate(
+                        [
+                            ref_of(value)[:, pl.ds(pl.multiple_of(start + quarter * width, 128), width)]
+                            for start, width in segments
+                        ],
+                        axis=1,
+                    )
+                    for value in rights
+                ],
+                axis=0,
+            )
             for z in range(z_size):
+                low = begin + 2 * z * size
                 left = jnp.concatenate(
-                    [ref[:, 2 * z * size : 2 * (z + 1) * size] for ref in group], axis=0
+                    [ref_of(value)[:, low : low + 2 * size] for value in lefts], axis=0
                 )
                 both = matmul_left(left, right).astype(jnp.bfloat16)
-                near, far = both[:size], both[size:]
-                mine_ref[z, at : at + size, :] = jnp.where(first, near, far)
-                theirs_ref[z, at : at + size, :] = jnp.where(first, far, near)
+                even, odd = both[:size], both[size:]
+                if apart:
+                    refs[-2][z, at : at + size, :] = jnp.where(first, even, odd)
+                    refs[-1][z, at : at + size, :] = jnp.where(first, odd, even)
+                else:
+                    refs[-1][z, 0, at : at + size, :] = even
+                    refs[-1][z, 1, at : at + size, :] = odd
             at += size
 
-    out = shape((z_size, sum(rows), columns), jnp.bfloat16)
-    args = (spots,) + tuple(ref for group in lefts for ref in group) + tuple(rights)
-    tokens = total * rights[0].shape[0]
+    if apart:
+        outs = (shape((z_size, sum(rows), columns), jnp.bfloat16),) * 2
+    else:
+        outs = (shape((z_size, 2, sum(rows), columns), jnp.bfloat16),)
+    tokens = sum(value.shape[0] for value in terms[0][3])
+    flops = 4 * z_size * tokens * sum(rows) * columns
+    return call_whole(body, outs, (spots, *arrays), flops, name="outer", after=after)
+
+
+def pack_grads(raw, in_gain, taps, bias, ssm_gain, ff_gain, heads, parts):
+    def body(*refs):
+        raw_ref, in_ref, taps_ref, bias_ref, ssm_ref, ff_ref = refs[:6]
+        out = refs[-1]
+        out[...] = jnp.zeros(out.shape, jnp.float32)
+
+        def put(part, row, ref, size):
+            begin = part * size
+            rows = ref.shape[0]
+            for at in range(0, size, 128):
+                count = min(128, size - at)
+                out[part, row : row + rows, :count] = ref[:, begin + at : begin + at + count]
+                row += rows
+
+        for part in range(parts):
+            at = 0
+            for ref in (raw_ref, in_ref, taps_ref, bias_ref, ssm_ref, ff_ref):
+                size = ref.shape[1] // parts
+                put(part, at, ref, size)
+                at += ref.shape[0] * -(-size // 128)
+            for number, ref in enumerate(refs[6:9]):
+                out[part, 40 + number : 41 + number, :MH] = ref[...]
+
+    (out,) = call_whole(
+        body,
+        (shape((parts, 48, 128)),),
+        (raw, in_gain, taps, bias, ssm_gain, ff_gain) + tuple(heads),
+        0,
+        name="pack_grads",
+    )
+    return out
+
+
+def unpack_grads(spots, block, heads, sizes):
+    count = len(heads)
+
+    def body(spots_ref, block_ref, *refs):
+        z = spots_ref[0]
+        head_refs, outs = refs[:count], refs[count:]
+        total = jnp.zeros(heads[0].shape, jnp.float32)
+        for at in range(count):
+            step = lax.rem(z + (count - at), count)
+            row = head_refs[0][...]
+            for number in range(1, count):
+                row = jnp.where(step == number, head_refs[number][...], row)
+            total = total + row
+        outs[0][...] = block_ref[:MH, :].T
+        at = MH
+        for out, (rows, size) in zip(outs[1:], sizes):
+            for begin in range(0, size, 128):
+                width = min(128, size - begin)
+                out[:, begin : begin + width] = block_ref[at : at + rows, :width]
+                at += rows
+        for number, out in enumerate(outs[1 + len(sizes) :]):
+            out[...] = total[number : number + 1, :MH]
+
     return call_whole(
-        body, (out, out), args, 2 * tokens * sum(widths) * columns, name="outer"
+        body,
+        (shape((128, MH)),) + tuple(shape(size) for size in sizes) + (shape((1, MH)),) * 3,
+        (spots, block) + tuple(heads),
+        0,
+        name="unpack_grads",
     )
 
 
@@ -750,7 +851,7 @@
     )
 
 
-def forward_pass(tokens_f, gains, mats, a_log, dt_bias, skip_d, segment, position):
+def forward_pass(side, feed_grad, tokens_f, gains, mats, a_log, dt_bias, skip_d, segment, position):
     in_gain, conv_w, conv_b, ssm_gain, _, w_raw = gains
     w_conv, w_z, w_qkv = mats
     moves, allowed, cosine, sine = block_masks(segment, position)
@@ -774,9 +875,11 @@
         moves,
         allowed,
     )
-    act, scan, gated = mixer_front(*mixer_args)
+    act, scan, early_mine, early_theirs = mixer_front(
+        side, heads_out, normed, feed_grad, *mixer_args
+    )
     kept = (pull_norm_one, normed, mixer_args, act, scan, low, (cosine, sine, allowed))
-    return (gated, heads_out, kept)
+    return (early_mine, early_theirs, kept)
 
 
 def backward_pass(side, grads, w_raw, mats, kept):
@@ -808,14 +911,14 @@
     tokens_grad = (residual_grad + token_part).astype(jnp.bfloat16)
     raw_rows = matmul_left(raw_low, normed)
     small = (
-        grad_in_gain,
+        raw_rows,
+        grad_in_gain[None],
         grad_conv_w,
-        grad_conv_b[0],
-        grad_ssm_gain[0],
-        raw_rows,
-        grad_a_log[0],
-        grad_dt_bias[0],
-        grad_skip,
+        grad_conv_b,
+        grad_ssm_gain,
+        grad_a_log,
+        grad_dt_bias,
+        grad_skip[None],
     )
     return (tokens_grad, (mixed_mine, mixed_theirs), small)
 
@@ -879,8 +982,6 @@
             "y": table(lambda s, r: s * copies + (r ^ 2)),
             "c": table(lambda s, r: s * copies + (r ^ 1)),
             "z": table(lambda s, r: ((s + 2) % shards_of) * copies + r),
-            "z_one": table(lambda s, r: (s ^ 2) * copies + r),
-            "z_two": table(lambda s, r: (s ^ 4) * copies + r),
         }
 
     def send(self, value, axis):
@@ -922,36 +1023,54 @@
             ]
         )
 
-    def exchange(self, lefts, mine, theirs, segments):
-        rights = [mine, self.send(theirs, "y")]
-        rights = rights + [self.send(value, "c") for value in rights]
-        groups = []
-        for left in lefts:
-            group = [left, self.send(left, "y")]
-            groups.append(group + [self.send(value, "c") for value in group])
-        spots = jnp.stack([self.x, self.c]).astype(jnp.int32)
-        return outer(spots, groups, rights, segments, self.z_size)
-
-    def reduce(self, mine, theirs):
-        moved = self.send(theirs, "x")
-
-        def block(step):
-            at = (self.z + 2 * self.z_size - 1 - step) % self.z_size
-            return lax.dynamic_index_in_dim(mine, at, 0, False).astype(
-                jnp.float32
-            ) + lax.dynamic_index_in_dim(moved, at, 0, False).astype(jnp.float32)
-
+    def near(self, mine, theirs):
+        values = [mine, self.send(theirs, "y")]
+        return values + [self.send(value, "c") for value in values]
+
+    def around(self, block):
         total = block(0).astype(jnp.bfloat16)
         for step in range(1, self.z_size):
             arrived = self.send(total, "z")
             total = (arrived.astype(jnp.float32) + block(step)).astype(jnp.bfloat16)
+        return total
+
+    def at_step(self, value, step):
+        at = (self.z + 2 * self.z_size - 1 - step) % self.z_size
+        return lax.dynamic_index_in_dim(value, at, 0, False).astype(jnp.float32)
+
+    def reduce_small(self, value):
+        value = value + self.send(value, "c")
+        value = value + self.send(value, "y")
+        value = value.reshape(self.z_size, 2, 48, 128)
+        mine = lax.dynamic_index_in_dim(value, self.x, 1, False)
+        theirs = lax.dynamic_index_in_dim(value, 1 - self.x, 1, False)
+        value = mine + self.send(theirs, "x")
+        heads = [value[0, 40:]]
+        total = self.at_step(value, 0)
+        for step in range(1, self.z_size):
+            arrived = self.send(total, "z")
+            heads.append(arrived[40:])
+            total = jnp.concatenate([arrived[:40] + self.at_step(value, step)[:40], arrived[40:]])
+        return total, heads
+
+    def quarters(self, total):
         by_y = self.send(total, "y")
         return (total, self.send(total, "c"), by_y, self.send(by_y, "c"))
 
-    def total(self, value):
-        for axis in ("c", "y", "x", "z_one", "z_two"):
-            value = value + self.send(value, axis)
-        return value
+    def reduce_xz(self, mine, theirs):
+        moved = self.send(theirs, "x")
+        return self.quarters(
+            self.around(lambda step: self.at_step(mine, step) + self.at_step(moved, step))
+        )
+
+    def reduce_zx(self, value):
+        total = self.around(lambda step: self.at_step(value, step))
+        mine = lax.dynamic_index_in_dim(total, self.x, 0, False)
+        theirs = lax.dynamic_index_in_dim(total, 1 - self.x, 0, False)
+        moved = self.send(theirs, "x")
+        return self.quarters(
+            (mine.astype(jnp.float32) + moved.astype(jnp.float32)).astype(jnp.bfloat16)
+        )
 
 
 def pack_small(in_gain, conv_w, conv_b, ssm_gain, ff_gain, raw):
@@ -1044,48 +1163,42 @@
         pack = lax.all_gather(pack, "shard", axis=0)
     gains = unpack_small(small_all, own_small)
     segment, position = layout(seq_lengths[0], seq_starts[0], tokens.shape[0])
-    gated, heads_out, kept = forward_pass(
-        tokens.astype(jnp.float32), gains, mats, a_log, dt_bias, skip_d, segment, position
-    )
     side = jnp.stack([links.y if quick else jnp.int32(0)]).astype(jnp.int32)
     valid = (segment >= 0).astype(jnp.float32)[:, None]
+    feed_grad = jnp.where(valid > 0.0, cotangent, 0.0).astype(jnp.bfloat16)
+    early_mine, early_theirs, kept = forward_pass(
+        side,
+        feed_grad,
+        tokens.astype(jnp.float32),
+        gains,
+        mats,
+        a_log,
+        dt_bias,
+        skip_d,
+        segment,
+        position,
+    )
     (
         result,
-        normed_two,
-        hidden,
-        feed_mine,
-        feed_theirs,
-        gu_mine,
-        gu_theirs,
-        branch_mine,
-        branch_theirs,
+        late_mine,
+        late_theirs,
         residual_grad,
         grad_ff_gain,
         gated_grad,
         heads_grad,
     ) = middle(
-        side, pack, spans, tokens, gated, heads_out, cotangent, valid, gains[4].astype(jnp.float32)[None]
+        side, pack, spans, tokens, early_mine, cotangent, valid, gains[4].astype(jnp.float32)[None]
     )
     tokens_grad, (mixed_mine, mixed_theirs), small = backward_pass(
         side, (residual_grad, gated_grad, heads_grad), gains[5], mats, kept
     )
-    small = small + (grad_ff_gain[0],)
-    normed = kept[1]
-    flat = jnp.concatenate([value.reshape(-1) for value in small])
-    flat = jnp.pad(flat, (0, -flat.shape[0] % 1024)).reshape(-1, 128)
-    flat = (links.total(flat) if quick else lax.psum(flat, AXES)).reshape(-1)
-    totals = []
-    at = 0
-    for value in small:
-        totals.append(flat[at : at + value.size].reshape(value.shape))
-        at += value.size
     here = lax.axis_index("shard")
+    model = w_in.shape[0] * parts
 
     def mine(value):
         size = value.shape[-1] // parts
         return lax.dynamic_slice_in_dim(value, here * size, size, value.ndim - 1)
 
-    raw_part = mine(totals[4]).T
     q_cols = QH * ATTENTION_HEAD
     k_cols = KVH * ATTENTION_HEAD
     out_rows, attn_rows = w_out.shape[0], w_attn_out.shape[0]
@@ -1109,18 +1222,56 @@
                         (low - number * BLOCK, whole, low - edges[index], high - low)
                     )
         spots = jnp.stack([links.y, links.c]).astype(jnp.int32)
-        down_parts = links.exchange([hidden], feed_mine, feed_theirs, [(0, quarter)])
-        feed_parts = links.exchange(
-            [normed_two], gu_mine, gu_theirs, [(0, quarter_ff), (half_ff, quarter_ff)]
+        early_four = links.near(early_mine, early_theirs)
+        late_four = links.near(late_mine, late_theirs)
+        mixed_four = links.near(mixed_mine, mixed_theirs)
+        place_spots = jnp.stack([links.x, links.c]).astype(jnp.int32)
+        at_normed = width + q_cols
+        at_hidden = model + FF
+        packed = pack_grads(*small[:5], grad_ff_gain, small[5:], parts)
+        feed_parts = outer(
+            place_spots,
+            [
+                (
+                    late_four,
+                    0,
+                    model,
+                    late_four,
+                    [(model, quarter_ff), (model + half_ff, quarter_ff)],
+                )
+            ],
+            links.z_size,
+            True,
         )
-        out_parts = links.exchange([gated, heads_out], branch_mine, branch_theirs, [(0, quarter)])
-        mixed_parts = links.exchange([normed], mixed_mine, mixed_theirs, [(0, BLOCK)])
-        (down,) = finish(
-            spots, links.reduce(*down_parts), [(down_rows, BLOCK, plain(whole))]
+        out_right = (late_four, [(at_hidden + FF, quarter)])
+        (out_parts,) = outer(
+            place_spots,
+            [
+                (early_four, 0, width) + out_right,
+                (early_four, width, q_cols) + out_right,
+                (late_four, at_hidden, FF, early_four, [(at_normed + model, quarter)]),
+            ],
+            links.z_size,
+            False,
         )
+        mixed_parts = outer(
+            place_spots,
+            [(early_four, at_normed, model, mixed_four, [(0, BLOCK)])],
+            links.z_size,
+            True,
+        )
+        block, head_rows = links.reduce_small(packed)
+        raw_part, *totals = unpack_grads(
+            jnp.stack([links.z]).astype(jnp.int32),
+            block,
+            head_rows,
+            [(value.shape[0], value.shape[1] // parts) for value in small[1:5]]
+            + [(1, model // parts)],
+        )
+        totals = [totals[0][0], totals[1]] + [value[0] for value in totals[2:]]
         gate, up = finish(
             spots,
-            links.reduce(*feed_parts),
+            links.reduce_xz(*feed_parts),
             [
                 (
                     model_rows,
@@ -1130,17 +1281,22 @@
                 for at in (0, quarter_ff)
             ],
         )
-        out, attn = finish(
+        out, attn, down = finish(
             spots,
-            links.reduce(*out_parts),
+            links.reduce_zx(out_parts),
             [
-                (out_rows, BLOCK, plain(slice(0, out_rows))),
-                (attn_rows, BLOCK, plain(slice(out_rows, out_rows + attn_rows))),
+                (rows, BLOCK, plain(slice(at, at + rows)))
+                for rows, at in (
+                    (out_rows, 0),
+                    (attn_rows, out_rows),
+                    (down_rows, out_rows + attn_rows),
+                )
             ],
         )
+        mixed_pieces = links.reduce_xz(*mixed_parts)
         projection, query, key, value = finish(
             spots,
-            links.reduce(*mixed_parts),
+            mixed_pieces,
             [
                 (model_rows, columns, moves)
                 for columns, moves in zip(
@@ -1164,13 +1320,25 @@
             return lax.psum(part, "replica").astype(jnp.float32)
 
         half_ff = FF // 2
-        branch = joined(branch_mine, branch_theirs)
-        mixed = share(normed, joined(mixed_mine, mixed_theirs))
-        down = share(hidden, joined(feed_mine, feed_theirs))
-        gate = share(normed_two, joined(gu_mine[:, :half_ff], gu_theirs[:, :half_ff]))
-        up = share(normed_two, joined(gu_mine[:, half_ff:], gu_theirs[:, half_ff:]))
-        out = share(gated, branch)
-        attn = share(heads_out, branch)
+        branch = joined(late_mine[:, model + 2 * FF :], late_theirs[:, model + 2 * FF :])
+        mixed = share(kept[1], joined(mixed_mine, mixed_theirs))
+        hidden = late_mine[:, model + FF : model + 2 * FF]
+        down = share(hidden, feed_grad)
+        normed_two = late_mine[:, :model]
+        gate, up = [
+            share(
+                normed_two,
+                joined(late_mine[:, at : at + half_ff], late_theirs[:, at : at + half_ff]),
+            )
+            for at in (model, model + half_ff)
+        ]
+        out = share(early_mine[:, :width], branch)
+        attn = share(early_mine[:, width : width + q_cols], branch)
+        summed = [lax.psum(value, AXES) for value in small + (grad_ff_gain,)]
+        raw_part = mine(summed[0]).T
+        totals = [mine(summed[1])[0], mine(summed[2])]
+        totals += [mine(summed[at])[0] for at in (3, 4, 8)]
+        totals += [value[0] for value in summed[5:8]]
         at = width + channels
         projection = joined(mixed[:, :at], raw_part)
         query = mixed[:, at : at + q_cols]
@@ -1179,20 +1347,20 @@
     return (
         result,
         tokens_grad,
-        mine(totals[0]),
+        totals[0],
         projection,
-        mine(totals[1]),
-        mine(totals[2]),
+        totals[1],
+        totals[2],
         totals[5],
         totals[6],
         totals[7],
-        mine(totals[3]),
+        totals[3],
         out,
         query,
         key,
         value,
         attn,
-        mine(totals[8]),
+        totals[4],
         gate,
         up,
         down,

time: 424 us -> 359 us (0.85)
  waiting for transfers between devices: 182 us -> 155 us
  starting transfers between devices: 69.5 us -> 44.4 us
  other arithmetic: 17.2 us -> 8.17 us
  local copies, waits for them, and re-layouts: 48.1 us -> 40.6 us
    ppermute x81 -> x57, waiting for transfers between devices: 181 us -> 155 us  [send(): return lax.ppermute(value, AXES, self.tables[axis])]
    ppermute x81 -> x57, starting transfers between devices: 69.4 us -> 44.4 us  [send(): return lax.ppermute(value, AXES, self.tables[axis])]
    unnamed x263 -> x185, local copies, waits for them, and re-layouts: 32 us -> 31.8 us
  transfers between devices with their start and end apart: 82 -> 58, of which waited for: 31 -> 26; matrix products, arithmetic and copies ran while one was open for 9% -> 7% of each run, Pallas kernels for 18% -> 22%
where the time goes in v3:
time: 359 us; the launch traced here: 352 us
  waiting for transfers between devices  155 us (43%)
  Pallas kernels  78.2 us (22%)
  starting transfers between devices  44.4 us (12%)
  local copies, waits for them, and re-layouts  40.6 us (11%)
  between operations  16.1 us (4%)
  matrix products  9.72 us (3%)
  other arithmetic  8.17 us (2%)
    ppermute x57, waiting for transfers between devices, send(): return lax.ppermute(value, AXES, self.tables[axis])  155 us
    ppermute x57, starting transfers between devices, send(): return lax.ppermute(value, AXES, self.tables[axis])  44.4 us
    pallas_call x12, Pallas kernels, call_whole(): pl.pallas_call(ordered, out_shape=outs, in_specs=[pl.BlockSpec(memory_spa...  41.2 us
    unnamed x185, local copies, waits for them, and re-layouts  31.8 us
    pallas_call x11, Pallas kernels, place(): pl.pallas_call(body, out_shape=jax.ShapeDtypeStruct(tuple(shape), pieces[...  21.2 us
    pallas_call x1, Pallas kernels, middle(): pl.pallas_call(body, out_shape=outs, in_specs=[pl.BlockSpec(memory_space=...  15.7 us
  transfers between devices with their start and end apart: 58, of which 26 were waited for; matrix products, arithmetic and copies ran while one was open for 7% of the time, Pallas kernels for 22%

profile of v3, /device:TPU:0, one launch (start us, length us, event | category | flops | bytes accessed | tf_op | source)
XLA Modules:
  0.0 351.7 jit_solution(87688961103020959)
XLA Ops:
  14.9 3.1 collective-permute-start.15
  28.5 7.1 %collective-permute-done.10.refs_2_ = bf16[1,1,1,1,32,1792]{5,4,3,2,1,0:T(8,128)(2,1)S(1)} collective-permute-done((bf16[1,1,1,1,32,1792]{5,4,3,2,1,0:T(8,128)(2,1)S(1)}, bf16[1,1,1,1,32,1792]{5,4,3,2,1,0:T(8,128)(2,1)S(1)}, u32[]{:S(2)}, u32[]{:S(2)}) %collective-permute-start.10) | collective-permute-done | bytes 114720 | tf_op jit(solution)/shard_map/ppermute | solution.py:988
  37.4 7.5 %collective-permute-done.11.refs_3_ = bf16[1,1,1,1,32,1792]{5,4,3,2,1,0:T(8,128)(2,1)S(1)} collective-permute-done((bf16[1,1,1,1,32,1792]{5,4,3,2,1,0:T(8,128)(2,1)S(1)}, bf16[1,1,1,1,32,1792]{5,4,3,2,1,0:T(8,128)(2,1)S(1)}, u32[]{:S(2)}, u32[]{:S(2)}) %collective-permute-start.11) | collective-permute-done | bytes 114720 | tf_op jit(solution)/shard_map/ppermute | solution.py:988
  48.5 6.3 %collective-permute-done.17.refs_3_ = bf16[1,1,1,1,32,1536]{5,4,3,2,1,0:T(8,128)(2,1)S(1)} collective-permute-done((bf16[1,1,1,1,32,1536]{5,4,3,2,1,0:T(8,128)(2,1)S(1)}, bf16[1,1,1,1,32,1536]{5,4,3,2,1,0:T(8,128)(2,1)S(1)}, u32[]{:S(2)}, u32[]{:S(2)}) %collective-permute-start.17) | collective-permute-done | bytes 98336 | tf_op jit(solution)/shard_map/ppermute | solution.py:988
  60.1 12.4 %collective-permute-done.18.refs_1_ = bf16[4,1,1,1,32,1536]{5,4,3,2,1,0:T(8,128)(2,1)S(1)} collective-permute-done((bf16[4,1,1,1,32,1536]{5,4,3,2,1,0:T(8,128)(2,1)S(1)}, bf16[4,1,1,1,32,1536]{5,4,3,2,1,0:T(8,128)(2,1)S(1)}, u32[]{:S(2)}, u32[]{:S(2)}) %collective-permute-start.18) | collective-permute-done | bytes 393248 | tf_op jit(solution)/shard_map/ppermute | solution.py:988
  76.1 5.5 %collective-permute-done.2 = bf16[2,48,128]{2,1,0:T(8,128)(2,1)S(1)} collective-permute-done((bf16[2,48,128]{2,1,0:T(8,128)(2,1)S(1)}, bf16[2,48,128]{2,1,0:T(8,128)(2,1)S(1)}, u32[]{:S(2)}, u32[]{:S(2)}) %collective-permute-start.2) | collective-permute-done | bytes 24608 | tf_op jit(solution)/shard_map/ppermute | solution.py:988
  83.5 4.3 %collective-permute-done.3 = bf16[2,48,128]{2,1,0:T(8,128)(2,1)S(1)} collective-permute-done((bf16[2,48,128]{2,1,0:T(8,128)(2,1)S(1)}, bf16[2,48,128]{2,1,0:T(8,128)(2,1)S(1)}, u32[]{:S(2)}, u32[]{:S(2)}) %collective-permute-start.3) | collective-permute-done | bytes 24608 | tf_op jit(solution)/shard_map/ppermute | solution.py:988
  93.9 5.1 %collective-permute-done.5.refs_1_ = bf16[1,2,2,1,32,768]{5,4,3,2,1,0:T(8,128)(2,1)S(1)} collective-permute-done((bf16[1,2,2,1,32,768]{5,4,3,2,1,0:T(8,128)(2,1)S(1)}, bf16[1,2,2,1,32,768]{5,4,3,2,1,0:T(8,128)(2,1)S(1)}, u32[]{:S(2)}, u32[]{:S(2)}) %collective-permute-start.5) | collective-permute-done | bytes 196640 | tf_op jit(solution)/shard_map/ppermute | solution.py:988
  99.0 3.3 place.16.refs_0_
  102.4 8.7 %collective-permute-done.6.refs_2_ = bf16[1,2,2,1,32,768]{5,4,3,2,1,0:T(8,128)(2,1)S(1)} collective-permute-done((bf16[1,2,2,1,32,768]{5,4,3,2,1,0:T(8,128)(2,1)S(1)}, bf16[1,2,2,1,32,768]{5,4,3,2,1,0:T(8,128)(2,1)S(1)}, u32[]{:S(2)}, u32[]{:S(2)}) %collective-permute-start.6) | collective-permute-done | bytes 196640 | tf_op jit(solution)/shard_map/ppermute | solution.py:988
  111.1 14.4 %collective-permute-done.7.refs_3_ = bf16[1,2,2,1,32,768]{5,4,3,2,1,0:T(8,128)(2,1)S(1)} collective-permute-done((bf16[1,2,2,1,32,768]{5,4,3,2,1,0:T(8,128)(2,1)S(1)}, bf16[1,2,2,1,32,768]{5,4,3,2,1,0:T(8,128)(2,1)S(1)}, u32[]{:S(2)}, u32[]{:S(2)}) %collective-permute-start.7) | collective-permute-done | bytes 196640 | tf_op jit(solution)/shard_map/ppermute | solution.py:988
  144.7 5.4 %mixer_front.1 = (bf16[128,1792]{1,0:T(8,128)(2,1)S(1)}, f32[128,1536]{1,0:T(8,128)S(1)}, bf16[128,3584]{1,0:T(8,128)(2,1)S(1)}, bf16[128,3584]{1,0:T(8,128)(2,1)}) custom-call(s32[1]{0:T(128)} %bitcast.refs_0_.side_ref, bf16[128,512]{1,0:T(8,128)(2,1)S(1)} %get-tuple-element.65.refs_1_, bf16[128,1024]{1,0:T(8,128)(2,1)S(1)} %fusion.7.refs_2_, ...), custom_call_target="tpu_custom_call" | custom-call | flops 805306368 | bytes 5567684 | tf_op jit(solution)/shard_map/mixer_front/pallas_call | solution.py:94
  155.4 15.7 %middle.1 = (bf16[128,1024]{1,0:T(8,128)(2,1)}, bf16[128,5632]{1,0:T(8,128)(2,1)}, bf16[128,5632]{1,0:T(8,128)(2,1)}, f32[128,1024]{1,0:T(8,128)S(1)}, f32[1,102...) custom-call(s32[1]{0:T(128)} %bitcast.refs_0_.side_ref, bf16[32,256,1024]{2,1,0:T(8,128)(2,1)} %bitcast.201, ...), custom_call_target="tpu_custom_call" | custom-call | flops 4294967296 | bytes 16777216 | tf_op jit(solution)/shard_map/middle/pallas_call | solution.py:672
  179.5 3.9 %attention_back.1.refs_1_ = bf16[128,768]{1,0:T(8,128)(2,1)S(1)} custom-call(bf16[128,768]{1,0:T(8,128)(2,1)S(1)} %copy-done.55, bf16[128,512]{1,0:T(8,128)(2,1)S(1)} %copy-done.57, f32[128,128]{1,0:T(8,128)S(1)} %copy-done.28, f32[128,128]{1,0:T(8,128)S(1)} %copy-done.30, f32[128,128]{1,0:T(8,128)S(1)} %copy-done.26), custom_call_target="tpu_custom_call" | custom-call | flops 234881024 | bytes 720896 | tf_op jit(solution)/shard_map/attention_back/pallas_call | solution.py:94
  194.2 11.4 %mixer_back.1 = (bf16[128,1536]{1,0:T(8,128)(2,1)S(1)}, bf16[128,1792]{1,0:T(8,128)(2,1)S(1)}, bf16[128,24]{1,0:T(8,128)(2,1)S(1)}, bf16[128,2048]{1,0:T(8,128)(...) custom-call(s32[1]{0:T(128)} %bitcast.refs_0_.side_ref, ...), custom_call_target="tpu_custom_call" | custom-call | flops 1207959552 | bytes 6015364 | tf_op jit(solution)/shard_map/mixer_back/pallas_call | solution.py:94
  212.4 7.6 %collective-permute-done.30.refs_6_ = bf16[128,2048]{1,0:T(8,128)(2,1)} collective-permute-done((bf16[128,2048]{1,0:T(8,128)(2,1)}, bf16[128,2048]{1,0:T(8,128)(2,1)}, u32[]{:S(2)}, u32[]{:S(2)}) %collective-permute-start.30) | collective-permute-done | bytes 524320 | tf_op jit(solution)/shard_map/ppermute | solution.py:988
  223.8 3.2 outer.3
  229.7 4.9 %collective-permute-done.22 = f32[8,48,128]{2,1,0:T(8,128)S(1)} collective-permute-done((f32[8,48,128]{2,1,0:T(8,128)S(1)}, f32[8,48,128]{2,1,0:T(8,128)S(1)}, u32[]{:S(2)}, u32[]{:S(2)}) %collective-permute-start.22) | collective-permute-done | bytes 196640 | tf_op jit(solution)/shard_map/ppermute | solution.py:988
  236.0 4.2 %outer.4 = bf16[4,2,512,256]{3,2,1,0:T(8,128)(2,1)S(1)} custom-call(s32[2]{0:T(128)S(1)} %copy-done.46, bf16[128,3584]{1,0:T(8,128)(2,1)S(1)} %copy-done.4, bf16[128,3584]{1,0:T(8,128)(2,1)} %collective-permute-done.27.refs_2_, bf16[128,3584]{1,0:T(8,128)(2,1)} %collective-permute-done.28.refs_3_, bf16[128,3584]{1,0:T(8,128)(2,1)} %collective-permute-done.29.refs_4_, ...), custom_call_target="tpu_custom_call" | custom-call | flops 1073741824 | bytes 11534344 | tf_op jit(solution)/shard_map/outer/pallas_call | solution.py:94
  240.2 3.2 collective-permute-start.43
  243.4 3.1 outer.5
  247.3 7.9 %collective-permute-done.23 = f32[4,48,128]{2,1,0:T(8,128)S(1)} collective-permute-done((f32[4,48,128]{2,1,0:T(8,128)S(1)}, f32[4,48,128]{2,1,0:T(8,128)S(1)}, u32[]{:S(2)}, u32[]{:S(2)}) %collective-permute-start.23) | collective-permute-done | bytes 98336 | tf_op jit(solution)/shard_map/ppermute | solution.py:988
  255.2 3.2 collective-permute-start.24
  263.1 13.7 %collective-permute-done.50 = bf16[4,128,1024]{2,1,0:T(8,128)(2,1)S(1)} collective-permute-done((bf16[4,128,1024]{2,1,0:T(8,128)(2,1)S(1)}, bf16[4,128,1024]{2,1,0:T(8,128)(2,1)S(1)}, u32[]{:S(2)}, u32[]{:S(2)}) %collective-permute-start.50) | collective-permute-done | bytes 1048608 | tf_op jit(solution)/shard_map/ppermute | solution.py:988
  276.9 3.2 collective-permute-start.51
  284.1 5.7 %collective-permute-done.51 = bf16[128,1024]{1,0:T(8,128)(2,1)S(1)} collective-permute-done((bf16[128,1024]{1,0:T(8,128)(2,1)S(1)}, bf16[128,1024]{1,0:T(8,128)(2,1)S(1)}, u32[]{:S(2)}, u32[]{:S(2)}) %collective-permute-start.51) | collective-permute-done | bytes 262176 | tf_op jit(solution)/shard_map/ppermute | solution.py:988
  290.0 5.4 %collective-permute-done.35 = bf16[128,1024]{1,0:T(8,128)(2,1)S(1)} collective-permute-done((bf16[128,1024]{1,0:T(8,128)(2,1)S(1)}, bf16[128,1024]{1,0:T(8,128)(2,1)S(1)}, u32[]{:S(2)}, u32[]{:S(2)}) %collective-permute-start.35) | collective-permute-done | bytes 262176 | tf_op jit(solution)/shard_map/ppermute | solution.py:988
  295.6 16.7 %collective-permute-done.52 = bf16[128,1024]{1,0:T(8,128)(2,1)S(1)} collective-permute-done((bf16[128,1024]{1,0:T(8,128)(2,1)S(1)}, bf16[128,1024]{1,0:T(8,128)(2,1)S(1)}, u32[]{:S(2)}, u32[]{:S(2)}) %collective-permute-start.52) | collective-permute-done | bytes 262176 | tf_op jit(solution)/shard_map/ppermute | solution.py:988
  313.0 4.9 %collective-permute-done.36 = bf16[128,1024]{1,0:T(8,128)(2,1)S(1)} collective-permute-done((bf16[128,1024]{1,0:T(8,128)(2,1)S(1)}, bf16[128,1024]{1,0:T(8,128)(2,1)S(1)}, u32[]{:S(2)}, u32[]{:S(2)}) %collective-permute-start.36) | collective-permute-done | bytes 262176 | tf_op jit(solution)/shard_map/ppermute | solution.py:988
  318.4 3.7 %collective-permute-done.53 = bf16[128,1024]{1,0:T(8,128)(2,1)S(1)} collective-permute-done((bf16[128,1024]{1,0:T(8,128)(2,1)S(1)}, bf16[128,1024]{1,0:T(8,128)(2,1)S(1)}, u32[]{:S(2)}, u32[]{:S(2)}) %collective-permute-start.53) | collective-permute-done | bytes 262176 | tf_op jit(solution)/shard_map/ppermute | solution.py:988
  324.4 5.6 %collective-permute-done.26 = f32[48,128]{1,0:T(8,128)S(1)} collective-permute-done((f32[48,128]{1,0:T(8,128)S(1)}, f32[48,128]{1,0:T(8,128)S(1)}, u32[]{:S(2)}, u32[]{:S(2)}) %collective-permute-start.26) | collective-permute-done | bytes 24608 | tf_op jit(solution)/shard_map/ppermute | solution.py:988
  331.5 4.2 %collective-permute-done.48.refs_3_ = bf16[512,256]{1,0:T(8,128)(2,1)S(1)} collective-permute-done((bf16[512,256]{1,0:T(8,128)(2,1)S(1)}, bf16[512,256]{1,0:T(8,128)(2,1)S(1)}, u32[]{:S(2)}, u32[]{:S(2)}) %collective-permute-start.48) | collective-permute-done | bytes 262176 | tf_op jit(solution)/shard_map/ppermute | solution.py:988
  (407 shorter events, 121.2 us)
Async XLA Ops:
  7.2 146.4 %all-gather.3.cloned.1.call-start = ((), (), s32[]{:S(2)}) async-start(), calls=%async_computation | async-start | bytes 17301504 | tf_op jit(solution)/shard_map/all_gather | solution.py:1159
  14.9 20.8 %collective-permute-start.15 = (bf16[1,1,1,1,32,1536]{5,4,3,2,1,0:T(8,128)(2,1)S(1)}, bf16[1,1,1,1,32,1536]{5,4,3,2,1,0:T(8,128)(2,1)S(1)}, u32[]{:S(2)}, u32[]{:S(2)}) collective-permute-start(bf16[1,1,1,1,32,1536]{5,4,3,2,1,0:T(8,128)(2,1)S(1)} %constant_dynamic-slice_fusion.refs_0_), channel_id=1, source_target_pairs={{0,8},{1,9},{2,10},{3,11},{4,12},{5,13},{6,14},{7,15},{8,16},{9,17... | collective-permute-start | bytes 294920 | tf_op jit(solution)/shard_map/ppermute | solution.py:988
  18.3 39.9 %collective-permute-start = (bf16[48,128]{1,0:T(8,128)(2,1)S(1)}, bf16[48,128]{1,0:T(8,128)(2,1)S(1)}, u32[]{:S(2)}, u32[]{:S(2)}) collective-permute-start(bf16[48,128]{1,0:T(8,128)(2,1)S(1)} %pad.14), channel_id=1, source_target_pairs={{0,4},{1,5},{2,6},{3,7},{4,0},{5,1},{6,2},{7,3},{8,12},{9,13},{10,... | collective-permute-start | bytes 36872 | tf_op jit(solution)/shard_map/ppermute | solution.py:988
  22.4 65.4 %collective-permute-start.4 = (bf16[1,1,2,1,32,768]{5,4,3,2,1,0:T(8,128)(2,1)}, bf16[1,1,2,1,32,768]{5,4,3,2,1,0:T(8,128)(2,1)}, u32[]{:S(2)}, u32[]{:S(2)}) collective-permute-start(bf16[1,1,2,1,32,768]{5,4,3,2,1,0:T(8,128)(2,1)} %constant_dynamic-slice_fusion.2.refs_0_), channel_id=1, source_target_pairs={{0,4},{1,5},{2,6},{3,7},{4,0},{5,1},{6,2},{7,3},{8,12},{9,13},{10,... | collective-permute-start | bytes 294920 | tf_op jit(solution)/shard_map/ppermute | solution.py:988
  35.7 12.7 %collective-permute-start.16 = (bf16[1,1,1,1,32,1536]{5,4,3,2,1,0:T(8,128)(2,1)S(1)}, bf16[1,1,1,1,32,1536]{5,4,3,2,1,0:T(8,128)(2,1)S(1)}, u32[]{:S(2)}, u32[]{:S(2)}) collective-permute-start(bf16[1,1,1,1,32,1536]{5,4,3,2,1,0:T(8,128)(2,1)S(1)} %collective-permute-done.15.refs_1_), channel_id=1, source_target_pairs={{0,8},{1,9},{2,10},{3,11},{4,12},{5,13},{6,14},{7,15},{8,16},{9,17... | collective-permute-start | bytes 294920 | tf_op jit(solution)/shard_map/ppermute | solution.py:988
  56.5 16.0 %collective-permute-start.18 = (bf16[4,1,1,1,32,1536]{5,4,3,2,1,0:T(8,128)(2,1)S(1)}, bf16[4,1,1,1,32,1536]{5,4,3,2,1,0:T(8,128)(2,1)S(1)}, u32[]{:S(2)}, u32[]{:S(2)}) collective-permute-start(bf16[4,1,1,1,32,1536]{5,4,3,2,1,0:T(8,128)(2,1)S(1)} %place.18.refs_0_), channel_id=1, source_target_pairs={{0,2},{1,3},{2,0},{3,1},{4,6},{5,7},{6,4},{7,5},{8,10},{9,11},{10,... | collective-permute-start | bytes 1179656 | tf_op jit(solution)/shard_map/ppermute | solution.py:988
  59.5 39.6 %collective-permute-start.13 = (bf16[4,2,1,1,32,1792]{5,4,3,2,1,0:T(8,128)(2,1)S(1)}, bf16[4,2,1,1,32,1792]{5,4,3,2,1,0:T(8,128)(2,1)}, u32[]{:S(2)}, u32[]{:S(2)}) collective-permute-start(bf16[4,2,1,1,32,1792]{5,4,3,2,1,0:T(8,128)(2,1)S(1)} %place.15.refs_0_), channel_id=1, source_target_pairs={{0,2},{1,3},{2,0},{3,1},{4,6},{5,7},{6,4},{7,5},{8,10},{9,11},{10,... | collective-permute-start | bytes 2752520 | tf_op jit(solution)/shard_map/ppermute | solution.py:988
  60.0 15.6 %collective-permute-start.1 = (bf16[2,48,128]{2,1,0:T(8,128)(2,1)S(1)}, bf16[2,48,128]{2,1,0:T(8,128)(2,1)S(1)}, u32[]{:S(2)}, u32[]{:S(2)}) collective-permute-start(bf16[2,48,128]{2,1,0:T(8,128)(2,1)S(1)} %get-tuple-element.242), channel_id=1, source_target_pairs={{0,8},{1,9},{2,10},{3,11},{4,12},{5,13},{6,14},{7,15},{8,16},{9,17... | collective-permute-start | bytes 73736 | tf_op jit(solution)/shard_map/ppermute | solution.py:988
  73.6 16.0 %collective-permute-start.19 = (bf16[4,1,2,1,32,1536]{5,4,3,2,1,0:T(8,128)(2,1)S(1)}, bf16[4,1,2,1,32,1536]{5,4,3,2,1,0:T(8,128)(2,1)S(1)}, u32[]{:S(2)}, u32[]{:S(2)}) collective-permute-start(bf16[4,1,2,1,32,1536]{5,4,3,2,1,0:T(8,128)(2,1)S(1)} %place.19.refs_0_), channel_id=1, source_target_pairs={{0,4},{1,5},{2,6},{3,7},{4,0},{5,1},{6,2},{7,3},{8,12},{9,13},{10,... | collective-permute-start | bytes 2359304 | tf_op jit(solution)/shard_map/ppermute | solution.py:988
  93.8 43.2 %collective-permute-start.20 = (bf16[4,2,2,1,32,1536]{5,4,3,2,1,0:T(8,128)(2,1)S(1)}, bf16[4,2,2,1,32,1536]{5,4,3,2,1,0:T(8,128)(2,1)}, u32[]{:S(2)}, u32[]{:S(2)}) collective-permute-start(bf16[4,2,2,1,32,1536]{5,4,3,2,1,0:T(8,128)(2,1)S(1)} %place.20.refs_0_), channel_id=1, source_target_pairs={{0,1},{1,0},{2,3},{3,2},{4,5},{5,4},{6,7},{7,6},{8,9},{9,8},{10,11... | collective-permute-start | bytes 4718600 | tf_op jit(solution)/shard_map/ppermute | solution.py:988
  102.3 37.5 %collective-permute-start.14 = (bf16[4,2,2,1,32,1792]{5,4,3,2,1,0:T(8,128)(2,1)}, bf16[4,2,2,1,32,1792]{5,4,3,2,1,0:T(8,128)(2,1)}, u32[]{:S(2)}, u32[]{:S(2)}) collective-permute-start(bf16[4,2,2,1,32,1792]{5,4,3,2,1,0:T(8,128)(2,1)} %place.16.refs_0_), channel_id=1, source_target_pairs={{0,1},{1,0},{2,3},{3,2},{4,5},{5,4},{6,7},{7,6},{8,9},{9,8},{10,11... | collective-permute-start | bytes 5505032 | tf_op jit(solution)/shard_map/ppermute | solution.py:988
  111.1 14.4 %collective-permute-start.7 = (bf16[1,2,2,1,32,768]{5,4,3,2,1,0:T(8,128)(2,1)S(1)}, bf16[1,2,2,1,32,768]{5,4,3,2,1,0:T(8,128)(2,1)S(1)}, u32[]{:S(2)}, u32[]{:S(2)}) collective-permute-start(bf16[1,2,2,1,32,768]{5,4,3,2,1,0:T(8,128)(2,1)S(1)} %collective-permute-done.6.refs_2_), channel_id=1, source_target_pairs={{0,8},{1,9},{2,10},{3,11},{4,12},{5,13},{6,14},{7,15},{8,16},{9,17... | collective-permute-start | bytes 589832 | tf_op jit(solution)/shard_map/ppermute | solution.py:988
  152.8 22.7 %collective-permute-start.27 = (bf16[128,3584]{1,0:T(8,128)(2,1)}, bf16[128,3584]{1,0:T(8,128)(2,1)}, u32[]{:S(2)}, u32[]{:S(2)}) collective-permute-start(bf16[128,3584]{1,0:T(8,128)(2,1)} %get-tuple-element.85), channel_id=1, source_target_pairs={{0,2},{1,3},{2,0},{3,1},{4,6},{5,7},{6,4},{7,5},{8,10},{9,11},{10,... | collective-permute-start | bytes 2752520 | tf_op jit(solution)/shard_map/ppermute | solution.py:988
  173.2 37.5 %collective-permute-start.40 = (bf16[128,5632]{1,0:T(8,128)(2,1)}, bf16[128,5632]{1,0:T(8,128)(2,1)}, u32[]{:S(2)}, u32[]{:S(2)}) collective-permute-start(bf16[128,5632]{1,0:T(8,128)(2,1)} %get-tuple-element.99), channel_id=1, source_target_pairs={{0,2},{1,3},{2,0},{3,1},{4,6},{5,7},{6,4},{7,5},{8,10},{9,11},{10,... | collective-permute-start | bytes 4325384 | tf_op jit(solution)/shard_map/ppermute | solution.py:988
  175.1 36.7 %collective-permute-start.28 = (bf16[128,3584]{1,0:T(8,128)(2,1)}, bf16[128,3584]{1,0:T(8,128)(2,1)}, u32[]{:S(2)}, u32[]{:S(2)}) collective-permute-start(bf16[128,3584]{1,0:T(8,128)(2,1)} %copy-done.3), channel_id=1, source_target_pairs={{0,1},{1,0},{2,3},{3,2},{4,5},{5,4},{6,7},{7,6},{8,9},{9,8},{10,11... | collective-permute-start | bytes 2752520 | tf_op jit(solution)/shard_map/ppermute | solution.py:988
  175.5 47.8 %collective-permute-start.29 = (bf16[128,3584]{1,0:T(8,128)(2,1)}, bf16[128,3584]{1,0:T(8,128)(2,1)}, u32[]{:S(2)}, u32[]{:S(2)}) collective-permute-start(bf16[128,3584]{1,0:T(8,128)(2,1)} %collective-permute-done.27.refs_2_), channel_id=1, source_target_pairs={{0,1},{1,0},{2,3},{3,2},{4,5},{5,4},{6,7},{7,6},{8,9},{9,8},{10,11... | collective-permute-start | bytes 2752520 | tf_op jit(solution)/shard_map/ppermute | solution.py:988
  175.6 60.3 %collective-permute-start.41 = (bf16[128,5632]{1,0:T(8,128)(2,1)}, bf16[128,5632]{1,0:T(8,128)(2,1)}, u32[]{:S(2)}, u32[]{:S(2)}) collective-permute-start(bf16[128,5632]{1,0:T(8,128)(2,1)} %get-tuple-element.98.refs_5_.refs_1_), channel_id=1, source_target_pairs={{0,1},{1,0},{2,3},{3,2},{4,5},{5,4},{6,7},{7,6},{8,9},{9,8},{10,11... | collective-permute-start | bytes 4325384 | tf_op jit(solution)/shard_map/ppermute | solution.py:988
  205.6 14.4 %collective-permute-start.30 = (bf16[128,2048]{1,0:T(8,128)(2,1)}, bf16[128,2048]{1,0:T(8,128)(2,1)}, u32[]{:S(2)}, u32[]{:S(2)}) collective-permute-start(bf16[128,2048]{1,0:T(8,128)(2,1)} %get-tuple-element.87), channel_id=1, source_target_pairs={{0,2},{1,3},{2,0},{3,1},{4,6},{5,7},{6,4},{7,5},{8,10},{9,11},{10,... | collective-permute-start | bytes 1572872 | tf_op jit(solution)/shard_map/ppermute | solution.py:988
  210.8 25.2 %collective-permute-start.42 = (bf16[128,5632]{1,0:T(8,128)(2,1)}, bf16[128,5632]{1,0:T(8,128)(2,1)S(1)}, u32[]{:S(2)}, u32[]{:S(2)}) collective-permute-start(bf16[128,5632]{1,0:T(8,128)(2,1)} %collective-permute-done.40.refs_6_.refs_2_), channel_id=1, source_target_pairs={{0,1},{1,0},{2,3},{3,2},{4,5},{5,4},{6,7},{7,6},{8,9},{9,8},{10,11... | collective-permute-start | bytes 4325384 | tf_op jit(solution)/shard_map/ppermute | solution.py:988
  227.0 31.4 %collective-permute-start.33 = (bf16[4,128,1024]{2,1,0:T(8,128)(2,1)S(1)}, bf16[4,128,1024]{2,1,0:T(8,128)(2,1)S(1)}, u32[]{:S(2)}, u32[]{:S(2)}) collective-permute-start(bf16[4,128,1024]{2,1,0:T(8,128)(2,1)S(1)} %get-tuple-element.89), channel_id=1, source_target_pairs={{0,4},{1,5},{2,6},{3,7},{4,0},{5,1},{6,2},{7,3},{8,12},{9,13},{10,... | collective-permute-start | bytes 3145736 | tf_op jit(solution)/shard_map/ppermute | solution.py:988
  234.6 20.6 %collective-permute-start.23 = (f32[4,48,128]{2,1,0:T(8,128)S(1)}, f32[4,48,128]{2,1,0:T(8,128)S(1)}, u32[]{:S(2)}, u32[]{:S(2)}) collective-permute-start(f32[4,48,128]{2,1,0:T(8,128)S(1)} %dynamic-slice_bitcast_fusion.2), channel_id=1, source_target_pairs={{0,4},{1,5},{2,6},{3,7},{4,0},{5,1},{6,2},{7,3},{8,12},{9,13},{10,... | collective-permute-start | bytes 294920 | tf_op jit(solution)/shard_map/ppermute | solution.py:988
  240.2 20.8 %collective-permute-start.43 = (bf16[2,512,256]{2,1,0:T(8,128)(2,1)S(1)}, bf16[2,512,256]{2,1,0:T(8,128)(2,1)S(1)}, u32[]{:S(2)}, u32[]{:S(2)}) collective-permute-start(bf16[2,512,256]{2,1,0:T(8,128)(2,1)S(1)} %dynamic-slice_bitcast_fusion), channel_id=1, source_target_pairs={{0,8},{1,9},{2,10},{3,11},{4,12},{5,13},{6,14},{7,15},{8,16},{9,17... | collective-permute-start | bytes 1572872 | tf_op jit(solution)/shard_map/ppermute | solution.py:988
  246.5 30.3 %collective-permute-start.50 = (bf16[4,128,1024]{2,1,0:T(8,128)(2,1)S(1)}, bf16[4,128,1024]{2,1,0:T(8,128)(2,1)S(1)}, u32[]{:S(2)}, u32[]{:S(2)}) collective-permute-start(bf16[4,128,1024]{2,1,0:T(8,128)(2,1)S(1)} %get-tuple-element.107), channel_id=1, source_target_pairs={{0,4},{1,5},{2,6},{3,7},{4,0},{5,1},{6,2},{7,3},{8,12},{9,13},{10,... | collective-permute-start | bytes 3145736 | tf_op jit(solution)/shard_map/ppermute | solution.py:988
  258.5 21.6 %collective-permute-start.34 = (bf16[128,1024]{1,0:T(8,128)(2,1)S(1)}, bf16[128,1024]{1,0:T(8,128)(2,1)S(1)}, u32[]{:S(2)}, u32[]{:S(2)}) collective-permute-start(bf16[128,1024]{1,0:T(8,128)(2,1)S(1)} %fusion.20), channel_id=1, source_target_pairs={{0,8},{1,9},{2,10},{3,11},{4,12},{5,13},{6,14},{7,15},{8,16},{9,17... | collective-permute-start | bytes 786440 | tf_op jit(solution)/shard_map/ppermute | solution.py:988
  261.2 21.6 %collective-permute-start.44 = (bf16[2,512,256]{2,1,0:T(8,128)(2,1)S(1)}, bf16[2,512,256]{2,1,0:T(8,128)(2,1)S(1)}, u32[]{:S(2)}, u32[]{:S(2)}) collective-permute-start(bf16[2,512,256]{2,1,0:T(8,128)(2,1)S(1)} %fusion.4), channel_id=1, source_target_pairs={{0,8},{1,9},{2,10},{3,11},{4,12},{5,13},{6,14},{7,15},{8,16},{9,17... | collective-permute-start | bytes 1572872 | tf_op jit(solution)/shard_map/ppermute | solution.py:988
  263.1 26.9 %collective-permute-start.25 = (f32[48,128]{1,0:T(8,128)S(1)}, f32[48,128]{1,0:T(8,128)S(1)}, u32[]{:S(2)}, u32[]{:S(2)}) collective-permute-start(f32[48,128]{1,0:T(8,128)S(1)} %pad_maximum_fusion.4), channel_id=1, source_target_pairs={{0,8},{1,9},{2,10},{3,11},{4,12},{5,13},{6,14},{7,15},{8,16},{9,17... | collective-permute-start | bytes 73736 | tf_op jit(solution)/shard_map/ppermute | solution.py:988
  276.9 12.9 %collective-permute-start.51 = (bf16[128,1024]{1,0:T(8,128)(2,1)S(1)}, bf16[128,1024]{1,0:T(8,128)(2,1)S(1)}, u32[]{:S(2)}, u32[]{:S(2)}) collective-permute-start(bf16[128,1024]{1,0:T(8,128)(2,1)S(1)} %fusion.21), channel_id=1, source_target_pairs={{0,8},{1,9},{2,10},{3,11},{4,12},{5,13},{6,14},{7,15},{8,16},{9,17... | collective-permute-start | bytes 786440 | tf_op jit(solution)/shard_map/ppermute | solution.py:988
  280.2 15.2 %collective-permute-start.35 = (bf16[128,1024]{1,0:T(8,128)(2,1)S(1)}, bf16[128,1024]{1,0:T(8,128)(2,1)S(1)}, u32[]{:S(2)}, u32[]{:S(2)}) collective-permute-start(bf16[128,1024]{1,0:T(8,128)(2,1)S(1)} %fusion.19), channel_id=1, source_target_pairs={{0,8},{1,9},{2,10},{3,11},{4,12},{5,13},{6,14},{7,15},{8,16},{9,17... | collective-permute-start | bytes 786440 | tf_op jit(solution)/shard_map/ppermute | solution.py:988
  282.9 29.6 %collective-permute-start.45 = (bf16[2,512,256]{2,1,0:T(8,128)(2,1)S(1)}, bf16[2,512,256]{2,1,0:T(8,128)(2,1)S(1)}, u32[]{:S(2)}, u32[]{:S(2)}) collective-permute-start(bf16[2,512,256]{2,1,0:T(8,128)(2,1)S(1)} %fusion.3), channel_id=1, source_target_pairs={{0,8},{1,9},{2,10},{3,11},{4,12},{5,13},{6,14},{7,15},{8,16},{9,17... | collective-permute-start | bytes 1572872 | tf_op jit(solution)/shard_map/ppermute | solution.py:988
  289.9 22.3 %collective-permute-start.52 = (bf16[128,1024]{1,0:T(8,128)(2,1)S(1)}, bf16[128,1024]{1,0:T(8,128)(2,1)S(1)}, u32[]{:S(2)}, u32[]{:S(2)}) collective-permute-start(bf16[128,1024]{1,0:T(8,128)(2,1)S(1)} %fusion.16), channel_id=1, source_target_pairs={{0,8},{1,9},{2,10},{3,11},{4,12},{5,13},{6,14},{7,15},{8,16},{9,17... | collective-permute-start | bytes 786440 | tf_op jit(solution)/shard_map/ppermute | solution.py:988
  295.5 22.3 %collective-permute-start.36 = (bf16[128,1024]{1,0:T(8,128)(2,1)S(1)}, bf16[128,1024]{1,0:T(8,128)(2,1)S(1)}, u32[]{:S(2)}, u32[]{:S(2)}) collective-permute-start(bf16[128,1024]{1,0:T(8,128)(2,1)S(1)} %fusion.18), channel_id=1, source_target_pairs={{0,8},{1,9},{2,10},{3,11},{4,12},{5,13},{6,14},{7,15},{8,16},{9,17... | collective-permute-start | bytes 786440 | tf_op jit(solution)/shard_map/ppermute | solution.py:988
  322.6 13.1 %collective-permute-start.48 = (bf16[512,256]{1,0:T(8,128)(2,1)S(1)}, bf16[512,256]{1,0:T(8,128)(2,1)S(1)}, u32[]{:S(2)}, u32[]{:S(2)}) collective-permute-start(bf16[512,256]{1,0:T(8,128)(2,1)S(1)} %fusion.13.refs_1_), channel_id=1, source_target_pairs={{0,2},{1,3},{2,0},{3,1},{4,6},{5,7},{6,4},{7,5},{8,10},{9,11},{10,... | collective-permute-start | bytes 786440 | tf_op jit(solution)/shard_map/ppermute | solution.py:988
  (116 other events, 871.0 us)
Sparse Core Ops, SparseCore 0:
  14.8 138.5 all-gather.2

commit v4 on v3

--- a/solution.py
+++ b/solution.py
@@ -83,9 +83,30 @@
     return jnp.where(half, first, second)
 
 
-def call_whole(body, outs, args, flops, scratch=(), name="kernel", after=()):
-    moved = sum(arg.size * arg.dtype.itemsize for arg in args)
-    moved += sum(out.size * out.dtype.itemsize for out in outs)
+MICROS = {
+    "attention_front": 2.9,
+    "attention_back": 3.8,
+    "mixer_front": 5.5,
+    "mixer_back": 11.5,
+    "outer": 3.2,
+    "finish": 2.3,
+    "pack_grads": 1.0,
+    "unpack_grads": 1.0,
+    "hold": 1.5,
+    "stack": 1.5,
+    "middle": 15.8,
+    "place": 2.3,
+    "cut_rows": 1.5,
+}
+
+
+def cost(name):
+    return pl.CostEstimate(
+        flops=int(MICROS[name] * 1.1e9), bytes_accessed=0, transcendentals=0
+    )
+
+
+def call_whole(body, outs, args, scratch=(), name="kernel", after=()):
     count = len(args)
 
     def ordered(*refs):
@@ -102,7 +123,7 @@
         out_specs=[pl.BlockSpec(memory_space=pltpu.VMEM)] * len(outs),
         scratch_shapes=list(scratch),
         compiler_params=pltpu.CompilerParams(vmem_limit_bytes=40 * 1024 * 1024),
-        cost_estimate=pl.CostEstimate(flops=flops, bytes_accessed=moved, transcendentals=0),
+        cost_estimate=cost(name),
         name=name,
     )(*args, *after)
 
@@ -140,25 +161,29 @@
     return raised / jnp.sum(raised, axis=-1, keepdims=True)
 
 
-def attention_front(qkv, cosine, sine, allowed):
-    extent = qkv.shape[0]
+def attention_front(first, second, cosine, sine, allowed):
+    extent = first.shape[0]
     pair = 2 * ATTENTION_HEAD
     pairs = QH // 2
-
-    def body(qkv_ref, cos_ref, sin_ref, allowed_ref, low_ref, out_ref):
+    at_key = first.shape[1] - 2 * pair
+    at_query = second.shape[1] - pairs * pair
+
+    def body(first_ref, second_ref, cos_ref, sin_ref, allowed_ref, low_ref, out_ref):
         half = lane_half(extent)
         can = allowed_ref[...] > 0.0
         cos_val, sin_val = cos_ref[...], sin_ref[...]
-        key = turned(qkv_ref[:, pairs * pair : (pairs + 1) * pair], cos_val, sin_val, False)
+        key = turned(first_ref[:, at_key : at_key + pair], cos_val, sin_val, False)
         key = key.astype(jnp.bfloat16)
-        value = qkv_ref[:, (pairs + 1) * pair :].astype(jnp.bfloat16)
+        value = first_ref[:, at_key + pair :].astype(jnp.bfloat16)
         low_ref[:, pairs * pair : (pairs + 1) * pair] = key
         low_ref[:, (pairs + 1) * pair :] = value
         keys = [k.astype(jnp.bfloat16) for k in doubled(key.astype(jnp.float32), half)]
         values = [v.astype(jnp.bfloat16) for v in doubled(value.astype(jnp.float32), half)]
         for number in range(pairs):
             spot = slice(number * pair, (number + 1) * pair)
-            query = turned(qkv_ref[:, spot], cos_val, sin_val, False).astype(jnp.bfloat16)
+            begin = at_query + number * pair
+            query = turned(second_ref[:, begin : begin + pair], cos_val, sin_val, False)
+            query = query.astype(jnp.bfloat16)
             low_ref[:, spot] = query
             group = number * KVH // pairs
             results = []
@@ -170,9 +195,11 @@
 
     return call_whole(
         body,
-        (shape(qkv.shape, jnp.bfloat16), shape((extent, pairs * pair), jnp.bfloat16)),
-        (qkv, cosine, sine, allowed),
-        QH * 8 * extent**3,
+        (
+            shape((extent, (pairs + 2) * pair), jnp.bfloat16),
+            shape((extent, pairs * pair), jnp.bfloat16),
+        ),
+        (first, second, cosine, sine, allowed),
         name="attention_front",
     )
 
@@ -223,7 +250,6 @@
         body,
         (shape(low.shape, jnp.bfloat16),),
         (low, heads_grad, cosine, sine, allowed),
-        QH * 14 * extent**3,
         name="attention_back",
     )
     return out
@@ -353,20 +379,14 @@
             shape((extent, at_feed + half_feed), jnp.bfloat16),
         ),
         (side, heads_out, normed, feed_grad, conv_in, raw_step, gate_z, taps, bias, shift, rate, skip, gain, moves, allowed),
-        MH * 16 * extent**3,
         name="mixer_front",
     )
 
 
-def mixed_columns(z_ref, low_ref, qkv_ref, at):
-    for ref in (z_ref, low_ref, qkv_ref):
-        if at < ref.shape[1]:
-            return ref[:, at : at + 256]
-        at -= ref.shape[1]
-
-
 def mixer_back(
+    after,
     side,
+    normed,
     qkv_low,
     gated_grad,
     scan,
@@ -390,6 +410,7 @@
 
     def body(
         side_ref,
+        normed_ref,
         qkv_ref,
         grad_ref,
         scan_ref,
@@ -408,6 +429,7 @@
         z_ref,
         low_ref,
         raw_low_ref,
+        raw_out,
         mine_ref,
         theirs_ref,
         gain_out,
@@ -492,7 +514,9 @@
         rate_out[...] = jnp.sum(decay_grad * step * step_rate, axis=0, keepdims=True)
         raw_grad = (step_grad + decay_grad * step_rate) * sigmoid(moved)
         shift_out[...] = jnp.sum(raw_grad, axis=0, keepdims=True)
-        raw_low_ref[...] = raw_grad.astype(jnp.bfloat16)
+        raw_low = raw_grad.astype(jnp.bfloat16)
+        raw_low_ref[...] = raw_low
+        raw_out[...] = matmul_left(raw_low, normed_ref[...])
         for at in range(0, channels, 256):
             spot = slice(at, at + 256)
             total = conv_sum(conv_ref, taps_ref, bias_ref, moves_ref, spot)
@@ -510,20 +534,22 @@
                 )
                 sums = sums + taps_ref[tap, spot] * pltpu.roll(kept, extent - offset, 0)
             low_ref[:, spot] = sums.astype(jnp.bfloat16)
+        q_cols = QH * ATTENTION_HEAD
+        z_ref[:, width:] = qkv_ref[:, :q_cols]
+        low_ref[:, channels:] = qkv_ref[:, q_cols:]
         first = side_ref[0] == 0
         for at in range(0, MIXED // 2, 256):
             spot = slice(at, at + 256)
-            near = mixed_columns(z_ref, low_ref, qkv_ref, at)
-            far = mixed_columns(z_ref, low_ref, qkv_ref, at + MIXED // 2)
-            mine_ref[:, spot] = jnp.where(first, near, far)
-            theirs_ref[:, spot] = jnp.where(first, far, near)
+            mine_ref[:, spot] = jnp.where(first, z_ref[:, spot], low_ref[:, spot])
+            theirs_ref[:, spot] = jnp.where(first, low_ref[:, spot], z_ref[:, spot])
 
     return call_whole(
         body,
         (
-            shape((extent, width), jnp.bfloat16),
-            shape((extent, channels), jnp.bfloat16),
+            shape((extent, MIXED // 2), jnp.bfloat16),
+            shape((extent, MIXED // 2), jnp.bfloat16),
             shape((extent, MH), jnp.bfloat16),
+            shape((MH, normed.shape[1])),
             shape((extent, MIXED // 2), jnp.bfloat16),
             shape((extent, MIXED // 2), jnp.bfloat16),
             shape((1, width)),
@@ -535,6 +561,7 @@
         ),
         (
             side,
+            normed,
             qkv_low,
             gated_grad,
             scan,
@@ -551,13 +578,13 @@
             moves,
             allowed,
         ),
-        MH * 24 * extent**3,
         scratch=(
             pltpu.VMEM((extent, width), jnp.bfloat16),
             pltpu.VMEM((extent, channels), jnp.float32),
             pltpu.VMEM((MH, extent), jnp.float32),
         ),
         name="mixer_back",
+        after=after,
     )
 
 
@@ -657,11 +684,10 @@
         heads_out[...] = matmul_right(branch, matrix(1)).astype(jnp.bfloat16)
 
     low = jnp.bfloat16
-    late = model + 2 * FF + model // 2
     outs = (
         shape((extent, model), low),
-        shape((extent, late), low),
-        shape((extent, late), low),
+        shape((extent, model + 2 * FF + model // 2), low),
+        shape((extent, model + 2 * FF + model // 2), low),
         shape((extent, model)),
         shape((1, model)),
         shape((extent, width)),
@@ -677,14 +703,13 @@
         scratch_shapes=[pltpu.VMEM((groups, count, BLOCK), low) for _, count in spans]
         + [pltpu.SemaphoreType.DMA((len(spans),))],
         compiler_params=pltpu.CompilerParams(vmem_limit_bytes=52 * 1024 * 1024),
-        cost_estimate=pl.CostEstimate(
-            flops=4 * extent * pack.size, bytes_accessed=2 * pack.size, transcendentals=0
-        ),
+        cost_estimate=cost("middle"),
         name="middle",
     )(*args)
 
 
-def outer(spots, terms, z_size, apart, after=()):
+def outer(spots, terms, z_size, apart, after=(), extra=None):
+    more = 16 if extra is not None else 0
     rows = [width // (2 * z_size) for _, _, width, _, _ in terms]
     columns = sum(size for _, size in terms[0][4])
     arrays = []
@@ -729,14 +754,89 @@
                     refs[-1][z, 0, at : at + size, :] = even
                     refs[-1][z, 1, at : at + size, :] = odd
             at += size
+        if extra is not None:
+            source = refs[len(arrays)]
+            blank = jnp.zeros((more, columns), jnp.bfloat16)
+            for z in range(z_size):
+                refs[-2][z, at : at + more, :] = blank
+                refs[-1][z, at : at + more, :] = blank
+                for row in range(extra.shape[2]):
+                    put = (z, slice(at + row // 8, at + row // 8 + 1), slice(row % 8 * 128, row % 8 * 128 + 128))
+                    even = source[z, 0, row : row + 1, :].astype(jnp.bfloat16)
+                    odd = source[z, 1, row : row + 1, :].astype(jnp.bfloat16)
+                    refs[-2][put] = jnp.where(first, even, odd)
+                    refs[-1][put] = jnp.where(first, odd, even)
 
     if apart:
-        outs = (shape((z_size, sum(rows), columns), jnp.bfloat16),) * 2
+        outs = (shape((z_size, sum(rows) + more, columns), jnp.bfloat16),) * 2
     else:
         outs = (shape((z_size, 2, sum(rows), columns), jnp.bfloat16),)
-    tokens = sum(value.shape[0] for value in terms[0][3])
-    flops = 4 * z_size * tokens * sum(rows) * columns
-    return call_whole(body, outs, (spots, *arrays), flops, name="outer", after=after)
+    return call_whole(
+        body,
+        outs,
+        (spots, *arrays) + (() if extra is None else (extra,)),
+        name="outer",
+        after=after,
+    )
+
+
+def stack(mine, other, after):
+    rows, columns = mine.shape
+
+    def body(mine_ref, other_ref, out):
+        out[:rows, :] = mine_ref[...]
+        out[rows:, :] = other_ref[...]
+
+    (out,) = call_whole(
+        body, (shape((2 * rows, columns), mine.dtype),), (mine, other), name="stack", after=after
+    )
+    return out
+
+
+def hold(value, after):
+    def body(value_ref, out):
+        out[...] = value_ref[...]
+
+    (out,) = call_whole(
+        body, (shape(value.shape, value.dtype),), (value,), name="hold", after=after
+    )
+    return out
+
+
+def cut_rows(turn, pieces, weights, groups):
+    sizes = []
+    moves = []
+    for number, (rows, columns, parts) in enumerate(groups):
+        sizes.append((rows, columns))
+        moves += [(number,) + part for part in parts]
+
+    def body(turn_ref, *refs):
+        outs, sems = refs[len(weights) : -1], refs[-1]
+        copies = []
+        for number, (group, index, column, columns, row, place_at) in enumerate(moves):
+            count = weights[index].shape[0] // pieces
+            begin = pl.multiple_of(turn_ref[0] * count, 16)
+            copy = pltpu.make_async_copy(
+                refs[index].at[pl.ds(begin, count), pl.ds(column, columns)],
+                outs[group].at[pl.ds(row, count), pl.ds(place_at, columns)],
+                sems.at[number],
+            )
+            copy.start()
+            copies.append(copy)
+        for copy in copies:
+            copy.wait()
+
+    return pl.pallas_call(
+        body,
+        out_shape=tuple(shape(size, jnp.bfloat16) for size in sizes),
+        in_specs=[pl.BlockSpec(memory_space=pltpu.SMEM)]
+        + [pl.BlockSpec(memory_space=pl.ANY)] * len(weights),
+        out_specs=[pl.BlockSpec(memory_space=pltpu.VMEM)] * len(sizes),
+        scratch_shapes=[pltpu.SemaphoreType.DMA((len(moves),))],
+        compiler_params=pltpu.CompilerParams(vmem_limit_bytes=24 * 1024 * 1024),
+        cost_estimate=cost("cut_rows"),
+        name="cut_rows",
+    )(turn, *weights)
 
 
 def pack_grads(raw, in_gain, taps, bias, ssm_gain, ff_gain, heads, parts):
@@ -766,7 +866,6 @@
         body,
         (shape((parts, 48, 128)),),
         (raw, in_gain, taps, bias, ssm_gain, ff_gain) + tuple(heads),
-        0,
         name="pack_grads",
     )
     return out
@@ -779,27 +878,34 @@
         z = spots_ref[0]
         head_refs, outs = refs[:count], refs[count:]
         total = jnp.zeros(heads[0].shape, jnp.float32)
+
+        def take(row, count, width):
+            parts = [
+                block_ref[at // 8 : at // 8 + 1, at % 8 * 128 : at % 8 * 128 + width]
+                for at in range(row, row + count)
+            ]
+            return jnp.concatenate(parts, axis=0).astype(jnp.float32)
+
         for at in range(count):
             step = lax.rem(z + (count - at), count)
             row = head_refs[0][...]
             for number in range(1, count):
                 row = jnp.where(step == number, head_refs[number][...], row)
-            total = total + row
-        outs[0][...] = block_ref[:MH, :].T
+            total = total + row.astype(jnp.float32)
+        outs[0][...] = take(0, MH, 128).T
         at = MH
         for out, (rows, size) in zip(outs[1:], sizes):
             for begin in range(0, size, 128):
                 width = min(128, size - begin)
-                out[:, begin : begin + width] = block_ref[at : at + rows, :width]
+                out[:, begin : begin + width] = take(at, rows, width)
                 at += rows
         for number, out in enumerate(outs[1 + len(sizes) :]):
-            out[...] = total[number : number + 1, :MH]
+            out[...] = total[:, number * 128 : number * 128 + MH]
 
     return call_whole(
         body,
         (shape((128, MH)),) + tuple(shape(size) for size in sizes) + (shape((1, MH)),) * 3,
         (spots, block) + tuple(heads),
-        0,
         name="unpack_grads",
     )
 
@@ -830,7 +936,7 @@
 
     args = (spots,) + tuple(pieces) + (() if extra is None else (extra,))
     return call_whole(
-        body, tuple(shape((rows, columns)) for rows, columns, _ in outs), args, 0, name="finish"
+        body, tuple(shape((rows, columns)) for rows, columns, _ in outs), args, name="finish"
     )
 
 
@@ -853,15 +959,14 @@
 
 def forward_pass(side, feed_grad, tokens_f, gains, mats, a_log, dt_bias, skip_d, segment, position):
     in_gain, conv_w, conv_b, ssm_gain, _, w_raw = gains
-    w_conv, w_z, w_qkv = mats
+    w_first, w_second = mats
     moves, allowed, cosine, sine = block_masks(segment, position)
     normed_f, pull_norm_one = jax.vjp(rms_scale, tokens_f, in_gain.astype(jnp.float32))
     normed = normed_f.astype(jnp.bfloat16)
-    qkv = matmul_plain(normed, w_qkv)
-    low, heads_out = attention_front(qkv, cosine, sine, allowed)
-    conv_in = matmul_plain(normed, w_conv)
+    conv_in = matmul_plain(normed, w_first)
+    gate_z = matmul_plain(normed, w_second)
     raw_step = matmul_right(normed, w_raw)
-    gate_z = matmul_plain(normed, w_z)
+    low, heads_out = attention_front(conv_in, gate_z, cosine, sine, allowed)
     mixer_args = (
         conv_in,
         raw_step,
@@ -882,8 +987,8 @@
     return (early_mine, early_theirs, kept)
 
 
-def backward_pass(side, grads, w_raw, mats, kept):
-    w_conv, w_z, w_qkv = mats
+def backward_pass(after, side, grads, w_raw, mats, kept):
+    w_first, w_second = mats
     pull_norm_one, normed, mixer_args, act, scan, low, turn_args = kept
     residual_grad, gated_grad, heads_grad = grads
     qkv_low = attention_back(low, heads_grad, *turn_args)
@@ -891,6 +996,7 @@
         z_low,
         conv_low,
         raw_low,
+        raw_rows,
         mixed_mine,
         mixed_theirs,
         grad_ssm_gain,
@@ -899,17 +1005,15 @@
         skip_lanes,
         grad_dt_bias,
         grad_a_log,
-    ) = mixer_back(side, qkv_low, gated_grad, scan, act, *mixer_args)
+    ) = mixer_back(after, side, normed, qkv_low, gated_grad, scan, act, *mixer_args)
     grad_skip = jnp.sum(skip_lanes.reshape(MH, HD), axis=1)
     normed_grad = (
-        matmul_right(qkv_low, w_qkv)
-        + matmul_right(z_low, w_z)
-        + matmul_right(conv_low, w_conv)
+        matmul_right(z_low, w_second)
+        + matmul_right(conv_low, w_first)
         + matmul_plain(raw_low, w_raw)
     )
     token_part, grad_in_gain = pull_norm_one(normed_grad)
     tokens_grad = (residual_grad + token_part).astype(jnp.bfloat16)
-    raw_rows = matmul_left(raw_low, normed)
     small = (
         raw_rows,
         grad_in_gain[None],
@@ -950,7 +1054,6 @@
         for store in stores:
             store.wait()
 
-    moved = 2 * sum(piece.size * piece.dtype.itemsize for piece in pieces)
     return pl.pallas_call(
         body,
         out_shape=jax.ShapeDtypeStruct(tuple(shape), pieces[0].dtype),
@@ -960,7 +1063,7 @@
         scratch_shapes=[pltpu.VMEM(piece.shape, piece.dtype) for piece in pieces]
         + [pltpu.SemaphoreType.DMA((2, total))],
         compiler_params=pltpu.CompilerParams(vmem_limit_bytes=24 * 1024 * 1024),
-        cost_estimate=pl.CostEstimate(flops=0, bytes_accessed=moved, transcendentals=0),
+        cost_estimate=cost("place"),
         name="place",
     )(jnp.stack(positions).astype(jnp.int32), *pieces)
 
@@ -997,15 +1100,12 @@
         spot = {"x": self.x, "y": self.y, "c": self.c}[axis]
         return place([value, self.send(value, axis)], [spot, 1 - spot], "zxyc".index(axis), 2)
 
-    def gather(self, own, order):
-        rows, columns = own.shape
-        cut = own.reshape(1, 1, 2, 2, rows // 4, columns)
-        cut = lax.dynamic_slice_in_dim(cut, self.c, 1, 3)
-        if "y" in order:
-            cut = lax.dynamic_slice_in_dim(cut, self.y, 1, 2)
+    def gather(self, value, order):
+        if value.ndim == 2:
+            value = value[None, None, None, None]
         for axis in order:
-            cut = self.spread(cut, axis)
-        return cut.reshape(-1, columns)
+            value = self.spread(value, axis)
+        return value
 
     def gather_small(self, own):
         other = self.send(own, "x")
@@ -1023,9 +1123,9 @@
             ]
         )
 
-    def near(self, mine, theirs):
-        values = [mine, self.send(theirs, "y")]
-        return values + [self.send(value, "c") for value in values]
+    def near(self, mine, theirs, after=()):
+        both = stack(mine, self.send(theirs, "y"), after)
+        return [both, self.send(both, "c")]
 
     def around(self, block):
         total = block(0).astype(jnp.bfloat16)
@@ -1038,36 +1138,43 @@
         at = (self.z + 2 * self.z_size - 1 - step) % self.z_size
         return lax.dynamic_index_in_dim(value, at, 0, False).astype(jnp.float32)
 
-    def reduce_small(self, value):
+    def add_small(self, value):
         value = value + self.send(value, "c")
         value = value + self.send(value, "y")
-        value = value.reshape(self.z_size, 2, 48, 128)
-        mine = lax.dynamic_index_in_dim(value, self.x, 1, False)
-        theirs = lax.dynamic_index_in_dim(value, 1 - self.x, 1, False)
-        value = mine + self.send(theirs, "x")
-        heads = [value[0, 40:]]
-        total = self.at_step(value, 0)
+        return value.reshape(self.z_size, 2, 48, 128)
+
+    def reduce_mixed(self, mine, theirs, after):
+        moved = self.send(theirs, "x")
+        total = (self.at_step(mine, 0) + self.at_step(moved, 0)).astype(jnp.bfloat16)
+        heads = [total[133:134]]
         for step in range(1, self.z_size):
             arrived = self.send(total, "z")
-            heads.append(arrived[40:])
-            total = jnp.concatenate([arrived[:40] + self.at_step(value, step)[:40], arrived[40:]])
-        return total, heads
-
-    def quarters(self, total):
+            heads.append(arrived[133:134])
+            block = self.at_step(mine, step) + self.at_step(moved, step)
+            row = lax.broadcasted_iota(jnp.int32, block.shape, 0)
+            block = jnp.where(row == 133, 0.0, block)
+            total = (arrived.astype(jnp.float32) + block).astype(jnp.bfloat16)
+        return moved, self.quarters(total[:128], after), total[128:], heads
+
+    def quarters(self, total, after=()):
         by_y = self.send(total, "y")
+        if after:
+            by_y = hold(by_y, after)
         return (total, self.send(total, "c"), by_y, self.send(by_y, "c"))
 
     def reduce_xz(self, mine, theirs):
         moved = self.send(theirs, "x")
-        return self.quarters(
+        return moved, self.quarters(
             self.around(lambda step: self.at_step(mine, step) + self.at_step(moved, step))
         )
 
-    def reduce_zx(self, value):
+
+    def reduce_zx(self, value, after):
         total = self.around(lambda step: self.at_step(value, step))
         mine = lax.dynamic_index_in_dim(total, self.x, 0, False)
         theirs = lax.dynamic_index_in_dim(total, 1 - self.x, 0, False)
         moved = self.send(theirs, "x")
+        mine = hold(mine, after)
         return self.quarters(
             (mine.astype(jnp.float32) + moved.astype(jnp.float32)).astype(jnp.bfloat16)
         )
@@ -1129,37 +1236,48 @@
     quick = parts == 8 and copies == 4
     links = Links(parts, copies)
     own_small = (in_gain, conv_w, conv_b, ssm_gain, ff_gain, w_in[:, width + channels :])
-    own = (
-        w_in[:, width : width + channels],
-        w_in[:, :width],
-        jnp.concatenate([w_query, w_key, w_value], axis=1),
-    )
-    blocks = (
-        w_out,
-        w_attn_out,
-        w_gate[:, :BLOCK],
-        w_gate[:, BLOCK:],
-        w_up[:, :BLOCK],
-        w_up[:, BLOCK:],
-        w_down,
-    )
     pieces = 4 if quick else 1
-    turn = links.y * 2 + links.c if quick else 0
-    cuts, spans, at = [], [], 0
-    for value in blocks:
-        count = value.shape[0] // pieces
-        cuts.append(lax.dynamic_slice_in_dim(value, turn * count, count, 0))
+    turn = jnp.stack([links.y * 2 + links.c if quick else jnp.int32(0)]).astype(jnp.int32)
+    weights = (w_in, w_query, w_key, w_value, w_out, w_attn_out, w_gate, w_up, w_down)
+    q_cols = QH * ATTENTION_HEAD
+    k_cols = KVH * ATTENTION_HEAD
+    spans, blocks, at = [], [], 0
+    for index, column in ((0, 0), (1, 0), (2, 0), (2, BLOCK), (3, 0), (3, BLOCK), (4, 0)):
+        count = weights[index + 4].shape[0] // pieces
+        blocks.append((index, column, BLOCK, at, 0))
         spans.append((at, count))
         at += count
-    pack = jnp.concatenate(cuts, axis=0)
+    (pack,) = cut_rows(turn, pieces, weights[4:], [(at, BLOCK, blocks)])
+    cut_in = w_in.shape[0] // pieces
+    first, second = cut_rows(
+        turn,
+        pieces,
+        weights[:4],
+        [
+            (
+                cut_in,
+                MIXED // 2,
+                [
+                    (0, width, channels, 0, 0),
+                    (2, 0, k_cols, 0, channels),
+                    (3, 0, k_cols, 0, channels + k_cols),
+                ],
+            ),
+            (cut_in, MIXED // 2, [(0, 0, width, 0, 0), (1, 0, q_cols, 0, width)]),
+        ],
+    )
     if quick:
-        orders = ("zxyc", "zyxc", "xzc")
         small_all = links.gather_small(pack_small(*own_small))
-        mats = tuple(links.gather(value, order) for value, order in zip(own, orders))
+        mats = tuple(
+            links.gather(value, order).reshape(-1, MIXED // 2)
+            for value, order in ((first, "zxyc"), (second, "zyxc"))
+        )
         pack = lax.all_gather(pack, AXES, axis=0)
     else:
         small_all = lax.all_gather(pack_small(*own_small), "shard", axis=0)
-        mats = tuple(lax.all_gather(value, "shard", axis=0, tiled=True) for value in own)
+        mats = tuple(
+            lax.all_gather(value, "shard", axis=0, tiled=True) for value in (first, second)
+        )
         pack = lax.all_gather(pack, "shard", axis=0)
     gains = unpack_small(small_all, own_small)
     segment, position = layout(seq_lengths[0], seq_starts[0], tokens.shape[0])
@@ -1189,45 +1307,48 @@
     ) = middle(
         side, pack, spans, tokens, early_mine, cotangent, valid, gains[4].astype(jnp.float32)[None]
     )
+    model = w_in.shape[0] * parts
+    quarter = BLOCK // 4
+    half_ff, quarter_ff = FF // 2, FF // 4
+    place_spots = jnp.stack([links.x, links.c]).astype(jnp.int32)
+    at_normed = width + q_cols
+    early_four = links.near(early_mine, early_theirs) if quick else ()
     tokens_grad, (mixed_mine, mixed_theirs), small = backward_pass(
-        side, (residual_grad, gated_grad, heads_grad), gains[5], mats, kept
+        early_four[:1], side, (residual_grad, gated_grad, heads_grad), gains[5], mats, kept
     )
     here = lax.axis_index("shard")
-    model = w_in.shape[0] * parts
 
     def mine(value):
         size = value.shape[-1] // parts
         return lax.dynamic_slice_in_dim(value, here * size, size, value.ndim - 1)
 
-    q_cols = QH * ATTENTION_HEAD
-    k_cols = KVH * ATTENTION_HEAD
     out_rows, attn_rows = w_out.shape[0], w_attn_out.shape[0]
     down_rows, model_rows = w_down.shape[0], w_in.shape[0]
     if quick:
-        quarter = BLOCK // 4
         whole = slice(None)
 
         def plain(rows):
             return [[(0, rows, number * quarter, quarter)] for number in range(4)]
 
-        half_ff, quarter_ff = FF // 2, FF // 4
-        edges = (0, width + channels, width + channels + q_cols, MIXED - k_cols, MIXED)
         mixed_moves = [[[] for _ in range(4)] for _ in range(4)]
-        for number in range(4):
-            for index in range(4):
-                low = max(edges[index], number * BLOCK)
-                high = min(edges[index + 1], (number + 1) * BLOCK)
+        begin = 0
+        for index, column, columns in (
+            (0, 0, width),
+            (1, 0, q_cols),
+            (0, width, channels),
+            (2, 0, k_cols),
+            (3, 0, k_cols),
+        ):
+            for number in range(4):
+                low = max(begin, number * BLOCK)
+                high = min(begin + columns, (number + 1) * BLOCK)
                 if low < high:
                     mixed_moves[index][number].append(
-                        (low - number * BLOCK, whole, low - edges[index], high - low)
+                        (low - number * BLOCK, whole, column + low - begin, high - low)
                     )
+            begin += columns
         spots = jnp.stack([links.y, links.c]).astype(jnp.int32)
-        early_four = links.near(early_mine, early_theirs)
-        late_four = links.near(late_mine, late_theirs)
-        mixed_four = links.near(mixed_mine, mixed_theirs)
-        place_spots = jnp.stack([links.x, links.c]).astype(jnp.int32)
-        at_normed = width + q_cols
-        at_hidden = model + FF
+        late_four = links.near(late_mine, late_theirs, (mixed_theirs,))
         packed = pack_grads(*small[:5], grad_ff_gain, small[5:], parts)
         feed_parts = outer(
             place_spots,
@@ -1243,6 +1364,7 @@
             links.z_size,
             True,
         )
+        at_hidden = model + FF
         out_right = (late_four, [(at_hidden + FF, quarter)])
         (out_parts,) = outer(
             place_spots,
@@ -1253,25 +1375,21 @@
             ],
             links.z_size,
             False,
-        )
+            feed_parts[1:],
+        )
+        mixed_four = links.near(mixed_mine, mixed_theirs, (out_parts,))
         mixed_parts = outer(
             place_spots,
             [(early_four, at_normed, model, mixed_four, [(0, BLOCK)])],
             links.z_size,
             True,
-        )
-        block, head_rows = links.reduce_small(packed)
-        raw_part, *totals = unpack_grads(
-            jnp.stack([links.z]).astype(jnp.int32),
-            block,
-            head_rows,
-            [(value.shape[0], value.shape[1] // parts) for value in small[1:5]]
-            + [(1, model // parts)],
-        )
-        totals = [totals[0][0], totals[1]] + [value[0] for value in totals[2:]]
+            (),
+            links.add_small(packed),
+        )
+        _, feed_pieces = links.reduce_xz(*feed_parts)
         gate, up = finish(
             spots,
-            links.reduce_xz(*feed_parts),
+            feed_pieces,
             [
                 (
                     model_rows,
@@ -1283,7 +1401,7 @@
         )
         out, attn, down = finish(
             spots,
-            links.reduce_zx(out_parts),
+            links.reduce_zx(out_parts, mixed_parts[1:]),
             [
                 (rows, BLOCK, plain(slice(at, at + rows)))
                 for rows, at in (
@@ -1293,7 +1411,17 @@
                 )
             ],
         )
-        mixed_pieces = links.reduce_xz(*mixed_parts)
+        mixed_moved, mixed_pieces, small_rows, head_rows = links.reduce_mixed(
+            *mixed_parts, (gate, out)
+        )
+        raw_part, *totals = unpack_grads(
+            jnp.stack([links.z]).astype(jnp.int32),
+            small_rows,
+            head_rows,
+            [(value.shape[0], value.shape[1] // parts) for value in small[1:5]]
+            + [(1, model // parts)],
+        )
+        totals = [totals[0][0], totals[1]] + [value[0] for value in totals[2:]]
         projection, query, key, value = finish(
             spots,
             mixed_pieces,
@@ -1319,11 +1447,9 @@
             )
             return lax.psum(part, "replica").astype(jnp.float32)
 
-        half_ff = FF // 2
         branch = joined(late_mine[:, model + 2 * FF :], late_theirs[:, model + 2 * FF :])
         mixed = share(kept[1], joined(mixed_mine, mixed_theirs))
-        hidden = late_mine[:, model + FF : model + 2 * FF]
-        down = share(hidden, feed_grad)
+        down = share(late_mine[:, model + FF : model + 2 * FF], feed_grad)
         normed_two = late_mine[:, :model]
         gate, up = [
             share(
@@ -1339,11 +1465,14 @@
         totals = [mine(summed[1])[0], mine(summed[2])]
         totals += [mine(summed[at])[0] for at in (3, 4, 8)]
         totals += [value[0] for value in summed[5:8]]
-        at = width + channels
-        projection = joined(mixed[:, :at], raw_part)
-        query = mixed[:, at : at + q_cols]
-        key = mixed[:, at + q_cols : at + q_cols + k_cols]
-        value = mixed[:, at + q_cols + k_cols :]
+        at = width + q_cols
+        projection = jnp.concatenate(
+            [mixed[:, :width], mixed[:, at : at + channels], raw_part], axis=1
+        )
+        query = mixed[:, width:at]
+        at += channels
+        key = mixed[:, at : at + k_cols]
+        value = mixed[:, at + k_cols :]
     return (
         result,
         tokens_grad,

time: 359 us -> 342 us (0.953)
  local copies, waits for them, and re-layouts: 40.6 us -> 24.4 us
  starting transfers between devices: 44.4 us -> 29.6 us
  waiting for transfers between devices: 155 us -> 163 us
  other arithmetic: 8.17 us -> 15.1 us
    ppermute x57 -> x45, starting transfers between devices: 44.4 us -> 29.6 us  [send(): return lax.ppermute(value, AXES, self.tables[axis])]
    unnamed x185 -> x148, local copies, waits for them, and re-layouts: 31.8 us -> 21.5 us
    ppermute x57 -> x45, waiting for transfers between devices: 155 us -> 163 us  [send(): return lax.ppermute(value, AXES, self.tables[axis])]
    pallas_call x12 -> x17, Pallas kernels: 41.2 us -> 46.7 us  [call_whole(): pl.pallas_call(ordered, out_shape=outs, in_specs=[pl.BlockSpec(memory_spa...]
    convert_element_type x9 -> x6, other arithmetic: 1.16 us -> 5.71 us  [around(): total = (arrived.astype(jnp.float32) + block(step)).astype(jnp.bfloat16)]
    pallas_call x11 -> x8, Pallas kernels: 21.2 us -> 16.8 us  [place(): pl.pallas_call(body, out_shape=jax.ShapeDtypeStruct(tuple(shape), pieces[...]
    convert_element_type x0 -> x4, other arithmetic: none -> 4.36 us  [the longest x3 3.33 us: reduce_mixed(): total = (arrived.astype(jnp.float32) + block).astype(jnp.bfloat16)]
  transfers between devices with their start and end apart: 58 -> 46, of which waited for: 26 -> 29; matrix products, arithmetic and copies ran while one was open for 7% -> 8% of each run, Pallas kernels for 22% -> 18%
where the time goes in v4:
time: 342 us; the launch traced here: 338 us
  waiting for transfers between devices  163 us (48%)
  Pallas kernels  80.9 us (24%)
  starting transfers between devices  29.6 us (9%)
  local copies, waits for them, and re-layouts  24.4 us (7%)
  between operations  15.9 us (5%)
  other arithmetic  15.1 us (4%)
  matrix products  8.58 us (3%)
    ppermute x45, waiting for transfers between devices, send(): return lax.ppermute(value, AXES, self.tables[axis])  163 us
    pallas_call x17, Pallas kernels, call_whole(): pl.pallas_call(ordered, out_shape=outs, in_specs=[pl.BlockSpec(memory_spa...  46.7 us
    ppermute x45, starting transfers between devices, send(): return lax.ppermute(value, AXES, self.tables[axis])  29.6 us
    unnamed x148, local copies, waits for them, and re-layouts  21.5 us
    pallas_call x8, Pallas kernels, place(): pl.pallas_call(body, out_shape=jax.ShapeDtypeStruct(tuple(shape), pieces[...  16.8 us
    pallas_call x1, Pallas kernels, middle(): pl.pallas_call(body, out_shape=outs, in_specs=[pl.BlockSpec(memory_space=...  16 us
    dot_general x3, matrix products, matmul_right(): lax.dot_general(left, right, (((1,), (1,)), ((), ())), preferred_element_...  6.96 us
  transfers between devices with their start and end apart: 46, of which 29 were waited for; matrix products, arithmetic and copies ran while one was open for 8% of the time, Pallas kernels for 18%

profile of v4, /device:TPU:0, one launch (start us, length us, event | category | flops | bytes accessed | tf_op | source)
XLA Modules:
  0.0 337.9 jit_solution(18156701064657561753)
XLA Ops:
  14.0 3.0 collective-permute-start
  21.8 4.6 %collective-permute-done.4.refs_1_ = bf16[1,1,1,1,32,2048]{5,4,3,2,1,0:T(8,128)(2,1)S(1)} collective-permute-done((bf16[1,1,1,1,32,2048]{5,4,3,2,1,0:T(8,128)(2,1)S(1)}, bf16[1,1,1,1,32,2048]{5,4,3,2,1,0:T(8,128)(2,1)S(1)}, u32[]{:S(2)}, u32[]{:S(2)}) %collective-permute-start.4) | collective-permute-done | bytes 131104 | tf_op jit(solution)/shard_map/ppermute | solution.py:1091
  28.7 8.5 %collective-permute-done.5.refs_2_ = bf16[1,1,1,1,32,2048]{5,4,3,2,1,0:T(8,128)(2,1)S(1)} collective-permute-done((bf16[1,1,1,1,32,2048]{5,4,3,2,1,0:T(8,128)(2,1)S(1)}, bf16[1,1,1,1,32,2048]{5,4,3,2,1,0:T(8,128)(2,1)S(1)}, u32[]{:S(2)}, u32[]{:S(2)}) %collective-permute-start.5) | collective-permute-done | bytes 131104 | tf_op jit(solution)/shard_map/ppermute | solution.py:1091
  37.3 5.5 %collective-permute-done.11.refs_2_ = bf16[1,1,1,1,32,2048]{5,4,3,2,1,0:T(8,128)(2,1)S(1)} collective-permute-done((bf16[1,1,1,1,32,2048]{5,4,3,2,1,0:T(8,128)(2,1)S(1)}, bf16[1,1,1,1,32,2048]{5,4,3,2,1,0:T(8,128)(2,1)S(1)}, u32[]{:S(2)}, u32[]{:S(2)}) %collective-permute-start.11) | collective-permute-done | bytes 131104 | tf_op jit(solution)/shard_map/ppermute | solution.py:1091
  42.8 5.3 %collective-permute-done.6.refs_3_ = bf16[1,1,1,1,32,2048]{5,4,3,2,1,0:T(8,128)(2,1)S(1)} collective-permute-done((bf16[1,1,1,1,32,2048]{5,4,3,2,1,0:T(8,128)(2,1)S(1)}, bf16[1,1,1,1,32,2048]{5,4,3,2,1,0:T(8,128)(2,1)S(1)}, u32[]{:S(2)}, u32[]{:S(2)}) %collective-permute-start.6) | collective-permute-done | bytes 131104 | tf_op jit(solution)/shard_map/ppermute | solution.py:1091
  55.4 8.6 %collective-permute-done.7.refs_1_ = bf16[4,1,1,1,32,2048]{5,4,3,2,1,0:T(8,128)(2,1)S(1)} collective-permute-done((bf16[4,1,1,1,32,2048]{5,4,3,2,1,0:T(8,128)(2,1)S(1)}, bf16[4,1,1,1,32,2048]{5,4,3,2,1,0:T(8,128)(2,1)S(1)}, u32[]{:S(2)}, u32[]{:S(2)}) %collective-permute-start.7) | collective-permute-done | bytes 524320 | tf_op jit(solution)/shard_map/ppermute | solution.py:1091
  66.5 9.0 %collective-permute-done.13.refs_1_ = bf16[4,1,1,1,32,2048]{5,4,3,2,1,0:T(8,128)(2,1)S(1)} collective-permute-done((bf16[4,1,1,1,32,2048]{5,4,3,2,1,0:T(8,128)(2,1)S(1)}, bf16[4,1,1,1,32,2048]{5,4,3,2,1,0:T(8,128)(2,1)S(1)}, u32[]{:S(2)}, u32[]{:S(2)}) %collective-permute-start.13) | collective-permute-done | bytes 524320 | tf_op jit(solution)/shard_map/ppermute | solution.py:1091
  79.7 6.1 %collective-permute-done.1 = bf16[2,48,128]{2,1,0:T(8,128)(2,1)S(1)} collective-permute-done((bf16[2,48,128]{2,1,0:T(8,128)(2,1)S(1)}, bf16[2,48,128]{2,1,0:T(8,128)(2,1)S(1)}, u32[]{:S(2)}, u32[]{:S(2)}) %collective-permute-start.1) | collective-permute-done | bytes 24608 | tf_op jit(solution)/shard_map/ppermute | solution.py:1091
  85.8 7.2 %collective-permute-done.8.refs_1_ = bf16[4,2,1,1,32,2048]{5,4,3,2,1,0:T(8,128)(2,1)S(1)} collective-permute-done((bf16[4,2,1,1,32,2048]{5,4,3,2,1,0:T(8,128)(2,1)S(1)}, bf16[4,2,1,1,32,2048]{5,4,3,2,1,0:T(8,128)(2,1)S(1)}, u32[]{:S(2)}, u32[]{:S(2)}) %collective-permute-start.8) | collective-permute-done | bytes 1048608 | tf_op jit(solution)/shard_map/ppermute | solution.py:1091
  99.4 3.1 place.14.refs_0_
  103.3 5.6 %collective-permute-done.3 = bf16[2,48,128]{2,1,0:T(8,128)(2,1)S(1)} collective-permute-done((bf16[2,48,128]{2,1,0:T(8,128)(2,1)S(1)}, bf16[2,48,128]{2,1,0:T(8,128)(2,1)S(1)}, u32[]{:S(2)}, u32[]{:S(2)}) %collective-permute-start.3) | collective-permute-done | bytes 24608 | tf_op jit(solution)/shard_map/ppermute | solution.py:1091
  112.9 4.1 %place.15 = bf16[4,2,2,2,32,2048]{5,4,3,2,1,0:T(8,128)(2,1)S(1)} custom-call(s32[2]{0:T(128)S(1)} %pad_add_fusion.1.where, bf16[4,2,2,1,32,2048]{5,4,3,2,1,0:T(8,128)(2,1)} %place.14.refs_0_, bf16[4,2,2,1,32,2048]{5,4,3,2,1,0:T(8,128)(2,1)} %collective-permute-done.15.refs_1_), custom_call_target="tpu_custom_call" | custom-call | flops 2529999872 | tf_op jit(solution)/shard_map/place/pallas_call | solution.py:1057
  119.7 2.9 attention_front.1
  123.3 5.4 %mixer_front.1 = (bf16[128,1792]{1,0:T(8,128)(2,1)S(1)}, f32[128,1536]{1,0:T(8,128)S(1)}, bf16[128,3584]{1,0:T(8,128)(2,1)S(1)}, bf16[128,3584]{1,0:T(8,128)(2,1)}) custom-call(s32[1]{0:T(128)} %bitcast.refs_0_.side_ref, bf16[128,512]{1,0:T(8,128)(2,1)S(1)} %get-tuple-element.70.refs_1_, bf16[128,1024]{1,0:T(8,128)(2,1)S(1)} %fusion.12.refs_2_.refs_1_, ...), custom_call_target="tpu_custom_call" | custom-call | flops 6049999872 | tf_op jit(solution)/shard_map/mixer_front/pallas_call | solution.py:115
  133.1 20.6 %collective-permute-done.16.refs_1_ = bf16[128,3584]{1,0:T(8,128)(2,1)} collective-permute-done((bf16[128,3584]{1,0:T(8,128)(2,1)}, bf16[128,3584]{1,0:T(8,128)(2,1)}, u32[]{:S(2)}, u32[]{:S(2)}) %collective-permute-start.16) | collective-permute-done | bytes 917536 | tf_op jit(solution)/shard_map/ppermute | solution.py:1091
  157.4 16.0 %middle.1 = (bf16[128,1024]{1,0:T(8,128)(2,1)}, bf16[128,5632]{1,0:T(8,128)(2,1)}, bf16[128,5632]{1,0:T(8,128)(2,1)}, f32[128,1024]{1,0:T(8,128)S(1)}, f32[1,102...) custom-call(s32[1]{0:T(128)} %bitcast.refs_0_.side_ref, bf16[32,256,1024]{2,1,0:T(8,128)(2,1)} %bitcast.194, ...), custom_call_target="tpu_custom_call" | custom-call | flops 17379999744 | tf_op jit(solution)/shard_map/middle/pallas_call | solution.py:698
  175.2 3.7 %attention_back.1.refs_2_ = bf16[128,768]{1,0:T(8,128)(2,1)S(1)} custom-call(bf16[128,768]{1,0:T(8,128)(2,1)S(1)} %copy-done.39, bf16[128,512]{1,0:T(8,128)(2,1)S(1)} %get-tuple-element.75.refs_1_, f32[128,128]{1,0:T(8,128)S(1)} %copy.115.refs_2_, f32[128,128]{1,0:T(8,128)S(1)} %copy.116.refs_3_, f32[128,128]{1,0:T(8,128)S(1)} %fusion.23.refs_4_.refs_14_.refs_16_), custom_call_target="tpu_custom_call" | custom-call | flops 4180000000 | tf_op jit(solution)/shard_map/attention_back/pallas_call | solution.py:115
  179.0 10.8 %mixer_back.1 = (bf16[128,2048]{1,0:T(8,128)(2,1)S(1)}, bf16[128,2048]{1,0:T(8,128)(2,1)S(1)}, bf16[128,24]{1,0:T(8,128)(2,1)S(1)}, f32[24,1024]{1,0:T(8,128)S(1...) custom-call(s32[1]{0:T(128)} %bitcast.refs_0_.side_ref, ...), custom_call_target="tpu_custom_call" | custom-call | flops 12650000384 | tf_op jit(solution)/shard_map/mixer_back/pallas_call | solution.py:115
  189.9 16.4 %collective-permute-done.19.refs_1_ = bf16[128,5632]{1,0:T(8,128)(2,1)S(1)} collective-permute-done((bf16[128,5632]{1,0:T(8,128)(2,1)}, bf16[128,5632]{1,0:T(8,128)(2,1)S(1)}, u32[]{:S(2)}, u32[]{:S(2)}) %collective-permute-start.19) | collective-permute-done | bytes 1441824 | tf_op jit(solution)/shard_map/ppermute | solution.py:1091
  209.1 3.9 %fusion.38 = f32[128,1024]{1,0:T(8,128)S(1)} fusion(bf16[128,2048]{1,0:T(8,128)(2,1)} %copy-done.10, bf16[1024,2048]{1,0:T(8,128)(2,1)} %bitcast.165), kind=kOutput, calls=%fused_computation.115 | convolution fusion | flops 536870912 | bytes 5242880 | tf_op jit(solution)/shard_map/dot_general | solution.py:35
  214.7 4.3 %outer.3 = (bf16[4,128,1024]{2,1,0:T(8,128)(2,1)S(1)}, bf16[4,128,1024]{2,1,0:T(8,128)(2,1)}) custom-call(s32[2]{0:T(128)S(1)} %pad_add_fusion.6.refs_0_, bf16[256,5632]{1,0:T(8,128)(2,1)S(1)} %stack.131.refs_1_.refs_3_, bf16[256,5632]{1,0:T(8,128)(2,1)} %collective-permute-done.20.refs_2_.refs_4_), custom_call_target="tpu_custom_call" | custom-call | flops 3520000000 | tf_op jit(solution)/shard_map/outer/pallas_call | solution.py:115
  220.0 4.3 %outer.4.refs_2_ = bf16[4,2,512,256]{3,2,1,0:T(8,128)(2,1)S(1)} custom-call(s32[2]{0:T(128)S(1)} %pad_add_fusion.6.refs_0_, bf16[256,3584]{1,0:T(8,128)(2,1)} %stack.130.refs_17_.refs_1_, bf16[256,3584]{1,0:T(8,128)(2,1)} %collective-permute-done.17.refs_2_, bf16[256,5632]{1,0:T(8,128)(2,1)S(1)} %stack.131.refs_1_.refs_3_, ...), custom_call_target="tpu_custom_call" | custom-call | flops 3520000000 | tf_op jit(solution)/shard_map/outer/pallas_call | solution.py:115
  228.0 2.9 fusion.13
  234.6 5.3 %collective-permute-done.23 = f32[8,48,128]{2,1,0:T(8,128)S(1)} collective-permute-done((f32[8,48,128]{2,1,0:T(8,128)S(1)}, f32[8,48,128]{2,1,0:T(8,128)S(1)}, u32[]{:S(2)}, u32[]{:S(2)}) %collective-permute-start.23) | collective-permute-done | bytes 196640 | tf_op jit(solution)/shard_map/ppermute | solution.py:1091
  239.8 2.9 collective-permute-done.37
  247.3 5.2 %outer.5 = (bf16[4,144,1024]{2,1,0:T(8,128)(2,1)S(1)}, bf16[4,144,1024]{2,1,0:T(8,128)(2,1)}) custom-call(s32[2]{0:T(128)S(1)} %pad_add_fusion.6.refs_0_, bf16[256,3584]{1,0:T(8,128)(2,1)} %stack.130.refs_17_.refs_1_, bf16[256,3584]{1,0:T(8,128)(2,1)} %collective-permute-done.17.refs_2_, bf16[256,2048]{1,0:T(8,128)(2,1)} %stack.132.refs_3_, ...), custom_call_target="tpu_custom_call" | custom-call | flops 3520000000 | tf_op jit(solution)/shard_map/outer/pallas_call | solution.py:115
  252.8 11.6 %collective-permute-done.31 = bf16[128,1024]{1,0:T(8,128)(2,1)} collective-permute-done((bf16[128,1024]{1,0:T(8,128)(2,1)}, bf16[128,1024]{1,0:T(8,128)(2,1)}, u32[]{:S(2)}, u32[]{:S(2)}) %collective-permute-start.31) | collective-permute-done | bytes 262176 | tf_op jit(solution)/shard_map/ppermute | solution.py:1091
  267.1 9.7 %collective-permute-done.32 = bf16[128,1024]{1,0:T(8,128)(2,1)S(1)} collective-permute-done((bf16[128,1024]{1,0:T(8,128)(2,1)S(1)}, bf16[128,1024]{1,0:T(8,128)(2,1)S(1)}, u32[]{:S(2)}, u32[]{:S(2)}) %collective-permute-start.32) | collective-permute-done | bytes 262176 | tf_op jit(solution)/shard_map/ppermute | solution.py:1091
  281.3 6.8 %collective-permute-done.39 = bf16[2,512,256]{2,1,0:T(8,128)(2,1)S(1)} collective-permute-done((bf16[2,512,256]{2,1,0:T(8,128)(2,1)S(1)}, bf16[2,512,256]{2,1,0:T(8,128)(2,1)S(1)}, u32[]{:S(2)}, u32[]{:S(2)}) %collective-permute-start.39) | collective-permute-done | bytes 524320 | tf_op jit(solution)/shard_map/ppermute | solution.py:1091
  290.0 7.3 %collective-permute-done.25 = bf16[144,1024]{1,0:T(8,128)(2,1)S(1)} collective-permute-done((bf16[144,1024]{1,0:T(8,128)(2,1)S(1)}, bf16[144,1024]{1,0:T(8,128)(2,1)S(1)}, u32[]{:S(2)}, u32[]{:S(2)}) %collective-permute-start.25) | collective-permute-done | bytes 294944 | tf_op jit(solution)/shard_map/ppermute | solution.py:1091
  301.7 5.3 %collective-permute-done.26 = bf16[144,1024]{1,0:T(8,128)(2,1)S(1)} collective-permute-done((bf16[144,1024]{1,0:T(8,128)(2,1)S(1)}, bf16[144,1024]{1,0:T(8,128)(2,1)S(1)}, u32[]{:S(2)}, u32[]{:S(2)}) %collective-permute-start.26) | collective-permute-done | bytes 294944 | tf_op jit(solution)/shard_map/ppermute | solution.py:1091
  311.6 3.1 collective-permute-done.42.refs_3_
  (328 shorter events, 103.3 us)
Async XLA Ops:
  7.2 150.2 %all-gather.3.cloned.1.call-start = ((), (), s32[]{:S(2)}) async-start(), calls=%async_computation | async-start | bytes 17301504 | tf_op jit(solution)/shard_map/all_gather | solution.py:1275
  14.0 65.6 %collective-permute-start = (bf16[48,128]{1,0:T(8,128)(2,1)S(1)}, bf16[48,128]{1,0:T(8,128)(2,1)S(1)}, u32[]{:S(2)}, u32[]{:S(2)}) collective-permute-start(bf16[48,128]{1,0:T(8,128)(2,1)S(1)} %pad.14), channel_id=1, source_target_pairs={{0,4},{1,5},{2,6},{3,7},{4,0},{5,1},{6,2},{7,3},{8,12},{9,13},{10,... | collective-permute-start | bytes 36872 | tf_op jit(solution)/shard_map/ppermute | solution.py:1091
  26.4 10.8 %collective-permute-start.5 = (bf16[1,1,1,1,32,2048]{5,4,3,2,1,0:T(8,128)(2,1)S(1)}, bf16[1,1,1,1,32,2048]{5,4,3,2,1,0:T(8,128)(2,1)S(1)}, u32[]{:S(2)}, u32[]{:S(2)}) collective-permute-start(bf16[1,1,1,1,32,2048]{5,4,3,2,1,0:T(8,128)(2,1)S(1)} %collective-permute-done.4.refs_1_), channel_id=1, source_target_pairs={{0,8},{1,9},{2,10},{3,11},{4,12},{5,13},{6,14},{7,15},{8,16},{9,17... | collective-permute-start | bytes 393224 | tf_op jit(solution)/shard_map/ppermute | solution.py:1091
  27.8 15.0 %collective-permute-start.11 = (bf16[1,1,1,1,32,2048]{5,4,3,2,1,0:T(8,128)(2,1)S(1)}, bf16[1,1,1,1,32,2048]{5,4,3,2,1,0:T(8,128)(2,1)S(1)}, u32[]{:S(2)}, u32[]{:S(2)}) collective-permute-start(bf16[1,1,1,1,32,2048]{5,4,3,2,1,0:T(8,128)(2,1)S(1)} %collective-permute-done.10.refs_1_), channel_id=1, source_target_pairs={{0,8},{1,9},{2,10},{3,11},{4,12},{5,13},{6,14},{7,15},{8,16},{9,17... | collective-permute-start | bytes 393224 | tf_op jit(solution)/shard_map/ppermute | solution.py:1091
  37.1 10.9 %collective-permute-start.6 = (bf16[1,1,1,1,32,2048]{5,4,3,2,1,0:T(8,128)(2,1)S(1)}, bf16[1,1,1,1,32,2048]{5,4,3,2,1,0:T(8,128)(2,1)S(1)}, u32[]{:S(2)}, u32[]{:S(2)}) collective-permute-start(bf16[1,1,1,1,32,2048]{5,4,3,2,1,0:T(8,128)(2,1)S(1)} %collective-permute-done.5.refs_2_), channel_id=1, source_target_pairs={{0,8},{1,9},{2,10},{3,11},{4,12},{5,13},{6,14},{7,15},{8,16},{9,17... | collective-permute-start | bytes 393224 | tf_op jit(solution)/shard_map/ppermute | solution.py:1091
  50.0 14.0 %collective-permute-start.7 = (bf16[4,1,1,1,32,2048]{5,4,3,2,1,0:T(8,128)(2,1)S(1)}, bf16[4,1,1,1,32,2048]{5,4,3,2,1,0:T(8,128)(2,1)S(1)}, u32[]{:S(2)}, u32[]{:S(2)}) collective-permute-start(bf16[4,1,1,1,32,2048]{5,4,3,2,1,0:T(8,128)(2,1)S(1)} %place.8.refs_0_), channel_id=1, source_target_pairs={{0,4},{1,5},{2,6},{3,7},{4,0},{5,1},{6,2},{7,3},{8,12},{9,13},{10,... | collective-permute-start | bytes 1572872 | tf_op jit(solution)/shard_map/ppermute | solution.py:1091
  53.1 22.4 %collective-permute-start.13 = (bf16[4,1,1,1,32,2048]{5,4,3,2,1,0:T(8,128)(2,1)S(1)}, bf16[4,1,1,1,32,2048]{5,4,3,2,1,0:T(8,128)(2,1)S(1)}, u32[]{:S(2)}, u32[]{:S(2)}) collective-permute-start(bf16[4,1,1,1,32,2048]{5,4,3,2,1,0:T(8,128)(2,1)S(1)} %place.12.refs_0_), channel_id=1, source_target_pairs={{0,2},{1,3},{2,0},{3,1},{4,6},{5,7},{6,4},{7,5},{8,10},{9,11},{10,... | collective-permute-start | bytes 1572872 | tf_op jit(solution)/shard_map/ppermute | solution.py:1091
  64.8 28.2 %collective-permute-start.8 = (bf16[4,2,1,1,32,2048]{5,4,3,2,1,0:T(8,128)(2,1)S(1)}, bf16[4,2,1,1,32,2048]{5,4,3,2,1,0:T(8,128)(2,1)S(1)}, u32[]{:S(2)}, u32[]{:S(2)}) collective-permute-start(bf16[4,2,1,1,32,2048]{5,4,3,2,1,0:T(8,128)(2,1)S(1)} %place.9.refs_0_), channel_id=1, source_target_pairs={{0,2},{1,3},{2,0},{3,1},{4,6},{5,7},{6,4},{7,5},{8,10},{9,11},{10,... | collective-permute-start | bytes 3145736 | tf_op jit(solution)/shard_map/ppermute | solution.py:1091
  77.2 22.2 %collective-permute-start.14 = (bf16[4,1,2,1,32,2048]{5,4,3,2,1,0:T(8,128)(2,1)}, bf16[4,1,2,1,32,2048]{5,4,3,2,1,0:T(8,128)(2,1)}, u32[]{:S(2)}, u32[]{:S(2)}) collective-permute-start(bf16[4,1,2,1,32,2048]{5,4,3,2,1,0:T(8,128)(2,1)} %place.13.refs_0_), channel_id=1, source_target_pairs={{0,4},{1,5},{2,6},{3,7},{4,0},{5,1},{6,2},{7,3},{8,12},{9,13},{10,... | collective-permute-start | bytes 3145736 | tf_op jit(solution)/shard_map/ppermute | solution.py:1091
  85.8 16.8 %collective-permute-start.2 = (bf16[2,48,128]{2,1,0:T(8,128)(2,1)S(1)}, bf16[2,48,128]{2,1,0:T(8,128)(2,1)S(1)}, u32[]{:S(2)}, u32[]{:S(2)}) collective-permute-start(bf16[2,48,128]{2,1,0:T(8,128)(2,1)S(1)} %collective-permute-done.1), channel_id=1, source_target_pairs={{0,8},{1,9},{2,10},{3,11},{4,12},{5,13},{6,14},{7,15},{8,16},{9,17... | collective-permute-start | bytes 73736 | tf_op jit(solution)/shard_map/ppermute | solution.py:1091
  97.6 12.8 %collective-permute-start.9 = (bf16[4,2,2,1,32,2048]{5,4,3,2,1,0:T(8,128)(2,1)S(1)}, bf16[4,2,2,1,32,2048]{5,4,3,2,1,0:T(8,128)(2,1)}, u32[]{:S(2)}, u32[]{:S(2)}) collective-permute-start(bf16[4,2,2,1,32,2048]{5,4,3,2,1,0:T(8,128)(2,1)S(1)} %place.10.refs_0_), channel_id=1, source_target_pairs={{0,1},{1,0},{2,3},{3,2},{4,5},{5,4},{6,7},{7,6},{8,9},{9,8},{10,11... | collective-permute-start | bytes 6291464 | tf_op jit(solution)/shard_map/ppermute | solution.py:1091
  102.5 10.4 %collective-permute-start.15 = (bf16[4,2,2,1,32,2048]{5,4,3,2,1,0:T(8,128)(2,1)}, bf16[4,2,2,1,32,2048]{5,4,3,2,1,0:T(8,128)(2,1)}, u32[]{:S(2)}, u32[]{:S(2)}) collective-permute-start(bf16[4,2,2,1,32,2048]{5,4,3,2,1,0:T(8,128)(2,1)} %place.14.refs_0_), channel_id=1, source_target_pairs={{0,1},{1,0},{2,3},{3,2},{4,5},{5,4},{6,7},{7,6},{8,9},{9,8},{10,11... | collective-permute-start | bytes 6291464 | tf_op jit(solution)/shard_map/ppermute | solution.py:1091
  131.2 22.5 %collective-permute-start.16 = (bf16[128,3584]{1,0:T(8,128)(2,1)}, bf16[128,3584]{1,0:T(8,128)(2,1)}, u32[]{:S(2)}, u32[]{:S(2)}) collective-permute-start(bf16[128,3584]{1,0:T(8,128)(2,1)} %get-tuple-element.79), channel_id=1, source_target_pairs={{0,2},{1,3},{2,0},{3,1},{4,6},{5,7},{6,4},{7,5},{8,10},{9,11},{10,... | collective-permute-start | bytes 2752520 | tf_op jit(solution)/shard_map/ppermute | solution.py:1091
  173.4 32.8 %collective-permute-start.19 = (bf16[128,5632]{1,0:T(8,128)(2,1)}, bf16[128,5632]{1,0:T(8,128)(2,1)S(1)}, u32[]{:S(2)}, u32[]{:S(2)}) collective-permute-start(bf16[128,5632]{1,0:T(8,128)(2,1)} %get-tuple-element.86), channel_id=1, source_target_pairs={{0,2},{1,3},{2,0},{3,1},{4,6},{5,7},{6,4},{7,5},{8,10},{9,11},{10,... | collective-permute-start | bytes 4325384 | tf_op jit(solution)/shard_map/ppermute | solution.py:1091
  206.6 13.4 %collective-permute-start.17 = (bf16[256,3584]{1,0:T(8,128)(2,1)}, bf16[256,3584]{1,0:T(8,128)(2,1)}, u32[]{:S(2)}, u32[]{:S(2)}) collective-permute-start(bf16[256,3584]{1,0:T(8,128)(2,1)} %stack.130.refs_17_.refs_1_), channel_id=1, source_target_pairs={{0,1},{1,0},{2,3},{3,2},{4,5},{5,4},{6,7},{7,6},{8,9},{9,8},{10,11... | collective-permute-start | bytes 5505032 | tf_op jit(solution)/shard_map/ppermute | solution.py:1091
  207.2 17.1 %collective-permute-start.18 = (bf16[128,2048]{1,0:T(8,128)(2,1)}, bf16[128,2048]{1,0:T(8,128)(2,1)S(1)}, u32[]{:S(2)}, u32[]{:S(2)}) collective-permute-start(bf16[128,2048]{1,0:T(8,128)(2,1)} %copy-done.9), channel_id=1, source_target_pairs={{0,2},{1,3},{2,0},{3,1},{4,6},{5,7},{6,4},{7,5},{8,10},{9,11},{10,... | collective-permute-start | bytes 1572872 | tf_op jit(solution)/shard_map/ppermute | solution.py:1091
  220.0 25.5 %collective-permute-start.30 = (bf16[4,128,1024]{2,1,0:T(8,128)(2,1)}, bf16[4,128,1024]{2,1,0:T(8,128)(2,1)}, u32[]{:S(2)}, u32[]{:S(2)}) collective-permute-start(bf16[4,128,1024]{2,1,0:T(8,128)(2,1)} %get-tuple-element.87.refs_5_), channel_id=1, source_target_pairs={{0,4},{1,5},{2,6},{3,7},{4,0},{5,1},{6,2},{7,3},{8,12},{9,13},{10,... | collective-permute-start | bytes 3145736 | tf_op jit(solution)/shard_map/ppermute | solution.py:1091
  225.4 21.9 %collective-permute-start.21 = (bf16[256,2048]{1,0:T(8,128)(2,1)}, bf16[256,2048]{1,0:T(8,128)(2,1)}, u32[]{:S(2)}, u32[]{:S(2)}) collective-permute-start(bf16[256,2048]{1,0:T(8,128)(2,1)} %stack.132.refs_3_), channel_id=1, source_target_pairs={{0,1},{1,0},{2,3},{3,2},{4,5},{5,4},{6,7},{7,6},{8,9},{9,8},{10,11... | collective-permute-start | bytes 3145736 | tf_op jit(solution)/shard_map/ppermute | solution.py:1091
  226.8 15.9 %collective-permute-start.37 = (bf16[2,512,256]{2,1,0:T(8,128)(2,1)}, bf16[2,512,256]{2,1,0:T(8,128)(2,1)S(1)}, u32[]{:S(2)}, u32[]{:S(2)}) collective-permute-start(bf16[2,512,256]{2,1,0:T(8,128)(2,1)} %dynamic-slice_bitcast_fusion), channel_id=1, source_target_pairs={{0,8},{1,9},{2,10},{3,11},{4,12},{5,13},{6,14},{7,15},{8,16},{9,17... | collective-permute-start | bytes 1572872 | tf_op jit(solution)/shard_map/ppermute | solution.py:1091
  243.6 22.1 %collective-permute-start.38 = (bf16[2,512,256]{2,1,0:T(8,128)(2,1)}, bf16[2,512,256]{2,1,0:T(8,128)(2,1)}, u32[]{:S(2)}, u32[]{:S(2)}) collective-permute-start(bf16[2,512,256]{2,1,0:T(8,128)(2,1)} %fusion.3), channel_id=1, source_target_pairs={{0,8},{1,9},{2,10},{3,11},{4,12},{5,13},{6,14},{7,15},{8,16},{9,17... | collective-permute-start | bytes 1572872 | tf_op jit(solution)/shard_map/ppermute | solution.py:1091
  247.3 17.2 %collective-permute-start.31 = (bf16[128,1024]{1,0:T(8,128)(2,1)}, bf16[128,1024]{1,0:T(8,128)(2,1)}, u32[]{:S(2)}, u32[]{:S(2)}) collective-permute-start(bf16[128,1024]{1,0:T(8,128)(2,1)} %fusion.21), channel_id=1, source_target_pairs={{0,8},{1,9},{2,10},{3,11},{4,12},{5,13},{6,14},{7,15},{8,16},{9,17... | collective-permute-start | bytes 786440 | tf_op jit(solution)/shard_map/ppermute | solution.py:1091
  252.5 27.5 %collective-permute-start.24 = (bf16[4,144,1024]{2,1,0:T(8,128)(2,1)}, bf16[4,144,1024]{2,1,0:T(8,128)(2,1)}, u32[]{:S(2)}, u32[]{:S(2)}) collective-permute-start(bf16[4,144,1024]{2,1,0:T(8,128)(2,1)} %get-tuple-element.97.refs_1_), channel_id=1, source_target_pairs={{0,4},{1,5},{2,6},{3,7},{4,0},{5,1},{6,2},{7,3},{8,12},{9,13},{10,... | collective-permute-start | bytes 3538952 | tf_op jit(solution)/shard_map/ppermute | solution.py:1091
  265.7 11.1 %collective-permute-start.32 = (bf16[128,1024]{1,0:T(8,128)(2,1)S(1)}, bf16[128,1024]{1,0:T(8,128)(2,1)S(1)}, u32[]{:S(2)}, u32[]{:S(2)}) collective-permute-start(bf16[128,1024]{1,0:T(8,128)(2,1)S(1)} %fusion.20), channel_id=1, source_target_pairs={{0,8},{1,9},{2,10},{3,11},{4,12},{5,13},{6,14},{7,15},{8,16},{9,17... | collective-permute-start | bytes 786440 | tf_op jit(solution)/shard_map/ppermute | solution.py:1091
  267.0 21.1 %collective-permute-start.39 = (bf16[2,512,256]{2,1,0:T(8,128)(2,1)S(1)}, bf16[2,512,256]{2,1,0:T(8,128)(2,1)S(1)}, u32[]{:S(2)}, u32[]{:S(2)}) collective-permute-start(bf16[2,512,256]{2,1,0:T(8,128)(2,1)S(1)} %fusion.2), channel_id=1, source_target_pairs={{0,8},{1,9},{2,10},{3,11},{4,12},{5,13},{6,14},{7,15},{8,16},{9,17... | collective-permute-start | bytes 1572872 | tf_op jit(solution)/shard_map/ppermute | solution.py:1091
  277.9 20.7 %collective-permute-start.33 = (bf16[128,1024]{1,0:T(8,128)(2,1)S(1)}, bf16[128,1024]{1,0:T(8,128)(2,1)S(1)}, u32[]{:S(2)}, u32[]{:S(2)}) collective-permute-start(bf16[128,1024]{1,0:T(8,128)(2,1)S(1)} %fusion.19), channel_id=1, source_target_pairs={{0,8},{1,9},{2,10},{3,11},{4,12},{5,13},{6,14},{7,15},{8,16},{9,17... | collective-permute-start | bytes 786440 | tf_op jit(solution)/shard_map/ppermute | solution.py:1091
  281.0 16.3 %collective-permute-start.25 = (bf16[144,1024]{1,0:T(8,128)(2,1)S(1)}, bf16[144,1024]{1,0:T(8,128)(2,1)S(1)}, u32[]{:S(2)}, u32[]{:S(2)}) collective-permute-start(bf16[144,1024]{1,0:T(8,128)(2,1)S(1)} %bitcast.179), channel_id=1, source_target_pairs={{0,8},{1,9},{2,10},{3,11},{4,12},{5,13},{6,14},{7,15},{8,16},{9,17... | collective-permute-start | bytes 884744 | tf_op jit(solution)/shard_map/ppermute | solution.py:1091
  288.2 19.9 %collective-permute-start.40 = (bf16[512,256]{1,0:T(8,128)(2,1)S(1)}, bf16[512,256]{1,0:T(8,128)(2,1)S(1)}, u32[]{:S(2)}, u32[]{:S(2)}) collective-permute-start(bf16[512,256]{1,0:T(8,128)(2,1)S(1)} %get-tuple-element.236), channel_id=1, source_target_pairs={{0,4},{1,5},{2,6},{3,7},{4,0},{5,1},{6,2},{7,3},{8,12},{9,13},{10,... | collective-permute-start | bytes 786440 | tf_op jit(solution)/shard_map/ppermute | solution.py:1091
  298.4 8.6 %collective-permute-start.26 = (bf16[144,1024]{1,0:T(8,128)(2,1)S(1)}, bf16[144,1024]{1,0:T(8,128)(2,1)S(1)}, u32[]{:S(2)}, u32[]{:S(2)}) collective-permute-start(bf16[144,1024]{1,0:T(8,128)(2,1)S(1)} %fusion.11), channel_id=1, source_target_pairs={{0,8},{1,9},{2,10},{3,11},{4,12},{5,13},{6,14},{7,15},{8,16},{9,17... | collective-permute-start | bytes 884744 | tf_op jit(solution)/shard_map/ppermute | solution.py:1091
  299.7 20.0 %collective-permute-start.34 = (bf16[128,1024]{1,0:T(8,128)(2,1)S(1)}, bf16[128,1024]{1,0:T(8,128)(2,1)S(1)}, u32[]{:S(2)}, u32[]{:S(2)}) collective-permute-start(bf16[128,1024]{1,0:T(8,128)(2,1)S(1)} %fusion.18.refs_1_), channel_id=1, source_target_pairs={{0,1},{1,0},{2,3},{3,2},{4,5},{5,4},{6,7},{7,6},{8,9},{9,8},{10,11... | collective-permute-start | bytes 786440 | tf_op jit(solution)/shard_map/ppermute | solution.py:1091
  299.8 10.4 %collective-permute-start.35 = (bf16[128,1024]{1,0:T(8,128)(2,1)S(1)}, bf16[128,1024]{1,0:T(8,128)(2,1)S(1)}, u32[]{:S(2)}, u32[]{:S(2)}) collective-permute-start(bf16[128,1024]{1,0:T(8,128)(2,1)S(1)} %fusion.18.refs_1_), channel_id=1, source_target_pairs={{0,2},{1,3},{2,0},{3,1},{4,6},{5,7},{6,4},{7,5},{8,10},{9,11},{10,... | collective-permute-start | bytes 786440 | tf_op jit(solution)/shard_map/ppermute | solution.py:1091
  310.2 9.6 %collective-permute-start.36 = (bf16[128,1024]{1,0:T(8,128)(2,1)S(1)}, bf16[128,1024]{1,0:T(8,128)(2,1)S(1)}, u32[]{:S(2)}, u32[]{:S(2)}) collective-permute-start(bf16[128,1024]{1,0:T(8,128)(2,1)S(1)} %collective-permute-done.35.refs_3_), channel_id=1, source_target_pairs={{0,1},{1,0},{2,3},{3,2},{4,5},{5,4},{6,7},{7,6},{8,9},{9,8},{10,11... | collective-permute-start | bytes 786440 | tf_op jit(solution)/shard_map/ppermute | solution.py:1091
  311.1 10.7 %collective-permute-start.41 = (bf16[512,256]{1,0:T(8,128)(2,1)S(1)}, bf16[512,256]{1,0:T(8,128)(2,1)S(1)}, u32[]{:S(2)}, u32[]{:S(2)}) collective-permute-start(bf16[512,256]{1,0:T(8,128)(2,1)S(1)} %add_convert_fusion.1.refs_1_), channel_id=1, source_target_pairs={{0,1},{1,0},{2,3},{3,2},{4,5},{5,4},{6,7},{7,6},{8,9},{9,8},{10,11... | collective-permute-start | bytes 786440 | tf_op jit(solution)/shard_map/ppermute | solution.py:1091
  (86 other events, 576.4 us)
Sparse Core Ops, SparseCore 0:
  13.8 131.9 all-gather.2

commit v5 on v4

--- a/solution.py
+++ b/solution.py
@@ -830,7 +830,7 @@
         body,
         out_shape=tuple(shape(size, jnp.bfloat16) for size in sizes),
         in_specs=[pl.BlockSpec(memory_space=pltpu.SMEM)]
-        + [pl.BlockSpec(memory_space=pl.ANY)] * len(weights),
+        + [pl.BlockSpec(memory_space=pltpu.HBM)] * len(weights),
         out_specs=[pl.BlockSpec(memory_space=pltpu.VMEM)] * len(sizes),
         scratch_shapes=[pltpu.SemaphoreType.DMA((len(moves),))],
         compiler_params=pltpu.CompilerParams(vmem_limit_bytes=24 * 1024 * 1024),
@@ -1139,7 +1139,6 @@
         return lax.dynamic_index_in_dim(value, at, 0, False).astype(jnp.float32)
 
     def add_small(self, value):
-        value = value + self.send(value, "c")
         value = value + self.send(value, "y")
         return value.reshape(self.z_size, 2, 48, 128)
 
@@ -1348,8 +1347,9 @@
                     )
             begin += columns
         spots = jnp.stack([links.y, links.c]).astype(jnp.int32)
-        late_four = links.near(late_mine, late_theirs, (mixed_theirs,))
         packed = pack_grads(*small[:5], grad_ff_gain, small[5:], parts)
+        packed = packed + links.send(packed, "c")
+        late_four = links.near(late_mine, late_theirs, (packed,))
         feed_parts = outer(
             place_spots,
             [

time: 342 us -> 343 us (level)
  Pallas kernels: 80.9 us -> 76.2 us
    pallas_call x17, Pallas kernels: 46.7 us -> 41.9 us  [call_whole(): pl.pallas_call(ordered, out_shape=outs, in_specs=[pl.BlockSpec(memory_spa...]
    unnamed x148 -> x126, local copies, waits for them, and re-layouts: 21.5 us -> 24.4 us
  transfers between devices with their start and end apart: 46 -> 46, of which waited for: 29 -> 29; matrix products, arithmetic and copies ran while one was open for 8% -> 9% of each run, Pallas kernels for 18% -> 16%
where the time goes in v5:
time: 343 us; the launch traced here: 338 us
  waiting for transfers between devices  163 us (48%)
  Pallas kernels  76.2 us (22%)
  starting transfers between devices  28.3 us (8%)
  local copies, waits for them, and re-layouts  27.2 us (8%)
  other arithmetic  17.8 us (5%)
  between operations  15.9 us (5%)
  matrix products  9.37 us (3%)
    ppermute x45, waiting for transfers between devices, send(): return lax.ppermute(value, AXES, self.tables[axis])  163 us
    pallas_call x17, Pallas kernels, call_whole(): pl.pallas_call(ordered, out_shape=outs, in_specs=[pl.BlockSpec(memory_spa...  41.9 us
    ppermute x45, starting transfers between devices, send(): return lax.ppermute(value, AXES, self.tables[axis])  28.3 us
    unnamed x126, local copies, waits for them, and re-layouts  24.4 us
    pallas_call x8, Pallas kernels, place(): pl.pallas_call(body, out_shape=jax.ShapeDtypeStruct(tuple(shape), pieces[...  16.8 us
    pallas_call x1, Pallas kernels, middle(): pl.pallas_call(body, out_shape=outs, in_specs=[pl.BlockSpec(memory_space=...  16 us
    dot_general x3, matrix products, matmul_right(): lax.dot_general(left, right, (((1,), (1,)), ((), ())), preferred_element_...  6.94 us
  transfers between devices with their start and end apart: 46, of which 29 were waited for; matrix products, arithmetic and copies ran while one was open for 9% of the time, Pallas kernels for 16%

profile of v5, /device:TPU:0, one launch (start us, length us, event | category | flops | bytes accessed | tf_op | source)
XLA Modules:
  0.0 338.1 jit_solution(5208301425001623713)
XLA Ops:
  14.0 3.0 collective-permute-start
  21.8 4.6 %collective-permute-done.4.refs_1_ = bf16[1,1,1,1,32,2048]{5,4,3,2,1,0:T(8,128)(2,1)S(1)} collective-permute-done((bf16[1,1,1,1,32,2048]{5,4,3,2,1,0:T(8,128)(2,1)S(1)}, bf16[1,1,1,1,32,2048]{5,4,3,2,1,0:T(8,128)(2,1)S(1)}, u32[]{:S(2)}, u32[]{:S(2)}) %collective-permute-start.4) | collective-permute-done | bytes 131104 | tf_op jit(solution)/shard_map/ppermute | solution.py:1091
  28.7 8.5 %collective-permute-done.5.refs_2_ = bf16[1,1,1,1,32,2048]{5,4,3,2,1,0:T(8,128)(2,1)S(1)} collective-permute-done((bf16[1,1,1,1,32,2048]{5,4,3,2,1,0:T(8,128)(2,1)S(1)}, bf16[1,1,1,1,32,2048]{5,4,3,2,1,0:T(8,128)(2,1)S(1)}, u32[]{:S(2)}, u32[]{:S(2)}) %collective-permute-start.5) | collective-permute-done | bytes 131104 | tf_op jit(solution)/shard_map/ppermute | solution.py:1091
  37.3 5.5 %collective-permute-done.11.refs_2_ = bf16[1,1,1,1,32,2048]{5,4,3,2,1,0:T(8,128)(2,1)S(1)} collective-permute-done((bf16[1,1,1,1,32,2048]{5,4,3,2,1,0:T(8,128)(2,1)S(1)}, bf16[1,1,1,1,32,2048]{5,4,3,2,1,0:T(8,128)(2,1)S(1)}, u32[]{:S(2)}, u32[]{:S(2)}) %collective-permute-start.11) | collective-permute-done | bytes 131104 | tf_op jit(solution)/shard_map/ppermute | solution.py:1091
  42.8 5.3 %collective-permute-done.6.refs_3_ = bf16[1,1,1,1,32,2048]{5,4,3,2,1,0:T(8,128)(2,1)S(1)} collective-permute-done((bf16[1,1,1,1,32,2048]{5,4,3,2,1,0:T(8,128)(2,1)S(1)}, bf16[1,1,1,1,32,2048]{5,4,3,2,1,0:T(8,128)(2,1)S(1)}, u32[]{:S(2)}, u32[]{:S(2)}) %collective-permute-start.6) | collective-permute-done | bytes 131104 | tf_op jit(solution)/shard_map/ppermute | solution.py:1091
  55.4 8.6 %collective-permute-done.7.refs_1_ = bf16[4,1,1,1,32,2048]{5,4,3,2,1,0:T(8,128)(2,1)S(1)} collective-permute-done((bf16[4,1,1,1,32,2048]{5,4,3,2,1,0:T(8,128)(2,1)S(1)}, bf16[4,1,1,1,32,2048]{5,4,3,2,1,0:T(8,128)(2,1)S(1)}, u32[]{:S(2)}, u32[]{:S(2)}) %collective-permute-start.7) | collective-permute-done | bytes 524320 | tf_op jit(solution)/shard_map/ppermute | solution.py:1091
  66.5 9.0 %collective-permute-done.13.refs_1_ = bf16[4,1,1,1,32,2048]{5,4,3,2,1,0:T(8,128)(2,1)S(1)} collective-permute-done((bf16[4,1,1,1,32,2048]{5,4,3,2,1,0:T(8,128)(2,1)S(1)}, bf16[4,1,1,1,32,2048]{5,4,3,2,1,0:T(8,128)(2,1)S(1)}, u32[]{:S(2)}, u32[]{:S(2)}) %collective-permute-start.13) | collective-permute-done | bytes 524320 | tf_op jit(solution)/shard_map/ppermute | solution.py:1091
  79.7 6.1 %collective-permute-done.1 = bf16[2,48,128]{2,1,0:T(8,128)(2,1)S(1)} collective-permute-done((bf16[2,48,128]{2,1,0:T(8,128)(2,1)S(1)}, bf16[2,48,128]{2,1,0:T(8,128)(2,1)S(1)}, u32[]{:S(2)}, u32[]{:S(2)}) %collective-permute-start.1) | collective-permute-done | bytes 24608 | tf_op jit(solution)/shard_map/ppermute | solution.py:1091
  85.8 7.2 %collective-permute-done.8.refs_1_ = bf16[4,2,1,1,32,2048]{5,4,3,2,1,0:T(8,128)(2,1)S(1)} collective-permute-done((bf16[4,2,1,1,32,2048]{5,4,3,2,1,0:T(8,128)(2,1)S(1)}, bf16[4,2,1,1,32,2048]{5,4,3,2,1,0:T(8,128)(2,1)S(1)}, u32[]{:S(2)}, u32[]{:S(2)}) %collective-permute-start.8) | collective-permute-done | bytes 1048608 | tf_op jit(solution)/shard_map/ppermute | solution.py:1091
  99.4 3.1 place.14.refs_0_
  103.3 5.6 %collective-permute-done.3 = bf16[2,48,128]{2,1,0:T(8,128)(2,1)S(1)} collective-permute-done((bf16[2,48,128]{2,1,0:T(8,128)(2,1)S(1)}, bf16[2,48,128]{2,1,0:T(8,128)(2,1)S(1)}, u32[]{:S(2)}, u32[]{:S(2)}) %collective-permute-start.3) | collective-permute-done | bytes 24608 | tf_op jit(solution)/shard_map/ppermute | solution.py:1091
  112.6 4.1 %place.15 = bf16[4,2,2,2,32,2048]{5,4,3,2,1,0:T(8,128)(2,1)S(1)} custom-call(s32[2]{0:T(128)S(1)} %pad_add_fusion.1.where, bf16[4,2,2,1,32,2048]{5,4,3,2,1,0:T(8,128)(2,1)} %place.14.refs_0_, bf16[4,2,2,1,32,2048]{5,4,3,2,1,0:T(8,128)(2,1)} %collective-permute-done.15.refs_1_), custom_call_target="tpu_custom_call" | custom-call | flops 2529999872 | tf_op jit(solution)/shard_map/place/pallas_call | solution.py:1057
  119.4 2.9 attention_front.1
  123.0 5.4 %mixer_front.1 = (bf16[128,1792]{1,0:T(8,128)(2,1)S(1)}, f32[128,1536]{1,0:T(8,128)S(1)}, bf16[128,3584]{1,0:T(8,128)(2,1)S(1)}, bf16[128,3584]{1,0:T(8,128)(2,1)}) custom-call(s32[1]{0:T(128)} %bitcast.refs_0_.side_ref, bf16[128,512]{1,0:T(8,128)(2,1)S(1)} %get-tuple-element.70.refs_1_, bf16[128,1024]{1,0:T(8,128)(2,1)S(1)} %fusion.12.refs_2_.refs_1_, ...), custom_call_target="tpu_custom_call" | custom-call | flops 6049999872 | tf_op jit(solution)/shard_map/mixer_front/pallas_call | solution.py:115
  132.8 20.6 %collective-permute-done.16.refs_1_ = bf16[128,3584]{1,0:T(8,128)(2,1)} collective-permute-done((bf16[128,3584]{1,0:T(8,128)(2,1)}, bf16[128,3584]{1,0:T(8,128)(2,1)}, u32[]{:S(2)}, u32[]{:S(2)}) %collective-permute-start.16) | collective-permute-done | bytes 917536 | tf_op jit(solution)/shard_map/ppermute | solution.py:1091
  157.2 16.0 %middle.1 = (bf16[128,1024]{1,0:T(8,128)(2,1)}, bf16[128,5632]{1,0:T(8,128)(2,1)}, bf16[128,5632]{1,0:T(8,128)(2,1)}, f32[128,1024]{1,0:T(8,128)S(1)}, f32[1,102...) custom-call(s32[1]{0:T(128)} %bitcast.refs_0_.side_ref, bf16[32,256,1024]{2,1,0:T(8,128)(2,1)} %bitcast.194, ...), custom_call_target="tpu_custom_call" | custom-call | flops 17379999744 | tf_op jit(solution)/shard_map/middle/pallas_call | solution.py:698
  175.0 3.7 %attention_back.1.refs_2_ = bf16[128,768]{1,0:T(8,128)(2,1)S(1)} custom-call(bf16[128,768]{1,0:T(8,128)(2,1)S(1)} %copy-done.44, bf16[128,512]{1,0:T(8,128)(2,1)S(1)} %get-tuple-element.75.refs_1_, f32[128,128]{1,0:T(8,128)S(1)} %copy.115.refs_2_, f32[128,128]{1,0:T(8,128)S(1)} %copy.116.refs_3_, f32[128,128]{1,0:T(8,128)S(1)} %fusion.23.refs_4_.refs_14_.refs_16_), custom_call_target="tpu_custom_call" | custom-call | flops 4180000000 | tf_op jit(solution)/shard_map/attention_back/pallas_call | solution.py:115
  178.8 10.8 %mixer_back.1 = (bf16[128,2048]{1,0:T(8,128)(2,1)S(1)}, bf16[128,2048]{1,0:T(8,128)(2,1)S(1)}, bf16[128,24]{1,0:T(8,128)(2,1)S(1)}, f32[24,1024]{1,0:T(8,128)S(1...) custom-call(s32[1]{0:T(128)} %bitcast.refs_0_.side_ref, ...), custom_call_target="tpu_custom_call" | custom-call | flops 12650000384 | tf_op jit(solution)/shard_map/mixer_back/pallas_call | solution.py:115
  193.8 3.8 %fusion.38 = f32[128,1024]{1,0:T(8,128)S(1)} fusion(bf16[128,2048]{1,0:T(8,128)(2,1)S(1)} %get-tuple-element.81, bf16[1024,2048]{1,0:T(8,128)(2,1)} %bitcast.165), kind=kOutput, calls=%fused_computation.115 | convolution fusion | flops 536870912 | bytes 5242880 | tf_op jit(solution)/shard_map/dot_general | solution.py:35
  197.7 2.9 fusion.13
  202.3 3.8 %collective-permute-done.19.refs_1_ = bf16[128,5632]{1,0:T(8,128)(2,1)} collective-permute-done((bf16[128,5632]{1,0:T(8,128)(2,1)}, bf16[128,5632]{1,0:T(8,128)(2,1)}, u32[]{:S(2)}, u32[]{:S(2)}) %collective-permute-start.19) | collective-permute-done | bytes 1441824 | tf_op jit(solution)/shard_map/ppermute | solution.py:1091
  210.4 3.0 collective-permute-done.21.refs_2_.refs_4_
  218.2 4.4 %collective-permute-done.18.refs_1_ = bf16[128,2048]{1,0:T(8,128)(2,1)S(1)} collective-permute-done((bf16[128,2048]{1,0:T(8,128)(2,1)S(1)}, bf16[128,2048]{1,0:T(8,128)(2,1)S(1)}, u32[]{:S(2)}, u32[]{:S(2)}) %collective-permute-start.18) | collective-permute-done | bytes 524320 | tf_op jit(solution)/shard_map/ppermute | solution.py:1091
  226.2 5.9 %collective-permute-done.23 = f32[8,48,128]{2,1,0:T(8,128)} collective-permute-done((f32[8,48,128]{2,1,0:T(8,128)}, f32[8,48,128]{2,1,0:T(8,128)}, u32[]{:S(2)}, u32[]{:S(2)}) %collective-permute-start.23) | collective-permute-done | bytes 196640 | tf_op jit(solution)/shard_map/ppermute | solution.py:1091
  233.2 7.8 %collective-permute-done.37 = bf16[2,512,256]{2,1,0:T(8,128)(2,1)} collective-permute-done((bf16[2,512,256]{2,1,0:T(8,128)(2,1)}, bf16[2,512,256]{2,1,0:T(8,128)(2,1)}, u32[]{:S(2)}, u32[]{:S(2)}) %collective-permute-start.37) | collective-permute-done | bytes 524320 | tf_op jit(solution)/shard_map/ppermute | solution.py:1091
  246.2 4.1 %outer.5 = (bf16[4,144,1024]{2,1,0:T(8,128)(2,1)S(1)}, bf16[4,144,1024]{2,1,0:T(8,128)(2,1)}) custom-call(s32[2]{0:T(128)S(1)} %pad_add_fusion.6.refs_0_, bf16[256,3584]{1,0:T(8,128)(2,1)S(1)} %copy-done.15, bf16[256,3584]{1,0:T(8,128)(2,1)S(1)} %copy-done.17, bf16[256,2048]{1,0:T(8,128)(2,1)} %stack.132.refs_3_, ...), custom_call_target="tpu_custom_call" | custom-call | flops 3520000000 | tf_op jit(solution)/shard_map/outer/pallas_call | solution.py:115
  250.7 13.4 %collective-permute-done.31 = bf16[128,1024]{1,0:T(8,128)(2,1)} collective-permute-done((bf16[128,1024]{1,0:T(8,128)(2,1)}, bf16[128,1024]{1,0:T(8,128)(2,1)}, u32[]{:S(2)}, u32[]{:S(2)}) %collective-permute-start.31) | collective-permute-done | bytes 262176 | tf_op jit(solution)/shard_map/ppermute | solution.py:1091
  267.4 9.1 %collective-permute-done.32 = bf16[128,1024]{1,0:T(8,128)(2,1)S(1)} collective-permute-done((bf16[128,1024]{1,0:T(8,128)(2,1)S(1)}, bf16[128,1024]{1,0:T(8,128)(2,1)S(1)}, u32[]{:S(2)}, u32[]{:S(2)}) %collective-permute-start.32) | collective-permute-done | bytes 262176 | tf_op jit(solution)/shard_map/ppermute | solution.py:1091
  280.1 7.7 %collective-permute-done.39 = bf16[2,512,256]{2,1,0:T(8,128)(2,1)S(1)} collective-permute-done((bf16[2,512,256]{2,1,0:T(8,128)(2,1)S(1)}, bf16[2,512,256]{2,1,0:T(8,128)(2,1)S(1)}, u32[]{:S(2)}, u32[]{:S(2)}) %collective-permute-start.39) | collective-permute-done | bytes 524320 | tf_op jit(solution)/shard_map/ppermute | solution.py:1091
  288.1 9.4 %collective-permute-done.25 = bf16[144,1024]{1,0:T(8,128)(2,1)S(1)} collective-permute-done((bf16[144,1024]{1,0:T(8,128)(2,1)S(1)}, bf16[144,1024]{1,0:T(8,128)(2,1)S(1)}, u32[]{:S(2)}, u32[]{:S(2)}) %collective-permute-start.25) | collective-permute-done | bytes 294944 | tf_op jit(solution)/shard_map/ppermute | solution.py:1091
  301.8 5.5 %collective-permute-done.26 = bf16[144,1024]{1,0:T(8,128)(2,1)S(1)} collective-permute-done((bf16[144,1024]{1,0:T(8,128)(2,1)S(1)}, bf16[144,1024]{1,0:T(8,128)(2,1)S(1)}, u32[]{:S(2)}, u32[]{:S(2)}) %collective-permute-start.26) | collective-permute-done | bytes 294944 | tf_op jit(solution)/shard_map/ppermute | solution.py:1091
  311.8 3.2 collective-permute-done.42.refs_3_
  (306 shorter events, 108.3 us)
Async XLA Ops:
  7.2 150.0 %all-gather.3.cloned.1.call-start = ((), (), s32[]{:S(2)}) async-start(), calls=%async_computation | async-start | bytes 17301504 | tf_op jit(solution)/shard_map/all_gather | solution.py:1274
  14.0 65.6 %collective-permute-start = (bf16[48,128]{1,0:T(8,128)(2,1)S(1)}, bf16[48,128]{1,0:T(8,128)(2,1)S(1)}, u32[]{:S(2)}, u32[]{:S(2)}) collective-permute-start(bf16[48,128]{1,0:T(8,128)(2,1)S(1)} %pad.14), channel_id=1, source_target_pairs={{0,4},{1,5},{2,6},{3,7},{4,0},{5,1},{6,2},{7,3},{8,12},{9,13},{10,... | collective-permute-start | bytes 36872 | tf_op jit(solution)/shard_map/ppermute | solution.py:1091
  26.4 10.8 %collective-permute-start.5 = (bf16[1,1,1,1,32,2048]{5,4,3,2,1,0:T(8,128)(2,1)S(1)}, bf16[1,1,1,1,32,2048]{5,4,3,2,1,0:T(8,128)(2,1)S(1)}, u32[]{:S(2)}, u32[]{:S(2)}) collective-permute-start(bf16[1,1,1,1,32,2048]{5,4,3,2,1,0:T(8,128)(2,1)S(1)} %collective-permute-done.4.refs_1_), channel_id=1, source_target_pairs={{0,8},{1,9},{2,10},{3,11},{4,12},{5,13},{6,14},{7,15},{8,16},{9,17... | collective-permute-start | bytes 393224 | tf_op jit(solution)/shard_map/ppermute | solution.py:1091
  27.8 15.0 %collective-permute-start.11 = (bf16[1,1,1,1,32,2048]{5,4,3,2,1,0:T(8,128)(2,1)S(1)}, bf16[1,1,1,1,32,2048]{5,4,3,2,1,0:T(8,128)(2,1)S(1)}, u32[]{:S(2)}, u32[]{:S(2)}) collective-permute-start(bf16[1,1,1,1,32,2048]{5,4,3,2,1,0:T(8,128)(2,1)S(1)} %collective-permute-done.10.refs_1_), channel_id=1, source_target_pairs={{0,8},{1,9},{2,10},{3,11},{4,12},{5,13},{6,14},{7,15},{8,16},{9,17... | collective-permute-start | bytes 393224 | tf_op jit(solution)/shard_map/ppermute | solution.py:1091
  37.1 10.9 %collective-permute-start.6 = (bf16[1,1,1,1,32,2048]{5,4,3,2,1,0:T(8,128)(2,1)S(1)}, bf16[1,1,1,1,32,2048]{5,4,3,2,1,0:T(8,128)(2,1)S(1)}, u32[]{:S(2)}, u32[]{:S(2)}) collective-permute-start(bf16[1,1,1,1,32,2048]{5,4,3,2,1,0:T(8,128)(2,1)S(1)} %collective-permute-done.5.refs_2_), channel_id=1, source_target_pairs={{0,8},{1,9},{2,10},{3,11},{4,12},{5,13},{6,14},{7,15},{8,16},{9,17... | collective-permute-start | bytes 393224 | tf_op jit(solution)/shard_map/ppermute | solution.py:1091
  50.0 14.0 %collective-permute-start.7 = (bf16[4,1,1,1,32,2048]{5,4,3,2,1,0:T(8,128)(2,1)S(1)}, bf16[4,1,1,1,32,2048]{5,4,3,2,1,0:T(8,128)(2,1)S(1)}, u32[]{:S(2)}, u32[]{:S(2)}) collective-permute-start(bf16[4,1,1,1,32,2048]{5,4,3,2,1,0:T(8,128)(2,1)S(1)} %place.8.refs_0_), channel_id=1, source_target_pairs={{0,4},{1,5},{2,6},{3,7},{4,0},{5,1},{6,2},{7,3},{8,12},{9,13},{10,... | collective-permute-start | bytes 1572872 | tf_op jit(solution)/shard_map/ppermute | solution.py:1091
  53.1 22.4 %collective-permute-start.13 = (bf16[4,1,1,1,32,2048]{5,4,3,2,1,0:T(8,128)(2,1)S(1)}, bf16[4,1,1,1,32,2048]{5,4,3,2,1,0:T(8,128)(2,1)S(1)}, u32[]{:S(2)}, u32[]{:S(2)}) collective-permute-start(bf16[4,1,1,1,32,2048]{5,4,3,2,1,0:T(8,128)(2,1)S(1)} %place.12.refs_0_), channel_id=1, source_target_pairs={{0,2},{1,3},{2,0},{3,1},{4,6},{5,7},{6,4},{7,5},{8,10},{9,11},{10,... | collective-permute-start | bytes 1572872 | tf_op jit(solution)/shard_map/ppermute | solution.py:1091
  64.8 28.2 %collective-permute-start.8 = (bf16[4,2,1,1,32,2048]{5,4,3,2,1,0:T(8,128)(2,1)S(1)}, bf16[4,2,1,1,32,2048]{5,4,3,2,1,0:T(8,128)(2,1)S(1)}, u32[]{:S(2)}, u32[]{:S(2)}) collective-permute-start(bf16[4,2,1,1,32,2048]{5,4,3,2,1,0:T(8,128)(2,1)S(1)} %place.9.refs_0_), channel_id=1, source_target_pairs={{0,2},{1,3},{2,0},{3,1},{4,6},{5,7},{6,4},{7,5},{8,10},{9,11},{10,... | collective-permute-start | bytes 3145736 | tf_op jit(solution)/shard_map/ppermute | solution.py:1091
  77.2 22.2 %collective-permute-start.14 = (bf16[4,1,2,1,32,2048]{5,4,3,2,1,0:T(8,128)(2,1)}, bf16[4,1,2,1,32,2048]{5,4,3,2,1,0:T(8,128)(2,1)}, u32[]{:S(2)}, u32[]{:S(2)}) collective-permute-start(bf16[4,1,2,1,32,2048]{5,4,3,2,1,0:T(8,128)(2,1)} %place.13.refs_0_), channel_id=1, source_target_pairs={{0,4},{1,5},{2,6},{3,7},{4,0},{5,1},{6,2},{7,3},{8,12},{9,13},{10,... | collective-permute-start | bytes 3145736 | tf_op jit(solution)/shard_map/ppermute | solution.py:1091
  85.8 16.9 %collective-permute-start.2 = (bf16[2,48,128]{2,1,0:T(8,128)(2,1)S(1)}, bf16[2,48,128]{2,1,0:T(8,128)(2,1)S(1)}, u32[]{:S(2)}, u32[]{:S(2)}) collective-permute-start(bf16[2,48,128]{2,1,0:T(8,128)(2,1)S(1)} %collective-permute-done.1), channel_id=1, source_target_pairs={{0,8},{1,9},{2,10},{3,11},{4,12},{5,13},{6,14},{7,15},{8,16},{9,17... | collective-permute-start | bytes 73736 | tf_op jit(solution)/shard_map/ppermute | solution.py:1091
  97.6 12.5 %collective-permute-start.9 = (bf16[4,2,2,1,32,2048]{5,4,3,2,1,0:T(8,128)(2,1)S(1)}, bf16[4,2,2,1,32,2048]{5,4,3,2,1,0:T(8,128)(2,1)}, u32[]{:S(2)}, u32[]{:S(2)}) collective-permute-start(bf16[4,2,2,1,32,2048]{5,4,3,2,1,0:T(8,128)(2,1)S(1)} %place.10.refs_0_), channel_id=1, source_target_pairs={{0,1},{1,0},{2,3},{3,2},{4,5},{5,4},{6,7},{7,6},{8,9},{9,8},{10,11... | collective-permute-start | bytes 6291464 | tf_op jit(solution)/shard_map/ppermute | solution.py:1091
  102.5 10.1 %collective-permute-start.15 = (bf16[4,2,2,1,32,2048]{5,4,3,2,1,0:T(8,128)(2,1)}, bf16[4,2,2,1,32,2048]{5,4,3,2,1,0:T(8,128)(2,1)}, u32[]{:S(2)}, u32[]{:S(2)}) collective-permute-start(bf16[4,2,2,1,32,2048]{5,4,3,2,1,0:T(8,128)(2,1)} %place.14.refs_0_), channel_id=1, source_target_pairs={{0,1},{1,0},{2,3},{3,2},{4,5},{5,4},{6,7},{7,6},{8,9},{9,8},{10,11... | collective-permute-start | bytes 6291464 | tf_op jit(solution)/shard_map/ppermute | solution.py:1091
  131.0 22.5 %collective-permute-start.16 = (bf16[128,3584]{1,0:T(8,128)(2,1)}, bf16[128,3584]{1,0:T(8,128)(2,1)}, u32[]{:S(2)}, u32[]{:S(2)}) collective-permute-start(bf16[128,3584]{1,0:T(8,128)(2,1)} %get-tuple-element.79), channel_id=1, source_target_pairs={{0,2},{1,3},{2,0},{3,1},{4,6},{5,7},{6,4},{7,5},{8,10},{9,11},{10,... | collective-permute-start | bytes 2752520 | tf_op jit(solution)/shard_map/ppermute | solution.py:1091
  173.2 32.9 %collective-permute-start.19 = (bf16[128,5632]{1,0:T(8,128)(2,1)}, bf16[128,5632]{1,0:T(8,128)(2,1)}, u32[]{:S(2)}, u32[]{:S(2)}) collective-permute-start(bf16[128,5632]{1,0:T(8,128)(2,1)} %get-tuple-element.86), channel_id=1, source_target_pairs={{0,2},{1,3},{2,0},{3,1},{4,6},{5,7},{6,4},{7,5},{8,10},{9,11},{10,... | collective-permute-start | bytes 4325384 | tf_op jit(solution)/shard_map/ppermute | solution.py:1091
  208.7 13.9 %collective-permute-start.18 = (bf16[128,2048]{1,0:T(8,128)(2,1)S(1)}, bf16[128,2048]{1,0:T(8,128)(2,1)S(1)}, u32[]{:S(2)}, u32[]{:S(2)}) collective-permute-start(bf16[128,2048]{1,0:T(8,128)(2,1)S(1)} %copy-done.26), channel_id=1, source_target_pairs={{0,2},{1,3},{2,0},{3,1},{4,6},{5,7},{6,4},{7,5},{8,10},{9,11},{10,... | collective-permute-start | bytes 1572872 | tf_op jit(solution)/shard_map/ppermute | solution.py:1091
  216.2 26.7 %collective-permute-start.30 = (bf16[4,128,1024]{2,1,0:T(8,128)(2,1)}, bf16[4,128,1024]{2,1,0:T(8,128)(2,1)}, u32[]{:S(2)}, u32[]{:S(2)}) collective-permute-start(bf16[4,128,1024]{2,1,0:T(8,128)(2,1)} %get-tuple-element.95.refs_5_), channel_id=1, source_target_pairs={{0,4},{1,5},{2,6},{3,7},{4,0},{5,1},{6,2},{7,3},{8,12},{9,13},{10,... | collective-permute-start | bytes 3145736 | tf_op jit(solution)/shard_map/ppermute | solution.py:1091
  223.6 21.0 %collective-permute-start.22 = (bf16[256,2048]{1,0:T(8,128)(2,1)}, bf16[256,2048]{1,0:T(8,128)(2,1)}, u32[]{:S(2)}, u32[]{:S(2)}) collective-permute-start(bf16[256,2048]{1,0:T(8,128)(2,1)} %stack.132.refs_3_), channel_id=1, source_target_pairs={{0,1},{1,0},{2,3},{3,2},{4,5},{5,4},{6,7},{7,6},{8,9},{9,8},{10,11... | collective-permute-start | bytes 3145736 | tf_op jit(solution)/shard_map/ppermute | solution.py:1091
  224.5 16.4 %collective-permute-start.37 = (bf16[2,512,256]{2,1,0:T(8,128)(2,1)}, bf16[2,512,256]{2,1,0:T(8,128)(2,1)}, u32[]{:S(2)}, u32[]{:S(2)}) collective-permute-start(bf16[2,512,256]{2,1,0:T(8,128)(2,1)} %dynamic-slice_bitcast_fusion), channel_id=1, source_target_pairs={{0,8},{1,9},{2,10},{3,11},{4,12},{5,13},{6,14},{7,15},{8,16},{9,17... | collective-permute-start | bytes 1572872 | tf_op jit(solution)/shard_map/ppermute | solution.py:1091
  242.9 22.6 %collective-permute-start.38 = (bf16[2,512,256]{2,1,0:T(8,128)(2,1)}, bf16[2,512,256]{2,1,0:T(8,128)(2,1)}, u32[]{:S(2)}, u32[]{:S(2)}) collective-permute-start(bf16[2,512,256]{2,1,0:T(8,128)(2,1)} %fusion.3), channel_id=1, source_target_pairs={{0,8},{1,9},{2,10},{3,11},{4,12},{5,13},{6,14},{7,15},{8,16},{9,17... | collective-permute-start | bytes 1572872 | tf_op jit(solution)/shard_map/ppermute | solution.py:1091
  244.6 19.5 %collective-permute-start.31 = (bf16[128,1024]{1,0:T(8,128)(2,1)}, bf16[128,1024]{1,0:T(8,128)(2,1)}, u32[]{:S(2)}, u32[]{:S(2)}) collective-permute-start(bf16[128,1024]{1,0:T(8,128)(2,1)} %fusion.21), channel_id=1, source_target_pairs={{0,8},{1,9},{2,10},{3,11},{4,12},{5,13},{6,14},{7,15},{8,16},{9,17... | collective-permute-start | bytes 786440 | tf_op jit(solution)/shard_map/ppermute | solution.py:1091
  250.2 27.9 %collective-permute-start.24 = (bf16[4,144,1024]{2,1,0:T(8,128)(2,1)}, bf16[4,144,1024]{2,1,0:T(8,128)(2,1)}, u32[]{:S(2)}, u32[]{:S(2)}) collective-permute-start(bf16[4,144,1024]{2,1,0:T(8,128)(2,1)} %get-tuple-element.97.refs_1_), channel_id=1, source_target_pairs={{0,4},{1,5},{2,6},{3,7},{4,0},{5,1},{6,2},{7,3},{8,12},{9,13},{10,... | collective-permute-start | bytes 3538952 | tf_op jit(solution)/shard_map/ppermute | solution.py:1091
  265.4 11.1 %collective-permute-start.32 = (bf16[128,1024]{1,0:T(8,128)(2,1)S(1)}, bf16[128,1024]{1,0:T(8,128)(2,1)S(1)}, u32[]{:S(2)}, u32[]{:S(2)}) collective-permute-start(bf16[128,1024]{1,0:T(8,128)(2,1)S(1)} %fusion.20), channel_id=1, source_target_pairs={{0,8},{1,9},{2,10},{3,11},{4,12},{5,13},{6,14},{7,15},{8,16},{9,17... | collective-permute-start | bytes 786440 | tf_op jit(solution)/shard_map/ppermute | solution.py:1091
  266.7 21.1 %collective-permute-start.39 = (bf16[2,512,256]{2,1,0:T(8,128)(2,1)S(1)}, bf16[2,512,256]{2,1,0:T(8,128)(2,1)S(1)}, u32[]{:S(2)}, u32[]{:S(2)}) collective-permute-start(bf16[2,512,256]{2,1,0:T(8,128)(2,1)S(1)} %fusion.2), channel_id=1, source_target_pairs={{0,8},{1,9},{2,10},{3,11},{4,12},{5,13},{6,14},{7,15},{8,16},{9,17... | collective-permute-start | bytes 1572872 | tf_op jit(solution)/shard_map/ppermute | solution.py:1091
  277.6 21.1 %collective-permute-start.33 = (bf16[128,1024]{1,0:T(8,128)(2,1)S(1)}, bf16[128,1024]{1,0:T(8,128)(2,1)S(1)}, u32[]{:S(2)}, u32[]{:S(2)}) collective-permute-start(bf16[128,1024]{1,0:T(8,128)(2,1)S(1)} %fusion.19), channel_id=1, source_target_pairs={{0,8},{1,9},{2,10},{3,11},{4,12},{5,13},{6,14},{7,15},{8,16},{9,17... | collective-permute-start | bytes 786440 | tf_op jit(solution)/shard_map/ppermute | solution.py:1091
  279.2 18.3 %collective-permute-start.25 = (bf16[144,1024]{1,0:T(8,128)(2,1)S(1)}, bf16[144,1024]{1,0:T(8,128)(2,1)S(1)}, u32[]{:S(2)}, u32[]{:S(2)}) collective-permute-start(bf16[144,1024]{1,0:T(8,128)(2,1)S(1)} %bitcast.179), channel_id=1, source_target_pairs={{0,8},{1,9},{2,10},{3,11},{4,12},{5,13},{6,14},{7,15},{8,16},{9,17... | collective-permute-start | bytes 884744 | tf_op jit(solution)/shard_map/ppermute | solution.py:1091
  288.0 20.5 %collective-permute-start.40 = (bf16[512,256]{1,0:T(8,128)(2,1)S(1)}, bf16[512,256]{1,0:T(8,128)(2,1)S(1)}, u32[]{:S(2)}, u32[]{:S(2)}) collective-permute-start(bf16[512,256]{1,0:T(8,128)(2,1)S(1)} %get-tuple-element.236), channel_id=1, source_target_pairs={{0,4},{1,5},{2,6},{3,7},{4,0},{5,1},{6,2},{7,3},{8,12},{9,13},{10,... | collective-permute-start | bytes 786440 | tf_op jit(solution)/shard_map/ppermute | solution.py:1091
  298.6 8.7 %collective-permute-start.26 = (bf16[144,1024]{1,0:T(8,128)(2,1)S(1)}, bf16[144,1024]{1,0:T(8,128)(2,1)S(1)}, u32[]{:S(2)}, u32[]{:S(2)}) collective-permute-start(bf16[144,1024]{1,0:T(8,128)(2,1)S(1)} %fusion.11), channel_id=1, source_target_pairs={{0,8},{1,9},{2,10},{3,11},{4,12},{5,13},{6,14},{7,15},{8,16},{9,17... | collective-permute-start | bytes 884744 | tf_op jit(solution)/shard_map/ppermute | solution.py:1091
  299.9 20.0 %collective-permute-start.34 = (bf16[128,1024]{1,0:T(8,128)(2,1)S(1)}, bf16[128,1024]{1,0:T(8,128)(2,1)S(1)}, u32[]{:S(2)}, u32[]{:S(2)}) collective-permute-start(bf16[128,1024]{1,0:T(8,128)(2,1)S(1)} %fusion.18.refs_1_), channel_id=1, source_target_pairs={{0,1},{1,0},{2,3},{3,2},{4,5},{5,4},{6,7},{7,6},{8,9},{9,8},{10,11... | collective-permute-start | bytes 786440 | tf_op jit(solution)/shard_map/ppermute | solution.py:1091
  300.0 10.4 %collective-permute-start.35 = (bf16[128,1024]{1,0:T(8,128)(2,1)S(1)}, bf16[128,1024]{1,0:T(8,128)(2,1)S(1)}, u32[]{:S(2)}, u32[]{:S(2)}) collective-permute-start(bf16[128,1024]{1,0:T(8,128)(2,1)S(1)} %fusion.18.refs_1_), channel_id=1, source_target_pairs={{0,2},{1,3},{2,0},{3,1},{4,6},{5,7},{6,4},{7,5},{8,10},{9,11},{10,... | collective-permute-start | bytes 786440 | tf_op jit(solution)/shard_map/ppermute | solution.py:1091
  308.4 8.6 %collective-permute-start.27 = (bf16[144,1024]{1,0:T(8,128)(2,1)S(1)}, bf16[144,1024]{1,0:T(8,128)(2,1)S(1)}, u32[]{:S(2)}, u32[]{:S(2)}) collective-permute-start(bf16[144,1024]{1,0:T(8,128)(2,1)S(1)} %fusion.9), channel_id=1, source_target_pairs={{0,8},{1,9},{2,10},{3,11},{4,12},{5,13},{6,14},{7,15},{8,16},{9,17... | collective-permute-start | bytes 884744 | tf_op jit(solution)/shard_map/ppermute | solution.py:1091
  310.4 9.6 %collective-permute-start.36 = (bf16[128,1024]{1,0:T(8,128)(2,1)S(1)}, bf16[128,1024]{1,0:T(8,128)(2,1)S(1)}, u32[]{:S(2)}, u32[]{:S(2)}) collective-permute-start(bf16[128,1024]{1,0:T(8,128)(2,1)S(1)} %collective-permute-done.35.refs_3_), channel_id=1, source_target_pairs={{0,1},{1,0},{2,3},{3,2},{4,5},{5,4},{6,7},{7,6},{8,9},{9,8},{10,11... | collective-permute-start | bytes 786440 | tf_op jit(solution)/shard_map/ppermute | solution.py:1091
  311.3 10.8 %collective-permute-start.41 = (bf16[512,256]{1,0:T(8,128)(2,1)S(1)}, bf16[512,256]{1,0:T(8,128)(2,1)S(1)}, u32[]{:S(2)}, u32[]{:S(2)}) collective-permute-start(bf16[512,256]{1,0:T(8,128)(2,1)S(1)} %add_convert_fusion.1.refs_1_), channel_id=1, source_target_pairs={{0,1},{1,0},{2,3},{3,2},{4,5},{5,4},{6,7},{7,6},{8,9},{9,8},{10,11... | collective-permute-start | bytes 786440 | tf_op jit(solution)/shard_map/ppermute | solution.py:1091
  (75 other events, 355.2 us)
Sparse Core Ops, SparseCore 0:
  13.8 131.9 all-gather.2
